TPU v7x, 256 devices: a whole 4x4x8 slice. The times are simulated.
256 devices in a mesh: ctx: 16 (over y_hi, z), head: 16 (over y_lo, x, core).
Axes of the slice: x: 4, y: 4 (y_hi: 2, y_lo: 2; y = y_hi * 2 + y_lo), z: 8, core: 2. Of those that a mesh axis runs over, the one named last changes fastest.
Arguments:
- queries: bfloat16 [256, 128, 576], P('ctx', 'head'), may hold values from -48 to 48
- cache: bfloat16 [32768, 576], P('ctx'), may hold values from -6 to 6
- new_latents: bfloat16 [256, 576], P('ctx'), may hold values from -6 to 6
- cache_lengths: int32 [16], P('ctx'), may hold values from 1 to 2048, 20480 in all
- new_offsets: int32 [256], replicated, may hold values from 0 to 255, each once
- value_up_weight: bfloat16 [128, 512, 128], P('head'), may hold values from -6 to 6
Outputs:
- attention_out: bfloat16 [256, 128, 128], P('ctx', 'head')
Inputs may be any that keep to these rules, and one draw needn't show every extreme that they name: Block b holds cache_lengths[b] valid rows; the largest is exactly 2048. `new_offsets`: each of 0 to 255 appears once.
All inputs are finite; a program needn't handle non-finite values.
Results may differ from a plain program's by a relative error of at most 0.015.
Values may be sent and summed in bfloat16 or wider, within the bound.
No kernel may reach another device: no remote copies, remote signals or barrier semaphores. Data moves between devices by JAX's collectives and lax.ppermute only.
A program may use at most 64 MiB of HBM per device.

v0:
```python
import jax
import jax.numpy as jnp
from jax import lax
from jax.sharding import PartitionSpec as P

KVR = 512


softmax_scale = 192.0 ** (-0.5)
masked_value = -1e30


def attend_over_cached_context(query_rows, cache, valid_len):
    width = cache.shape[0]
    block_len = min(512, width)
    block_count = (valid_len + block_len - 1) // block_len
    row_count = query_rows.shape[0]
    initial = (
        jnp.zeros((row_count, KVR), jnp.float32),
        jnp.full((row_count,), masked_value, jnp.float32),
        jnp.zeros((row_count,), jnp.float32),
    )

    def visit_block(block_id, running):
        numer, highest, totals = running
        key_block = lax.dynamic_slice_in_dim(cache, block_id * block_len, block_len, 0)
        scores = (
            lax.dot_general(
                query_rows, key_block, (((1,), (1,)), ((), ())), preferred_element_type=jnp.float32
            )
            * softmax_scale
        )
        position = block_id * block_len + jnp.arange(block_len, dtype=jnp.int32)
        scores = jnp.where(position[None, :] < valid_len, scores, masked_value)
        new_high = jnp.maximum(highest, jnp.max(scores, axis=1))
        weights = jnp.exp(scores - new_high[:, None])
        rescale = jnp.exp(highest - new_high)
        totals = totals * rescale + jnp.sum(weights, axis=1)
        numer = numer * rescale[:, None] + jnp.dot(
            weights.astype(jnp.bfloat16), key_block[:, :KVR], preferred_element_type=jnp.float32
        )
        return (numer, new_high, totals)

    return lax.fori_loop(0, block_count, visit_block, initial)


def project_heads(latent_row_vectors, value_expanded):
    return jnp.einsum(
        "ujc,jcn->ujn", latent_row_vectors, value_expanded, precision=lax.Precision.HIGHEST
    )


def shards(queries, cache, new_latents, cache_lengths, new_offsets, value_up_weight):
    own_tokens, head_local, lat_width = queries.shape
    valid_len = cache_lengths[0]
    index_ctx = lax.axis_index("ctx")
    value_expanded = value_up_weight.astype(jnp.float32)
    piece = lax.all_gather(queries, "ctx", axis=0, tiled=True)
    piece_tokens = piece.shape[0]
    numer, highest, totals = attend_over_cached_context(
        piece.reshape(piece_tokens * head_local, lat_width), cache, valid_len
    )
    cache_numer = numer.reshape(piece_tokens, head_local, KVR)
    cache_high = highest.reshape(piece_tokens, head_local)
    cache_total = totals.reshape(piece_tokens, head_local)
    new_keys = lax.all_gather(new_latents, "ctx", axis=0, tiled=True)
    own_rows = queries.reshape(own_tokens * head_local, lat_width)
    new_scores = (
        lax.dot_general(
            own_rows, new_keys, (((1,), (1,)), ((), ())), preferred_element_type=jnp.float32
        )
        * softmax_scale
    )
    new_scores = new_scores.reshape(own_tokens, head_local, new_keys.shape[0])
    own_offsets = lax.dynamic_slice_in_dim(new_offsets, index_ctx * own_tokens, own_tokens, 0)
    allowed = new_offsets[None, :] <= own_offsets[:, None]
    new_scores = jnp.where(allowed[:, None, :], new_scores, masked_value)
    new_max = jnp.max(new_scores, axis=2)
    new_exp = jnp.exp(new_scores - new_max[:, :, None])
    new_total = jnp.sum(new_exp, axis=2)
    new_values = jnp.einsum(
        "thn,nk->thk",
        new_exp.astype(jnp.bfloat16),
        new_keys[:, :KVR],
        preferred_element_type=jnp.float32,
    )
    numer_parts, high_parts, total_parts = (
        lax.all_to_all(cache_numer[None], "ctx", split_axis=1, concat_axis=0, tiled=True),
        lax.all_to_all(cache_high[None], "ctx", split_axis=1, concat_axis=0, tiled=True),
        lax.all_to_all(cache_total[None], "ctx", split_axis=1, concat_axis=0, tiled=True),
    )
    overall = jnp.maximum(jnp.max(high_parts, axis=0), new_max)
    factors = jnp.exp(high_parts - overall[None])
    new_factor = jnp.exp(new_max - overall)
    numer = (
        jnp.sum(numer_parts * factors[:, :, :, None], axis=0) + new_values * new_factor[:, :, None]
    )
    denom = jnp.sum(total_parts * factors, axis=0) + new_total * new_factor
    final_output = project_heads(numer / denom[:, :, None], value_expanded)
    return final_output.astype(jnp.bfloat16)


def solution(mesh):
    return jax.shard_map(
        shards,
        mesh=mesh,
        in_specs=(
            P("ctx", "head", None),
            P("ctx", None),
            P("ctx", None),
            P("ctx"),
            P(),
            P("head", None, None),
        ),
        out_specs=P("ctx", "head", None),
        check_vma=False,
    )
```

profile of v0, /device:TPU:24, one launch (start us, length us, event | category | flops | bytes accessed | tf_op | source)
XLA Modules:
  0.0 322.1 jit_solution(10434214116760923012)
XLA Ops:
  7.9 92.6 %all-gather.2.cloned.1.call-done = bf16[256,8,576]{2,1,0:T(8,128)(2,1)} async-done(((bf16[16,8,576]{2,1,0:T(8,128)(2,1)}), bf16[256,8,576]{2,1,0:T(8,128)(2,1)}) %all-gather.2.cloned.1.call-update) | async-done | bytes 2359312 | tf_op jit(solution)/shard_map/all_gather | solution.py:58
  100.5 2.5 broadcast_in_dim.48
  103.0 37.7 %while.14 = (s32[]{:T(128)}, f32[2048,512]{1,0:T(8,128)}, f32[2048]{0:T(1024)S(1)}, f32[2048]{0:T(1024)S(1)}, s32[]{:T(128)}, /*index=5*/s32[]{:T(128)}, bf16[20...) while((s32[]{:T(128)}, f32[2048,512]{1,0:T(8,128)}, ...), condition=%wide.region_3.4_spmd, body=%wide.region_0.3_spmd.sunk | while | flops 2295337984 | bytes 58394856 | solution.py:44
  103.7 4.2 %fusion.40 = (f32[2048]{0:T(1024)S(1)}, f32[512,2048]{1,0:T(8,128)S(1)}) fusion(pred[512]{0:T(512)(128)(4,1)S(1)} %add_compare_fusion.2, bf16[2048,576]{1,0:T(8,128)(2,1)} %get-tuple-element.168, bf16[2048,576]{0,1:T(8,128)(2,1)} %get-tuple-element.167, s32[]{:T(128)S(6)} %select_n.58), kind=kOutput, calls=%fused_computation.3.clone.1 | convolution fusion | flops 1211103232 | bytes 7414276 | tf_op jit(solution)/shard_map/while/body/dot_general | solution.py:28
  107.9 0.9 fusion.41
  108.8 1.2 copy-done.1
  110.1 3.5 %multiply_add_fusion.6 = f32[2048,512]{1,0:T(8,128)S(1)} fusion(f32[2048,512]{1,0:T(8,128)S(1)} %copy-done.1, f32[512,2048]{1,0:T(8,128)S(1)} %get-tuple-element.133, f32[2048]{0:T(1024)S(1)} %max.19, f32[2048]{0:T(1024)S(1)} %get-tuple-element.135, pred[512]{0:T(512)(128)(4,1)S(1)} %add_compare_fusion.2, bf16[2048,576]{0,1:T(8,128)(2,1)} %get-tuple-element.167, ...), kind=kOutput, calls=%fused_computation.1.clone.1 | convolution fusion | flops 1080033280 | bytes 13124100 | tf_op jit(solution)/shard_map/while/body/dot_general | solution.py:39
  113.6 2.0 copy-done.2
  116.3 4.2 %fusion.40 = (f32[2048]{0:T(1024)S(1)}, f32[512,2048]{1,0:T(8,128)S(1)}) fusion(pred[512]{0:T(512)(128)(4,1)S(1)} %add_compare_fusion.2, bf16[2048,576]{1,0:T(8,128)(2,1)} %get-tuple-element.168, bf16[2048,576]{0,1:T(8,128)(2,1)} %get-tuple-element.167, s32[]{:T(128)S(6)} %select_n.58), kind=kOutput, calls=%fused_computation.3.clone.1 | convolution fusion | flops 1211103232 | bytes 7414276 | tf_op jit(solution)/shard_map/while/body/dot_general | solution.py:28
  120.5 0.9 fusion.41
  121.4 1.2 copy-done.1
  122.6 3.5 %multiply_add_fusion.6 = f32[2048,512]{1,0:T(8,128)S(1)} fusion(f32[2048,512]{1,0:T(8,128)S(1)} %copy-done.1, f32[512,2048]{1,0:T(8,128)S(1)} %get-tuple-element.133, f32[2048]{0:T(1024)S(1)} %max.19, f32[2048]{0:T(1024)S(1)} %get-tuple-element.135, pred[512]{0:T(512)(128)(4,1)S(1)} %add_compare_fusion.2, bf16[2048,576]{0,1:T(8,128)(2,1)} %get-tuple-element.167, ...), kind=kOutput, calls=%fused_computation.1.clone.1 | convolution fusion | flops 1080033280 | bytes 13124100 | tf_op jit(solution)/shard_map/while/body/dot_general | solution.py:39
  126.2 2.0 copy-done.2
  128.8 4.2 %fusion.40 = (f32[2048]{0:T(1024)S(1)}, f32[512,2048]{1,0:T(8,128)S(1)}) fusion(pred[512]{0:T(512)(128)(4,1)S(1)} %add_compare_fusion.2, bf16[2048,576]{1,0:T(8,128)(2,1)} %get-tuple-element.168, bf16[2048,576]{0,1:T(8,128)(2,1)} %get-tuple-element.167, s32[]{:T(128)S(6)} %select_n.58), kind=kOutput, calls=%fused_computation.3.clone.1 | convolution fusion | flops 1211103232 | bytes 7414276 | tf_op jit(solution)/shard_map/while/body/dot_general | solution.py:28
  133.0 0.9 fusion.41
  134.0 1.2 copy-done.1
  135.2 3.5 %multiply_add_fusion.6 = f32[2048,512]{1,0:T(8,128)S(1)} fusion(f32[2048,512]{1,0:T(8,128)S(1)} %copy-done.1, f32[512,2048]{1,0:T(8,128)S(1)} %get-tuple-element.133, f32[2048]{0:T(1024)S(1)} %max.19, f32[2048]{0:T(1024)S(1)} %get-tuple-element.135, pred[512]{0:T(512)(128)(4,1)S(1)} %add_compare_fusion.2, bf16[2048,576]{0,1:T(8,128)(2,1)} %get-tuple-element.167, ...), kind=kOutput, calls=%fused_computation.1.clone.1 | convolution fusion | flops 1080033280 | bytes 13124100 | tf_op jit(solution)/shard_map/while/body/dot_general | solution.py:39
  138.8 2.0 copy-done.2
  142.9 18.7 %all-to-all-start.1 = ((f32[16,1,128]{2,1,0:T(1,128)}), f32[16,1,128]{2,1,0:T(1,128)S(1)}, u32[]{:S(2)}, u32[]{:S(2)}) async-start(f32[16,1,128]{2,1,0:T(1,128)} %reshape.111), calls=%async_computation.1 | async-start | bytes 16384 | tf_op jit(solution)/shard_map/all_to_all | solution.py:89
  162.8 5.9 %all-to-all-done.1 = f32[16,1,128]{2,1,0:T(1,128)S(1)} async-done(((f32[16,1,128]{2,1,0:T(1,128)}), f32[16,1,128]{2,1,0:T(1,128)S(1)}, u32[]{:S(2)}, u32[]{:S(2)}) %all-to-all-start.1) | async-done | bytes 8224 | tf_op jit(solution)/shard_map/all_to_all | solution.py:89
  168.7 12.5 %all_to_all.36 = f32[16,1,128]{2,1,0:T(1,128)S(1)} all-to-all(f32[16,1,128]{2,1,0:T(1,128)S(1)} %reshape.113), channel_id=1, replica_groups=mesh['ctx'=16,'head'=16] {'ctx'}, dimensions={0} | all-to-all | bytes 16384 | tf_op jit(solution)/shard_map/all_to_all | solution.py:90
  181.2 7.4 %all-to-all-start = ((f32[1,256,8,512]{3,2,0,1:T(8,128)}), f32[1,256,8,512]{3,2,0,1:T(8,128)}, u32[]{:S(2)}, u32[]{:S(2)}) async-start(f32[1,256,8,512]{3,2,0,1:T(8,128)} %bitcast.36), calls=%async_computation | async-start | bytes 8388608 | tf_op jit(solution)/shard_map/all_to_all | solution.py:88
  188.7 119.7 %all_gather.7 = bf16[256,576]{1,0:T(8,128)(2,1)S(1)} all-gather(bf16[16,576]{1,0:T(8,128)(2,1)S(1)} %copy-done.4), channel_id=1, replica_groups=mesh['ctx'=16,'head'=16] {'ctx'}, dimensions={0}, use_global_device_ids=true | all-gather | bytes 313344 | tf_op jit(solution)/shard_map/all_gather | solution.py:66
  311.2 2.6 multiply_reduce_fusion
  (58 shorter events, 10.3 us)
Async XLA Ops:
  6.5 307.6 %copy-start = (bf16[8,512,128]{2,1,0:T(8,128)(2,1)S(1)}, bf16[8,512,128]{2,1,0:T(8,128)(2,1)}, u32[]{:S(2)}) copy-start(bf16[8,512,128]{2,1,0:T(8,128)(2,1)} %param.13) | copy-start | bytes 3145732
  6.5 94.0 %all-gather.2.cloned.1.call-start = ((), (), s32[]{:S(2)}) async-start(), calls=%async_computation.3 | async-start | bytes 2785280 | tf_op jit(solution)/shard_map/all_gather | solution.py:58
  107.9 2.2 copy-start.1
  113.6 2.0 copy-start.2
  120.5 2.2 copy-start.1
  126.2 2.0 copy-start.2
  133.0 2.2 copy-start.1
  138.7 2.0 copy-start.2
  142.9 25.8 %all-to-all-start.1 = ((f32[16,1,128]{2,1,0:T(1,128)}), f32[16,1,128]{2,1,0:T(1,128)S(1)}, u32[]{:S(2)}, u32[]{:S(2)}) async-start(f32[16,1,128]{2,1,0:T(1,128)} %reshape.111), calls=%async_computation.1 | async-start | bytes 16384 | tf_op jit(solution)/shard_map/all_to_all | solution.py:89
  181.2 7.4 %copy-start.5 = (s32[256]{0:T(256)S(1)}, s32[256]{0:T(256)}, u32[]{:S(2)}) copy-start(s32[256]{0:T(256)} %param.12) | copy-start | bytes 3076
  181.2 7.5 %copy-start.4 = (bf16[16,576]{1,0:T(8,128)(2,1)S(1)}, bf16[16,576]{1,0:T(8,128)(2,1)}, u32[]{:S(2)}) copy-start(bf16[16,576]{1,0:T(8,128)(2,1)} %param.10) | copy-start | bytes 55300
  181.2 127.3 %copy-start.3 = (bf16[16,8,576]{2,1,0:T(8,128)(2,1)S(1)}, bf16[16,8,576]{2,1,0:T(8,128)(2,1)}, u32[]{:S(2)}) copy-start(bf16[16,8,576]{2,1,0:T(8,128)(2,1)} %param.8) | copy-start | bytes 442372
  181.2 130.0 %all-to-all-start = ((f32[1,256,8,512]{3,2,0,1:T(8,128)}), f32[1,256,8,512]{3,2,0,1:T(8,128)}, u32[]{:S(2)}, u32[]{:S(2)}) async-start(f32[1,256,8,512]{3,2,0,1:T(8,128)} %bitcast.36), calls=%async_computation | async-start | bytes 8388608 | tf_op jit(solution)/shard_map/all_to_all | solution.py:88
Sparse Core Ops, SparseCore 0:
  9.9 90.5 all-gather.1
where the time goes:
time: 323 us; the launch traced here: 322 us
  blocking collectives  132 us (41%)
  waiting for transfers between devices  99.2 us (31%)
  starting transfers between devices  26.1 us (8%)
  matrix products  24.4 us (8%)
  local copies, waits for them, and re-layouts  15.2 us (5%)
  between operations  14.2 us (4%)
  other arithmetic  10.6 us (3%)
    all_gather x1, blocking collectives, shards(): new_keys = lax.all_gather(new_latents, 'ctx', axis=0, tiled=True)  120 us
    all_gather x1, waiting for transfers between devices, shards(): piece = lax.all_gather(queries, 'ctx', axis=0, tiled=True)  92.6 us
    all_to_all x1, starting transfers between devices, shards(): lax.all_to_all(cache_high[None], 'ctx', split_axis=1, concat_axis=0, tile...  18.7 us
    dot_general x3, matrix products, visit_block(): lax.dot_general(query_rows, key_block, (((1,), (1,)), ((), ())), preferre...  12.6 us
    all_to_all x1, blocking collectives, shards(): lax.all_to_all(cache_total[None], 'ctx', split_axis=1, concat_axis=0, til...  12.5 us
    dot_general x3, matrix products, visit_block(): jnp.dot(weights.astype(jnp.bfloat16), key_block[:, :KVR], preferred_eleme...  10.6 us
    while x15, local copies, waits for them, and re-layouts  9.59 us
    all_to_all x1, starting transfers between devices, shards(): lax.all_to_all(cache_numer[None], 'ctx', split_axis=1, concat_axis=0, til...  7.39 us
  transfers between devices with their start and end apart: 3, of which 2 were waited for; matrix products, arithmetic and copies ran while one was open for 1% of the time, Pallas kernels for 0%

commit v1 on v0

v1 whole, which is shorter than its diff:
```python
import functools

import jax
import jax.numpy as jnp
from jax import lax
from jax.experimental import pallas as pl
from jax.experimental.pallas import tpu as pltpu
from jax.sharding import PartitionSpec as P

KVR = 512
VDIM = 128
EXTRA = 32
STAT = 16
NZ = 8
OFFSETS = [0, 7, 1, 6, 2, 5, 3, 4]
SHARED = 256

exp_scale = 192.0 ** (-0.5) * 1.4426950408889634
masked_value = -1e30
NT = (((1,), (1,)), ((), ()))
small_cost = pl.CostEstimate(flops=10**6, bytes_accessed=10**4, transcendentals=0)
VMEM = pl.BlockSpec(memory_space=pltpu.VMEM)
SMEM = pl.BlockSpec(memory_space=pltpu.SMEM)


def dot_nt(a, b):
    return lax.dot_general(a, b, NT, preferred_element_type=jnp.float32)


def dot_nn(a, b):
    return jnp.dot(a, b, preferred_element_type=jnp.float32)


def pack_stats(high, total):
    lane = lax.broadcasted_iota(jnp.int32, (high.shape[0], 128), 1)
    return jnp.where(lane == 0, high, total)


def key_bias(width, valid):
    position = lax.broadcasted_iota(jnp.int32, (1, width), 1)
    return jnp.where(position < valid, 0.0, masked_value)


def pack_kernel(
    len_ref, keys_ref, new_ref, query_ref, shared_ref, direct_ref, rows_ref, stage_ref, new_vmem, query_vmem, flat_ref, sems
):
    head = lax.axis_index("head")
    core, side = lax.rem(head, 2), lax.rem(head // 2, 2)
    lat, few = shared_ref.shape
    width = direct_ref.shape[1]
    half = 2 * few + width
    own_tokens, heads, _ = query_ref.shape
    part = pl.multiple_of(core * half + side * few, 128)
    rest = pl.multiple_of(core * half + 2 * few, 128)
    load_query = pltpu.make_async_copy(query_ref, query_vmem, sems.at[0])
    load_new = pltpu.make_async_copy(new_ref, new_vmem, sems.at[1])
    load_shared = pltpu.make_async_copy(
        keys_ref.at[:, pl.ds(part, few)], stage_ref.at[0:lat, 0:few], sems.at[2]
    )
    load_direct = pltpu.make_async_copy(
        keys_ref.at[:, pl.ds(rest, width)], stage_ref.at[0:lat, few : few + width], sems.at[3]
    )
    send_shared = pltpu.make_async_copy(stage_ref.at[0:lat, 0:few], shared_ref, sems.at[4])
    send_direct = pltpu.make_async_copy(stage_ref.at[:, few : few + width], direct_ref, sems.at[5])
    load_shared.start()
    load_query.start()
    load_new.start()
    load_direct.start()
    length = len_ref[0]
    high = length // 256
    r = lax.broadcasted_iota(jnp.int32, (16, 128), 0)
    c = lax.broadcasted_iota(jnp.int32, (16, 128), 1)
    note = jnp.where(
        (r == 0) & (c == 0), high, jnp.where((r == 0) & (c == 1), length - high * 256, 0)
    ).astype(jnp.float32)
    stage_ref[lat + 16 : lat + 32, few + 128 : few + 256] = note.astype(jnp.bfloat16)
    load_shared.wait()
    send_shared.start()
    load_query.wait()
    queries = query_vmem[...].astype(jnp.float32).reshape(own_tokens * heads, lat)
    lanes = [slice(p, min(lat, p + 128)) for p in range(0, lat, 128)]
    for p, lane in enumerate(lanes):
        flat_ref[p, :, 0 : lane.stop - lane.start] = queries[:, lane]
    for one in range(heads):
        for p, lane in enumerate(lanes):
            rows = flat_ref[p, pl.ds(one, own_tokens, stride=heads), :]
            rows_ref[one * own_tokens : (one + 1) * own_tokens, lane] = rows[
                :, 0 : lane.stop - lane.start
            ].astype(jnp.bfloat16)
    load_new.wait()
    stage_ref[lat : lat + 16, few : few + KVR] = new_vmem[:, 0:KVR]
    stage_ref[lat + 16 : lat + 32, few : few + lat - KVR] = new_vmem[:, KVR:lat]
    load_direct.wait()
    send_direct.start()
    send_shared.wait()
    send_direct.wait()


def join_kernel(mine_ref, other_ref, direct_ref, near_ref):
    side = lax.rem(lax.axis_index("head") // 2, 2)
    lat, few = mine_ref.shape
    near_ref[0:lat, pl.ds(pl.multiple_of(side * few, 128), few)] = mine_ref[...]
    near_ref[0:lat, pl.ds(pl.multiple_of((1 - side) * few, 128), few)] = other_ref[...]
    near_ref[:, 2 * few :] = direct_ref[...]
    near_ref[lat:, 0 : 2 * few] = jnp.zeros((EXTRA, 2 * few), jnp.bfloat16)


def own_kernel(blocks, len_ref, *refs):
    query_refs, (keys_ref, acc_ref, stat_ref) = refs[:blocks], refs[blocks:]
    valid = len_ref[0]
    full = keys_ref.shape[1]
    widths = [full // 2, full * 3 // 4, full]

    def attend(width):
        rows = jnp.concatenate([r[...] for r in query_refs], axis=0)
        scores = dot_nn(rows, keys_ref[:, 0:width]) + key_bias(width, valid)
        high = jnp.max(scores, axis=1, keepdims=True)
        weights = jnp.exp2((scores - high) * exp_scale)
        total = jnp.sum(weights, axis=1, keepdims=True)
        acc_ref[...] = dot_nt(weights.astype(jnp.bfloat16), keys_ref[0:KVR, 0:width])
        stat_ref[...] = pack_stats(high, total)

    least = 0
    for width in widths:
        pl.when((valid > least) & (valid <= width))(functools.partial(attend, width))
        least = width


def attend_own(valid, blocks, keys):
    rows = sum(b.shape[0] for b in blocks)
    width = keys.shape[1]
    return pl.pallas_call(
        functools.partial(own_kernel, len(blocks)),
        in_specs=[SMEM] + [VMEM] * (len(blocks) + 1),
        out_specs=[VMEM, VMEM],
        out_shape=[
            jax.ShapeDtypeStruct((rows, KVR), jnp.float32),
            jax.ShapeDtypeStruct((rows, 128), jnp.float32),
        ],
        compiler_params=pltpu.CompilerParams(vmem_limit_bytes=12 * 2**20),
        cost_estimate=small_cost,
        name="attend_own",
    )(valid, *blocks, keys)


def partner_length(part_ref):
    lat = part_ref.shape[0] - EXTRA
    row = part_ref[lat + 16 : lat + 32, 2 * SHARED + 128 : 2 * SHARED + 256].astype(jnp.float32)
    r = lax.broadcasted_iota(jnp.int32, row.shape, 0)
    c = lax.broadcasted_iota(jnp.int32, row.shape, 1)
    high = jnp.sum(jnp.where((r == 0) & (c == 0), row, 0.0))
    low = jnp.sum(jnp.where((r == 0) & (c == 1), row, 0.0))
    return (high * 256.0 + low).astype(jnp.int32)


def fold(scores, values, acc, high, total):
    new_high = functools.reduce(
        jnp.maximum, [jnp.max(s, axis=1, keepdims=True) for s in scores], high
    )
    rescale = jnp.exp2((high - new_high) * exp_scale)
    acc = acc * rescale
    total = total * rescale
    for s, v in zip(scores, values):
        weights = jnp.exp2((s - new_high) * exp_scale)
        total = total + jnp.sum(weights, axis=1, keepdims=True)
        acc = acc + v(weights.astype(jnp.bfloat16))
    return acc, new_high, total


def final_kernel(counts, offset_ref, *refs):
    queries, refs = refs[:NZ], refs[NZ:]
    states, refs = refs[: 2 * len(counts)], refs[2 * len(counts) :]
    near_ref, far_ref, new_ref, up_ref, out_ref, latent_ref = refs
    pieces = [(g, 128 * i) for g, count in enumerate(counts) for i in range(count)]
    lat, width = near_ref.shape[0] - EXTRA, near_ref.shape[1]
    core = lax.rem(lax.axis_index("head"), 2)
    ctx = lax.axis_index("ctx")
    z, pair = lax.rem(ctx, NZ), ctx // NZ
    length = partner_length(near_ref)
    near_bias = key_bias(width, length - core * width)
    far_bias = key_bias(width, length - (1 - core) * width)
    first = 2 * SHARED
    partner_new = jnp.concatenate(
        [near_ref[lat : lat + 16, first : first + KVR], near_ref[lat + 16 : lat + 32, first : first + lat - KVR]],
        axis=1,
    )
    new_keys = jnp.concatenate([new_ref[...], partner_new], axis=0)
    lane = lax.broadcasted_iota(jnp.int32, (16, 32), 1)
    line = lax.broadcasted_iota(jnp.int32, (16, 32), 0)
    key_offsets = jnp.zeros((16, 32), jnp.int32)
    for k in range(32):
        side = pair if k < 16 else 1 - pair
        key_offsets = jnp.where(lane == k, offset_ref[(side * NZ + z) * 16 + k % 16], key_offsets)
    new_bias = []
    for block in range(NZ):
        first = (pair * NZ + lax.rem(z + OFFSETS[block], NZ)) * 16
        token_offsets = jnp.zeros((16, 32), jnp.int32)
        for t in range(16):
            token_offsets = jnp.where(line == t, offset_ref[first + t], token_offsets)
        new_bias.append(jnp.where(key_offsets <= token_offsets, 0.0, masked_value))
    wide = lax.broadcasted_iota(jnp.int32, (128, 128), 1)
    levels = jnp.zeros((128, 128), jnp.float32)
    for tile in range(NZ // 2):
        both = pieces[2 * tile : 2 * tile + 2]
        rows = jnp.concatenate([queries[2 * tile][...], queries[2 * tile + 1][...]], axis=0)
        stat = jnp.concatenate([states[2 * g + 1][r : r + 128, :] for g, r in both], axis=0)
        acc, high, total = fold(
            [
                dot_nn(rows, near_ref[0:lat, :]) + near_bias,
                dot_nn(rows, far_ref[0:lat, :]) + far_bias,
                dot_nt(rows, new_keys)
                + jnp.concatenate([new_bias[2 * tile]] * 8 + [new_bias[2 * tile + 1]] * 8, axis=0),
            ],
            [
                lambda w: dot_nt(w, near_ref[0:KVR, :]),
                lambda w: dot_nt(w, far_ref[0:KVR, :]),
                lambda w: dot_nn(w, new_keys[:, 0:KVR]),
            ],
            jnp.concatenate([states[2 * g][r : r + 128, :] for g, r in both], axis=0),
            stat[:, 0:1],
            stat[:, 1:2],
        )
        latent_ref[tile * 256 : (tile + 1) * 256, :] = (acc * (1.0 / total)).astype(jnp.bfloat16)
        level = high * exp_scale + jnp.log2(total)
        levels = jnp.where(wide == 2 * tile, level[:128], levels)
        levels = jnp.where(wide == 2 * tile + 1, level[128:], levels)
    slots = [lax.rem(z + OFFSETS[block], NZ) for block in range(NZ)]
    for head in range(8):
        latent = jnp.concatenate(
            [latent_ref[b * 128 + head * 16 : b * 128 + head * 16 + 16, :] for b in range(NZ)], axis=0
        )
        result = dot_nn(latent, up_ref[head]).astype(jnp.bfloat16)
        for block in range(NZ):
            out_ref[slots[block], head * 16 : head * 16 + 16, :] = result[block * 16 : block * 16 + 16]
    flat = levels.T
    p0 = flat.astype(jnp.bfloat16).astype(jnp.float32)
    p1 = (flat - p0).astype(jnp.bfloat16).astype(jnp.float32)
    p2 = flat - p0 - p1
    r = lax.broadcasted_iota(jnp.int32, (STAT, 128), 0)
    for block in range(NZ):
        stats = jnp.where(
            r == 0,
            p0[block : block + 1],
            jnp.where(r == 1, p1[block : block + 1], jnp.where(r == 2, p2[block : block + 1], 0.0)),
        )
        out_ref[slots[block], 128 : 128 + STAT, :] = stats.astype(jnp.bfloat16)


def merge_kernel(part_ref, out_ref, order_ref):
    levels = []
    for source in range(NZ):
        stats = part_ref[source, 128 : 128 + STAT, :].astype(jnp.float32)
        levels.append(stats[0:1] + stats[1:2] + stats[2:3])
    level = jnp.concatenate(levels, axis=0)
    factor = jnp.exp2(level - jnp.max(level, axis=0, keepdims=True))
    factor = factor / jnp.sum(factor, axis=0, keepdims=True)
    factor = jnp.concatenate([factor, jnp.zeros((128 - NZ, 128), jnp.float32)], axis=0).T
    total = jnp.zeros((128, VDIM), jnp.float32)
    for source in range(NZ):
        total = total + part_ref[source, 0:128, :].astype(jnp.float32) * factor[:, source : source + 1]
    for head in range(8):
        order_ref[pl.ds(head, 16, stride=8), :] = total[head * 16 : head * 16 + 16]
    out_ref[...] = order_ref[...].astype(jnp.bfloat16)


def shards(queries, cache, new_latents, cache_lengths, new_offsets, value_up_weight):
    own_tokens, head_local, lat = queries.shape
    rows = own_tokens * head_local
    z = lax.axis_index("ctx") % NZ
    keys = cache.T

    def across(a):
        moves = [
            (c * 16 + h, ((c + NZ) % 16) * 16 + (h + 8) % 16) for c in range(16) for h in range(16)
        ]
        return lax.ppermute(a, ("ctx", "head"), moves)

    def swap(a):
        return lax.ppermute(a, "head", [(h, h ^ 1) for h in range(16)])

    def shift(a, step):
        return lax.ppermute(
            a, "ctx", [(c, c // NZ * NZ + (c + step) % NZ) for c in range(16)]
        )

    width = cache.shape[0] // 2
    hbm = pl.BlockSpec(memory_space=pltpu.HBM)
    shared, direct, own = pl.pallas_call(
        pack_kernel,
        in_specs=[SMEM, hbm, hbm, hbm],
        out_specs=[hbm, hbm, VMEM],
        out_shape=[
            jax.ShapeDtypeStruct((lat, SHARED), jnp.bfloat16),
            jax.ShapeDtypeStruct((lat + EXTRA, width - 2 * SHARED), jnp.bfloat16),
            jax.ShapeDtypeStruct((rows, lat), jnp.bfloat16),
        ],
        scratch_shapes=[
            pltpu.VMEM((lat + EXTRA, width - SHARED), jnp.bfloat16),
            pltpu.VMEM((own_tokens, lat), jnp.bfloat16),
            pltpu.VMEM((own_tokens, head_local, lat), jnp.bfloat16),
            pltpu.VMEM((-(-lat // 128), rows, 128), jnp.float32),
            pltpu.SemaphoreType.DMA((6,)),
        ],
        compiler_params=pltpu.CompilerParams(vmem_limit_bytes=4 * 2**20),
        name="pack",
    )(
        cache_lengths,
        pltpu.with_memory_space_constraint(keys, pltpu.HBM),
        pltpu.with_memory_space_constraint(new_latents, pltpu.HBM),
        pltpu.with_memory_space_constraint(queries, pltpu.HBM),
    )
    mine = across(shared)

    state0 = attend_own(cache_lengths, [own], keys)
    up1, down1 = shift(own, 1), shift(own, -1)
    up1, down1, state0, direct = lax.optimization_barrier((up1, down1, state0, direct))
    direct = across(direct)
    up2, down2 = shift(up1, 1), shift(down1, -1)
    state1 = attend_own(cache_lengths, [up1, down1], keys)
    up2, down2, state1, mine = lax.optimization_barrier((up2, down2, state1, mine))
    other = lax.ppermute(mine, "head", [(h, h ^ 2) for h in range(16)])
    up3, down3 = shift(up2, 1), shift(down2, -1)
    four = lax.ppermute(
        jnp.where(z % 2 == 0, up2, down2),
        "ctx",
        [(c, c // NZ * NZ + (c + (2 if c % 2 == 0 else -2)) % NZ) for c in range(16)],
    )
    state2 = attend_own(cache_lengths, [up2, down2], keys)
    up3, down3, four, state2, other, direct = lax.optimization_barrier(
        (up3, down3, four, state2, other, direct)
    )
    near = pl.pallas_call(
        join_kernel,
        in_specs=[VMEM] * 3,
        out_specs=VMEM,
        out_shape=jax.ShapeDtypeStruct((lat + EXTRA, width), jnp.bfloat16),
        compiler_params=pltpu.CompilerParams(vmem_limit_bytes=6 * 2**20),
        cost_estimate=small_cost,
        name="join",
    )(mine, other, direct)
    far = swap(near)
    state3 = attend_own(cache_lengths, [up3, down3, four], keys)
    far, state3 = lax.optimization_barrier((far, state3))
    states = [part for state in (state0, state1, state2, state3) for part in state]
    parts = pl.pallas_call(
        functools.partial(final_kernel, [1, 2, 2, 3]),
        in_specs=[SMEM] + [VMEM] * (NZ + 12),
        out_specs=VMEM,
        out_shape=jax.ShapeDtypeStruct((NZ, rows + STAT, VDIM), jnp.bfloat16),
        scratch_shapes=[pltpu.VMEM((NZ * rows, KVR), jnp.bfloat16)],
        compiler_params=pltpu.CompilerParams(vmem_limit_bytes=16 * 2**20),
        cost_estimate=small_cost,
        name="attend_final",
    )(new_offsets, own, up1, down1, up2, down2, up3, down3, four, *states, near, far, new_latents, value_up_weight)
    got = lax.all_to_all(
        parts, "ctx", 0, 0, axis_index_groups=[[*range(NZ)], [*range(NZ, 2 * NZ)]], tiled=True
    )
    out = pl.pallas_call(
        merge_kernel,
        in_specs=[VMEM],
        out_specs=VMEM,
        out_shape=jax.ShapeDtypeStruct((rows, VDIM), jnp.bfloat16),
        scratch_shapes=[pltpu.VMEM((rows, VDIM), jnp.float32)],
        name="merge",
    )(got)
    return out.reshape(own_tokens, head_local, VDIM)


def solution(mesh):
    return jax.shard_map(
        shards,
        mesh=mesh,
        in_specs=(
            P("ctx", "head", None),
            P("ctx", None),
            P("ctx", None),
            P("ctx"),
            P(),
            P("head", None, None),
        ),
        out_specs=P("ctx", "head", None),
        check_vma=False,
    )
```

time: 323 us -> 70.1 us (0.22)
  the two profiles are of different devices: /device:TPU:24 before, /device:TPU:1 now
where the time goes in v1:
time: 70.1 us; the launch traced here: 70.3 us
  starting transfers between devices  24.4 us (35%)
  Pallas kernels  19.8 us (28%)
  blocking collectives  16.4 us (23%)
  waiting for transfers between devices  8.16 us (12%)
  between operations  0.79 us (1%)
  local copies, waits for them, and re-layouts  0.73 us (1%)
    all_to_all x1, blocking collectives, shards(): lax.all_to_all(parts, 'ctx', 0, 0, axis_index_groups=[[*range(NZ)], [*ran...  16.4 us
    ppermute x6, starting transfers between devices, shift(): lax.ppermute(a, 'ctx', [(c, c // NZ * NZ + (c + step) % NZ) for c in rang...  13 us
    pallas_call x1, Pallas kernels, shards(): pl.pallas_call(functools.partial(final_kernel, [1, 2, 2, 3]), in_specs=[S...  9.54 us
    ppermute x6, waiting for transfers between devices, shift(): lax.ppermute(a, 'ctx', [(c, c // NZ * NZ + (c + step) % NZ) for c in rang...  5.85 us
    ppermute x2, starting transfers between devices, across(): return lax.ppermute(a, ('ctx', 'head'), moves)  5.47 us
    pallas_call x4, Pallas kernels, attend_own(): pl.pallas_call(functools.partial(own_kernel, len(blocks)), in_specs=[SMEM...  4.74 us
    ppermute x1, starting transfers between devices, swap(): return lax.ppermute(a, 'head', [(h, h ^ 1) for h in range(16)])  4.67 us
    pallas_call x1, Pallas kernels, shards(): pl.pallas_call(pack_kernel, in_specs=[SMEM, hbm, hbm, hbm], out_specs=[hb...  2.31 us
  transfers between devices with their start and end apart: 11, of which 6 were waited for; matrix products, arithmetic and copies ran while one was open for 0% of the time, Pallas kernels for 7%

profile of v1, /device:TPU:1, one launch (start us, length us, event | category | flops | bytes accessed | tf_op | source)
XLA Modules:
  0.0 70.3 jit_solution(16942498161763690977)
XLA Ops:
  0.7 2.3 %pack.1 = (bf16[576,256]{1,0:T(8,128)(2,1)}, bf16[608,512]{1,0:T(8,128)(2,1)}, bf16[128,576]{1,0:T(8,128)(2,1)S(1)}) custom-call(s32[1]{0:T(128)S(6)} %copy.7.len_ref, bf16[576,2048]{1,0:T(8,128)(2,1)} %bitcast.2, bf16[16,576]{1,0:T(8,128)(2,1)} %refs_18_.1, bf16[16,8,576]{2,1,0:T(8,128)(2,1)} %query_ref.1), custom_call_target="tpu_custom_call" | custom-call | tf_op jit(solution)/shard_map/pack/pallas_call | solution.py:288
  3.0 6.5 %collective-permute-start.1 = (bf16[128,576]{1,0:T(8,128)(2,1)S(1)}, bf16[128,576]{1,0:T(8,128)(2,1)S(1)}, u32[]{:S(2)}, u32[]{:S(2)}) collective-permute-start(bf16[128,576]{1,0:T(8,128)(2,1)S(1)} %get-tuple-element.36.refs_0_), channel_id=1, source_target_pairs={{0,112},{16,0},{32,16},{48,32},{64,48},{80,64},{96,80},{112,96},{1... | collective-permute-start | bytes 442376 | tf_op jit(solution)/shard_map/ppermute | solution.py:282
  9.5 2.7 %collective-permute-start.4 = (bf16[576,256]{1,0:T(8,128)(2,1)}, bf16[576,256]{1,0:T(8,128)(2,1)S(1)}, u32[]{:S(2)}, u32[]{:S(2)}) collective-permute-start(bf16[576,256]{1,0:T(8,128)(2,1)} %get-tuple-element.44), channel_id=1, source_target_pairs={{0,136},{1,137},{2,138},{3,139},{4,140},{5,141},{6,142},{7,143},{8... | collective-permute-start | bytes 884744 | tf_op jit(solution)/shard_map/ppermute | solution.py:276
  12.2 0.9 %attend_own.4 = (f32[128,512]{1,0:T(8,128)S(1)}, f32[128,128]{1,0:T(8,128)S(1)}) custom-call(s32[1]{0:T(128)S(6)} %copy.7.len_ref, bf16[128,576]{1,0:T(8,128)(2,1)S(1)} %get-tuple-element.36.refs_0_, bf16[576,2048]{1,0:T(8,128)(2,1)S(1)} %bitcast.3), custom_call_target="tpu_custom_call" | custom-call | flops 1000000 | bytes 10000 | tf_op jit(solution)/shard_map/attend_own/pallas_call | solution.py:132
  13.1 0.7 copy-done.2
  13.8 1.6 %collective-permute-done.refs_0_.refs_1_ = bf16[128,576]{1,0:T(8,128)(2,1)S(1)} collective-permute-done((bf16[128,576]{1,0:T(8,128)(2,1)S(1)}, bf16[128,576]{1,0:T(8,128)(2,1)S(1)}, u32[]{:S(2)}, u32[]{:S(2)}) %collective-permute-start) | collective-permute-done | bytes 147488 | tf_op jit(solution)/shard_map/ppermute | solution.py:282
  15.4 2.7 %collective-permute-start.9 = (bf16[608,512]{1,0:T(8,128)(2,1)}, bf16[608,512]{1,0:T(8,128)(2,1)}, u32[]{:S(2)}, u32[]{:S(2)}) collective-permute-start(bf16[608,512]{1,0:T(8,128)(2,1)} %get-tuple-element.50), channel_id=1, source_target_pairs={{0,136},{1,137},{2,138},{3,139},{4,140},{5,141},{6,142},{7,143},{8... | collective-permute-start | bytes 1867784 | tf_op jit(solution)/shard_map/ppermute | solution.py:276
  18.2 2.7 %collective-permute-start.3 = (bf16[128,576]{1,0:T(8,128)(2,1)S(1)}, bf16[128,576]{1,0:T(8,128)(2,1)S(1)}, u32[]{:S(2)}, u32[]{:S(2)}) collective-permute-start(bf16[128,576]{1,0:T(8,128)(2,1)S(1)} %collective-permute-done.1.refs_1_.refs_2_), channel_id=1, source_target_pairs={{0,112},{16,0},{32,16},{48,32},{64,48},{80,64},{96,80},{112,96},{1... | collective-permute-start | bytes 442376 | tf_op jit(solution)/shard_map/ppermute | solution.py:282
  20.8 1.1 %attend_own.5 = (f32[256,512]{1,0:T(8,128)S(1)}, f32[256,128]{1,0:T(8,128)S(1)}) custom-call(s32[1]{0:T(128)S(6)} %copy.7.len_ref, bf16[128,576]{1,0:T(8,128)(2,1)S(1)} %collective-permute-done.refs_0_.refs_1_, bf16[128,576]{1,0:T(8,128)(2,1)S(1)} %collective-permute-done.1.refs_1_.refs_2_, bf16[576,2048]{1,0:T(8,128)(2,1)S(1)} %bitcast.4), custom_call_target="tpu_custom_call" | custom-call | flops 1000000 | bytes 10000 | tf_op jit(solution)/shard_map/attend_own/pallas_call | solution.py:132
  22.0 2.0 %collective-permute-done.2.refs_0_.refs_3_ = bf16[128,576]{1,0:T(8,128)(2,1)S(1)} collective-permute-done((bf16[128,576]{1,0:T(8,128)(2,1)S(1)}, bf16[128,576]{1,0:T(8,128)(2,1)S(1)}, u32[]{:S(2)}, u32[]{:S(2)}) %collective-permute-start.2) | collective-permute-done | bytes 147488 | tf_op jit(solution)/shard_map/ppermute | solution.py:282
  23.9 1.2 %collective-permute-start.8 = (bf16[576,256]{1,0:T(8,128)(2,1)S(1)}, bf16[576,256]{1,0:T(8,128)(2,1)S(1)}, u32[]{:S(2)}, u32[]{:S(2)}) collective-permute-start(bf16[576,256]{1,0:T(8,128)(2,1)S(1)} %collective-permute-done.4.mine_ref), channel_id=1, source_target_pairs={{0,2},{1,3},{2,0},{3,1},{4,6},{5,7},{6,4},{7,5},{8,10},{9,11},{10,... | collective-permute-start | bytes 884744 | tf_op jit(solution)/shard_map/ppermute | solution.py:321
  25.2 0.1 collective-permute-start.7
  25.3 3.8 %collective-permute-start.5 = (bf16[128,576]{1,0:T(8,128)(2,1)S(1)}, bf16[128,576]{1,0:T(8,128)(2,1)S(1)}, u32[]{:S(2)}, u32[]{:S(2)}) collective-permute-start(bf16[128,576]{1,0:T(8,128)(2,1)S(1)} %collective-permute-done.2.refs_0_.refs_3_), channel_id=1, source_target_pairs={{0,16},{16,32},{32,48},{48,64},{64,80},{80,96},{96,112},{112,0},{1... | collective-permute-start | bytes 442376 | tf_op jit(solution)/shard_map/ppermute | solution.py:282
  29.1 1.1 %attend_own.6 = (f32[256,512]{1,0:T(8,128)S(1)}, f32[256,128]{1,0:T(8,128)S(1)}) custom-call(s32[1]{0:T(128)S(6)} %copy.7.len_ref, bf16[128,576]{1,0:T(8,128)(2,1)S(1)} %collective-permute-done.2.refs_0_.refs_3_, bf16[128,576]{1,0:T(8,128)(2,1)S(1)} %collective-permute-done.3.refs_1_.refs_4_, bf16[576,2048]{1,0:T(8,128)(2,1)S(1)} %bitcast.5), custom_call_target="tpu_custom_call" | custom-call | flops 1000000 | bytes 10000 | tf_op jit(solution)/shard_map/attend_own/pallas_call | solution.py:132
  30.2 1.4 %collective-permute-done.7.refs_2_.refs_7_ = bf16[128,576]{1,0:T(8,128)(2,1)S(1)} collective-permute-done((bf16[128,576]{1,0:T(8,128)(2,1)S(1)}, bf16[128,576]{1,0:T(8,128)(2,1)S(1)}, u32[]{:S(2)}, u32[]{:S(2)}) %collective-permute-start.7) | collective-permute-done | bytes 147488 | tf_op jit(solution)/shard_map/ppermute | solution.py:323
  31.6 1.4 %collective-permute-done.5.refs_0_.refs_5_ = bf16[128,576]{1,0:T(8,128)(2,1)S(1)} collective-permute-done((bf16[128,576]{1,0:T(8,128)(2,1)S(1)}, bf16[128,576]{1,0:T(8,128)(2,1)S(1)}, u32[]{:S(2)}, u32[]{:S(2)}) %collective-permute-start.5) | collective-permute-done | bytes 147488 | tf_op jit(solution)/shard_map/ppermute | solution.py:282
  33.1 0.8 %collective-permute-done.6.refs_1_.refs_6_ = bf16[128,576]{1,0:T(8,128)(2,1)S(1)} collective-permute-done((bf16[128,576]{1,0:T(8,128)(2,1)S(1)}, bf16[128,576]{1,0:T(8,128)(2,1)S(1)}, u32[]{:S(2)}, u32[]{:S(2)}) %collective-permute-start.6) | collective-permute-done | bytes 147488 | tf_op jit(solution)/shard_map/ppermute | solution.py:282
  33.9 1.2 %join.1.refs_16_ = bf16[608,1024]{1,0:T(8,128)(2,1)S(1)} custom-call(bf16[576,256]{1,0:T(8,128)(2,1)S(1)} %collective-permute-done.4.mine_ref, bf16[576,256]{1,0:T(8,128)(2,1)S(1)} %collective-permute-done.8.other_ref, bf16[608,512]{1,0:T(8,128)(2,1)} %collective-permute-done.9.direct_ref), custom_call_target="tpu_custom_call" | custom-call | flops 1000000 | bytes 10000 | tf_op jit(solution)/shard_map/join/pallas_call | solution.py:332
  35.1 4.7 %collective-permute-start.10 = (bf16[608,1024]{1,0:T(8,128)(2,1)S(1)}, bf16[608,1024]{1,0:T(8,128)(2,1)S(1)}, u32[]{:S(2)}, u32[]{:S(2)}) collective-permute-start(bf16[608,1024]{1,0:T(8,128)(2,1)S(1)} %join.1.refs_16_), channel_id=1, source_target_pairs={{0,1},{1,0},{2,3},{3,2},{4,5},{5,4},{6,7},{7,6},{8,9},{9,8},{10,11... | collective-permute-start | bytes 3735560 | tf_op jit(solution)/shard_map/ppermute | solution.py:279
  39.8 1.7 %attend_own.7 = (f32[384,512]{1,0:T(8,128)S(1)}, f32[384,128]{1,0:T(8,128)S(1)}) custom-call(s32[1]{0:T(128)S(6)} %copy.7.len_ref, bf16[128,576]{1,0:T(8,128)(2,1)S(1)} %collective-permute-done.5.refs_0_.refs_5_, bf16[128,576]{1,0:T(8,128)(2,1)S(1)} %collective-permute-done.6.refs_1_.refs_6_, bf16[128,576]{1,0:T(8,128)(2,1)S(1)} %collective-permute-done.7.refs_2_.refs_7_, ...), custom_call_target="tpu_custom_call" | custom-call | flops 1000000 | bytes 10000 | tf_op jit(solution)/shard_map/attend_own/pallas_call | solution.py:132
  41.5 0.9 %collective-permute-done.10.refs_17_ = bf16[608,1024]{1,0:T(8,128)(2,1)S(1)} collective-permute-done((bf16[608,1024]{1,0:T(8,128)(2,1)S(1)}, bf16[608,1024]{1,0:T(8,128)(2,1)S(1)}, u32[]{:S(2)}, u32[]{:S(2)}) %collective-permute-start.10) | collective-permute-done | bytes 1245216 | tf_op jit(solution)/shard_map/ppermute | solution.py:279
  42.4 9.5 %attend_final.1 = bf16[8,144,128]{2,1,0:T(8,128)(2,1)S(1)} custom-call(s32[256]{0:T(256)S(1)} %copy-done.5, bf16[128,576]{1,0:T(8,128)(2,1)S(1)} %get-tuple-element.36.refs_0_, bf16[128,576]{1,0:T(8,128)(2,1)S(1)} %collective-permute-done.refs_0_.refs_1_, bf16[128,576]{1,0:T(8,128)(2,1)S(1)} %collective-permute-done.1.refs_1_.refs_2_, ...), custom_call_target="tpu_custom_call" | custom-call | flops 1000000 | bytes 10000 | tf_op jit(solution)/shard_map/attend_final/pallas_call | solution.py:345
  51.9 16.4 %all_to_all.5.part_ref = bf16[8,144,128]{2,1,0:T(8,128)(2,1)} all-to-all(bf16[8,144,128]{2,1,0:T(8,128)(2,1)S(1)} %attend_final.1), channel_id=1, replica_groups={{0,16,32,48,64,80,96,112},{128,144,160,176,192,208,224,240},{1,17,33,49..., dimensions={0} | all-to-all | bytes 589824 | tf_op jit(solution)/shard_map/all_to_all | solution.py:355
  68.4 2.0 %merge.1 = bf16[128,128]{1,0:T(8,128)(2,1)} custom-call(bf16[8,144,128]{2,1,0:T(8,128)(2,1)} %all_to_all.5.part_ref), custom_call_target="tpu_custom_call" | custom-call | tf_op jit(solution)/shard_map/merge/pallas_call | solution.py:358
  (20 shorter events, 0.1 us)
Async XLA Ops:
  0.7 11.6 %copy-start = (bf16[2048,576]{0,1:T(8,128)(2,1)S(1)}, bf16[2048,576]{0,1:T(8,128)(2,1)}, u32[]{:S(2)}) copy-start(bf16[2048,576]{0,1:T(8,128)(2,1)} %param.7) | copy-start | bytes 7077892
  3.0 10.8 %collective-permute-start.1 = (bf16[128,576]{1,0:T(8,128)(2,1)S(1)}, bf16[128,576]{1,0:T(8,128)(2,1)S(1)}, u32[]{:S(2)}, u32[]{:S(2)}) collective-permute-start(bf16[128,576]{1,0:T(8,128)(2,1)S(1)} %get-tuple-element.36.refs_0_), channel_id=1, source_target_pairs={{0,112},{16,0},{32,16},{48,32},{64,48},{80,64},{96,80},{112,96},{1... | collective-permute-start | bytes 442376 | tf_op jit(solution)/shard_map/ppermute | solution.py:282
  9.5 6.0 %collective-permute-start = (bf16[128,576]{1,0:T(8,128)(2,1)S(1)}, bf16[128,576]{1,0:T(8,128)(2,1)S(1)}, u32[]{:S(2)}, u32[]{:S(2)}) collective-permute-start(bf16[128,576]{1,0:T(8,128)(2,1)S(1)} %get-tuple-element.36.refs_0_), channel_id=1, source_target_pairs={{0,16},{16,32},{32,48},{48,64},{64,80},{80,96},{96,112},{112,0},{1... | collective-permute-start | bytes 442376 | tf_op jit(solution)/shard_map/ppermute | solution.py:282
  9.5 12.5 %collective-permute-start.4 = (bf16[576,256]{1,0:T(8,128)(2,1)}, bf16[576,256]{1,0:T(8,128)(2,1)S(1)}, u32[]{:S(2)}, u32[]{:S(2)}) collective-permute-start(bf16[576,256]{1,0:T(8,128)(2,1)} %get-tuple-element.44), channel_id=1, source_target_pairs={{0,136},{1,137},{2,138},{3,139},{4,140},{5,141},{6,142},{7,143},{8... | collective-permute-start | bytes 884744 | tf_op jit(solution)/shard_map/ppermute | solution.py:276
  13.1 0.7 %copy-start.2 = (f32[128,512]{1,0:T(8,128)}, f32[128,512]{1,0:T(8,128)S(1)}, u32[]{:S(2)}) copy-start(f32[128,512]{1,0:T(8,128)S(1)} %get-tuple-element.54.refs_8_) | copy-start | bytes 786436
  15.4 18.4 %collective-permute-start.9 = (bf16[608,512]{1,0:T(8,128)(2,1)}, bf16[608,512]{1,0:T(8,128)(2,1)}, u32[]{:S(2)}, u32[]{:S(2)}) collective-permute-start(bf16[608,512]{1,0:T(8,128)(2,1)} %get-tuple-element.50), channel_id=1, source_target_pairs={{0,136},{1,137},{2,138},{3,139},{4,140},{5,141},{6,142},{7,143},{8... | collective-permute-start | bytes 1867784 | tf_op jit(solution)/shard_map/ppermute | solution.py:276
  18.2 5.8 %collective-permute-start.2 = (bf16[128,576]{1,0:T(8,128)(2,1)S(1)}, bf16[128,576]{1,0:T(8,128)(2,1)S(1)}, u32[]{:S(2)}, u32[]{:S(2)}) collective-permute-start(bf16[128,576]{1,0:T(8,128)(2,1)S(1)} %collective-permute-done.refs_0_.refs_1_), channel_id=1, source_target_pairs={{0,16},{16,32},{32,48},{48,64},{64,80},{80,96},{96,112},{112,0},{1... | collective-permute-start | bytes 442376 | tf_op jit(solution)/shard_map/ppermute | solution.py:282
  18.2 5.8 %collective-permute-start.3 = (bf16[128,576]{1,0:T(8,128)(2,1)S(1)}, bf16[128,576]{1,0:T(8,128)(2,1)S(1)}, u32[]{:S(2)}, u32[]{:S(2)}) collective-permute-start(bf16[128,576]{1,0:T(8,128)(2,1)S(1)} %collective-permute-done.1.refs_1_.refs_2_), channel_id=1, source_target_pairs={{0,112},{16,0},{32,16},{48,32},{64,48},{80,64},{96,80},{112,96},{1... | collective-permute-start | bytes 442376 | tf_op jit(solution)/shard_map/ppermute | solution.py:282
  23.9 9.9 %collective-permute-start.8 = (bf16[576,256]{1,0:T(8,128)(2,1)S(1)}, bf16[576,256]{1,0:T(8,128)(2,1)S(1)}, u32[]{:S(2)}, u32[]{:S(2)}) collective-permute-start(bf16[576,256]{1,0:T(8,128)(2,1)S(1)} %collective-permute-done.4.mine_ref), channel_id=1, source_target_pairs={{0,2},{1,3},{2,0},{3,1},{4,6},{5,7},{6,4},{7,5},{8,10},{9,11},{10,... | collective-permute-start | bytes 884744 | tf_op jit(solution)/shard_map/ppermute | solution.py:321
  25.2 6.5 %collective-permute-start.7 = (bf16[128,576]{1,0:T(8,128)(2,1)S(1)}, bf16[128,576]{1,0:T(8,128)(2,1)S(1)}, u32[]{:S(2)}, u32[]{:S(2)}) collective-permute-start(bf16[128,576]{1,0:T(8,128)(2,1)S(1)} %broadcast_select_fusion), channel_id=1, source_target_pairs={{0,32},{16,112},{32,64},{48,16},{64,96},{80,48},{96,0},{112,80},{1... | collective-permute-start | bytes 442376 | tf_op jit(solution)/shard_map/ppermute | solution.py:323
  25.3 7.8 %collective-permute-start.5 = (bf16[128,576]{1,0:T(8,128)(2,1)S(1)}, bf16[128,576]{1,0:T(8,128)(2,1)S(1)}, u32[]{:S(2)}, u32[]{:S(2)}) collective-permute-start(bf16[128,576]{1,0:T(8,128)(2,1)S(1)} %collective-permute-done.2.refs_0_.refs_3_), channel_id=1, source_target_pairs={{0,16},{16,32},{32,48},{48,64},{64,80},{80,96},{96,112},{112,0},{1... | collective-permute-start | bytes 442376 | tf_op jit(solution)/shard_map/ppermute | solution.py:282
  29.1 4.8 %collective-permute-start.6 = (bf16[128,576]{1,0:T(8,128)(2,1)S(1)}, bf16[128,576]{1,0:T(8,128)(2,1)S(1)}, u32[]{:S(2)}, u32[]{:S(2)}) collective-permute-start(bf16[128,576]{1,0:T(8,128)(2,1)S(1)} %collective-permute-done.3.refs_1_.refs_4_), channel_id=1, source_target_pairs={{0,112},{16,0},{32,16},{48,32},{64,48},{80,64},{96,80},{112,96},{1... | collective-permute-start | bytes 442376 | tf_op jit(solution)/shard_map/ppermute | solution.py:282
  35.1 7.3 %copy-start.1 = (bf16[8,512,128]{2,1,0:T(8,128)(2,1)S(1)}, bf16[8,512,128]{2,1,0:T(8,128)(2,1)}, u32[]{:S(2)}) copy-start(bf16[8,512,128]{2,1,0:T(8,128)(2,1)} %refs_19_.1) | copy-start | bytes 3145732
  35.1 7.3 %copy-start.3 = (f32[128,512]{1,0:T(8,128)S(1)}, f32[128,512]{1,0:T(8,128)}, u32[]{:S(2)}) copy-start(f32[128,512]{1,0:T(8,128)} %copy-done.2) | copy-start | bytes 786436
  35.1 7.3 %copy-start.4 = (bf16[16,576]{1,0:T(8,128)(2,1)S(1)}, bf16[16,576]{1,0:T(8,128)(2,1)}, u32[]{:S(2)}) copy-start(bf16[16,576]{1,0:T(8,128)(2,1)} %refs_18_.1) | copy-start | bytes 55300
  35.1 7.3 %copy-start.5 = (s32[256]{0:T(256)S(1)}, s32[256]{0:T(256)}, u32[]{:S(2)}) copy-start(s32[256]{0:T(256)} %offset_ref.1) | copy-start | bytes 3076
  35.1 7.2 %collective-permute-start.10 = (bf16[608,1024]{1,0:T(8,128)(2,1)S(1)}, bf16[608,1024]{1,0:T(8,128)(2,1)S(1)}, u32[]{:S(2)}, u32[]{:S(2)}) collective-permute-start(bf16[608,1024]{1,0:T(8,128)(2,1)S(1)} %join.1.refs_16_), channel_id=1, source_target_pairs={{0,1},{1,0},{2,3},{3,2},{4,5},{5,4},{6,7},{7,6},{8,9},{9,8},{10,11... | collective-permute-start | bytes 3735560 | tf_op jit(solution)/shard_map/ppermute | solution.py:279

commit v2 on v1

--- a/solution.py
+++ b/solution.py
@@ -313,12 +313,14 @@
 
     state0 = attend_own(cache_lengths, [own], keys)
     up1, down1 = shift(own, 1), shift(own, -1)
-    up1, down1, state0, direct = lax.optimization_barrier((up1, down1, state0, direct))
+    state0, direct = lax.optimization_barrier((state0, direct))
     direct = across(direct)
+    up1, down1, state0 = lax.optimization_barrier((up1, down1, state0))
     up2, down2 = shift(up1, 1), shift(down1, -1)
     state1 = attend_own(cache_lengths, [up1, down1], keys)
-    up2, down2, state1, mine = lax.optimization_barrier((up2, down2, state1, mine))
+    state1, mine = lax.optimization_barrier((state1, mine))
     other = lax.ppermute(mine, "head", [(h, h ^ 2) for h in range(16)])
+    up2, down2, state1 = lax.optimization_barrier((up2, down2, state1))
     up3, down3 = shift(up2, 1), shift(down2, -1)
     four = lax.ppermute(
         jnp.where(z % 2 == 0, up2, down2),
@@ -362,7 +364,7 @@
         out_shape=jax.ShapeDtypeStruct((rows, VDIM), jnp.bfloat16),
         scratch_shapes=[pltpu.VMEM((rows, VDIM), jnp.float32)],
         name="merge",
-    )(got)
+    )(pltpu.with_memory_space_constraint(got, pltpu.VMEM))
     return out.reshape(own_tokens, head_local, VDIM)
 
 

time: 70.1 us -> 66.4 us (0.947)
  starting transfers between devices: 24.4 us -> 20.5 us
  Pallas kernels: 19.8 us -> 22.3 us
  waiting for transfers between devices: 8.16 us -> 5.98 us
    pallas_call x4, Pallas kernels: 4.74 us -> 8.22 us  [attend_own(): pl.pallas_call(functools.partial(own_kernel, len(blocks)), in_specs=[SMEM...]
    ppermute x2, starting transfers between devices: 5.47 us -> 2.74 us  [across(): return lax.ppermute(a, ('ctx', 'head'), moves)]
    ppermute x6, waiting for transfers between devices: 5.85 us -> 4.46 us  [shift(): lax.ppermute(a, 'ctx', [(c, c // NZ * NZ + (c + step) % NZ) for c in rang...]
    ppermute x1, starting transfers between devices: 4.67 us -> 3.51 us  [swap(): return lax.ppermute(a, 'head', [(h, h ^ 1) for h in range(16)])]
    pallas_call x1, Pallas kernels: 1.95 us -> 0.99 us  [shards(): pl.pallas_call(merge_kernel, in_specs=[VMEM], out_specs=VMEM, out_shape=j...]
    ppermute x2, waiting for transfers between devices: 0.01 us -> 0.89 us  [across(): return lax.ppermute(a, ('ctx', 'head'), moves)]
    ppermute x1, waiting for transfers between devices: 0.87 us -> 0.01 us  [swap(): return lax.ppermute(a, 'head', [(h, h ^ 1) for h in range(16)])]
    ppermute x1, waiting for transfers between devices: 1.43 us -> 0.62 us  [shards(): lax.ppermute(jnp.where(z % 2 == 0, up2, down2), 'ctx', [(c, c // NZ * NZ...]
  transfers between devices with their start and end apart: 11 -> 11, of which waited for: 6 -> 6; matrix products, arithmetic and copies ran while one was open for 0% -> 0% of each run, Pallas kernels for 7% -> 12%
where the time goes in v2:
time: 66.4 us; the launch traced here: 66.3 us
  Pallas kernels  22.3 us (34%)
  starting transfers between devices  20.5 us (31%)
  blocking collectives  15.9 us (24%)
  waiting for transfers between devices  5.98 us (9%)
  between operations  0.83 us (1%)
  local copies, waits for them, and re-layouts  0.73 us (1%)
    all_to_all x1, blocking collectives, shards(): lax.all_to_all(parts, 'ctx', 0, 0, axis_index_groups=[[*range(NZ)], [*ran...  15.9 us
    ppermute x6, starting transfers between devices, shift(): lax.ppermute(a, 'ctx', [(c, c // NZ * NZ + (c + step) % NZ) for c in rang...  13 us
    pallas_call x1, Pallas kernels, shards(): pl.pallas_call(functools.partial(final_kernel, [1, 2, 2, 3]), in_specs=[S...  9.54 us
    pallas_call x4, Pallas kernels, attend_own(): pl.pallas_call(functools.partial(own_kernel, len(blocks)), in_specs=[SMEM...  8.22 us
    ppermute x6, waiting for transfers between devices, shift(): lax.ppermute(a, 'ctx', [(c, c // NZ * NZ + (c + step) % NZ) for c in rang...  4.46 us
    ppermute x1, starting transfers between devices, swap(): return lax.ppermute(a, 'head', [(h, h ^ 1) for h in range(16)])  3.51 us
    ppermute x2, starting transfers between devices, across(): return lax.ppermute(a, ('ctx', 'head'), moves)  2.74 us
    pallas_call x1, Pallas kernels, shards(): pl.pallas_call(pack_kernel, in_specs=[SMEM, hbm, hbm, hbm], out_specs=[hb...  2.31 us
  transfers between devices with their start and end apart: 11, of which 6 were waited for; matrix products, arithmetic and copies ran while one was open for 0% of the time, Pallas kernels for 12%

profile of v2, /device:TPU:1, one launch (start us, length us, event | category | flops | bytes accessed | tf_op | source)
XLA Modules:
  0.0 66.3 jit_solution(9810020336004470640)
XLA Ops:
  0.7 2.3 %pack.1 = (bf16[576,256]{1,0:T(8,128)(2,1)}, bf16[608,512]{1,0:T(8,128)(2,1)}, bf16[128,576]{1,0:T(8,128)(2,1)S(1)}) custom-call(s32[1]{0:T(128)S(6)} %copy.7.len_ref, bf16[576,2048]{1,0:T(8,128)(2,1)} %bitcast.2, bf16[16,576]{1,0:T(8,128)(2,1)} %refs_18_.1, bf16[16,8,576]{2,1,0:T(8,128)(2,1)} %query_ref.1), custom_call_target="tpu_custom_call" | custom-call | tf_op jit(solution)/shard_map/pack/pallas_call | solution.py:288
  3.0 6.5 %collective-permute-start.1 = (bf16[128,576]{1,0:T(8,128)(2,1)S(1)}, bf16[128,576]{1,0:T(8,128)(2,1)S(1)}, u32[]{:S(2)}, u32[]{:S(2)}) collective-permute-start(bf16[128,576]{1,0:T(8,128)(2,1)S(1)} %get-tuple-element.40.refs_0_), channel_id=1, source_target_pairs={{0,112},{16,0},{32,16},{48,32},{64,48},{80,64},{96,80},{112,96},{1... | collective-permute-start | bytes 442376 | tf_op jit(solution)/shard_map/ppermute | solution.py:282
  9.5 2.7 %collective-permute-start.4 = (bf16[576,256]{1,0:T(8,128)(2,1)}, bf16[576,256]{1,0:T(8,128)(2,1)S(1)}, u32[]{:S(2)}, u32[]{:S(2)}) collective-permute-start(bf16[576,256]{1,0:T(8,128)(2,1)} %get-tuple-element.50), channel_id=1, source_target_pairs={{0,136},{1,137},{2,138},{3,139},{4,140},{5,141},{6,142},{7,143},{8... | collective-permute-start | bytes 884744 | tf_op jit(solution)/shard_map/ppermute | solution.py:276
  12.2 1.5 %attend_own.4 = (f32[128,512]{1,0:T(8,128)S(1)}, f32[128,128]{1,0:T(8,128)S(1)}) custom-call(s32[1]{0:T(128)S(6)} %copy.7.len_ref, bf16[128,576]{1,0:T(8,128)(2,1)S(1)} %get-tuple-element.40.refs_0_, bf16[576,2048]{1,0:T(8,128)(2,1)S(1)} %bitcast.3), custom_call_target="tpu_custom_call" | custom-call | flops 1000000 | bytes 10000 | tf_op jit(solution)/shard_map/attend_own/pallas_call | solution.py:132
  13.7 0.7 %copy-done.2 = f32[128,512]{1,0:T(8,128)} copy-done((f32[128,512]{1,0:T(8,128)}, f32[128,512]{1,0:T(8,128)S(1)}, u32[]{:S(2)}) %copy-start.2) | copy-done | bytes 262168
  14.4 1.0 %collective-permute-done.refs_0_.refs_1_ = bf16[128,576]{1,0:T(8,128)(2,1)S(1)} collective-permute-done((bf16[128,576]{1,0:T(8,128)(2,1)S(1)}, bf16[128,576]{1,0:T(8,128)(2,1)S(1)}, u32[]{:S(2)}, u32[]{:S(2)}) %collective-permute-start) | collective-permute-done | bytes 147488 | tf_op jit(solution)/shard_map/ppermute | solution.py:282
  15.4 2.7 %collective-permute-start.3 = (bf16[128,576]{1,0:T(8,128)(2,1)S(1)}, bf16[128,576]{1,0:T(8,128)(2,1)S(1)}, u32[]{:S(2)}, u32[]{:S(2)}) collective-permute-start(bf16[128,576]{1,0:T(8,128)(2,1)S(1)} %collective-permute-done.1.refs_1_.refs_2_), channel_id=1, source_target_pairs={{0,112},{16,0},{32,16},{48,32},{64,48},{80,64},{96,80},{112,96},{1... | collective-permute-start | bytes 442376 | tf_op jit(solution)/shard_map/ppermute | solution.py:282
  18.1 1.9 %attend_own.5 = (f32[256,512]{1,0:T(8,128)S(1)}, f32[256,128]{1,0:T(8,128)S(1)}) custom-call(s32[1]{0:T(128)S(6)} %copy.7.len_ref, bf16[128,576]{1,0:T(8,128)(2,1)S(1)} %collective-permute-done.refs_0_.refs_1_, bf16[128,576]{1,0:T(8,128)(2,1)S(1)} %collective-permute-done.1.refs_1_.refs_2_, bf16[576,2048]{1,0:T(8,128)(2,1)S(1)} %bitcast.4), custom_call_target="tpu_custom_call" | custom-call | flops 1000000 | bytes 10000 | tf_op jit(solution)/shard_map/attend_own/pallas_call | solution.py:132
  20.0 1.1 %collective-permute-done.2.refs_0_.refs_3_ = bf16[128,576]{1,0:T(8,128)(2,1)S(1)} collective-permute-done((bf16[128,576]{1,0:T(8,128)(2,1)S(1)}, bf16[128,576]{1,0:T(8,128)(2,1)S(1)}, u32[]{:S(2)}, u32[]{:S(2)}) %collective-permute-start.2) | collective-permute-done | bytes 147488 | tf_op jit(solution)/shard_map/ppermute | solution.py:282
  21.1 1.2 %collective-permute-start.8 = (bf16[576,256]{1,0:T(8,128)(2,1)S(1)}, bf16[576,256]{1,0:T(8,128)(2,1)S(1)}, u32[]{:S(2)}, u32[]{:S(2)}) collective-permute-start(bf16[576,256]{1,0:T(8,128)(2,1)S(1)} %collective-permute-done.4.mine_ref), channel_id=1, source_target_pairs={{0,2},{1,3},{2,0},{3,1},{4,6},{5,7},{6,4},{7,5},{8,10},{9,11},{10,... | collective-permute-start | bytes 884744 | tf_op jit(solution)/shard_map/ppermute | solution.py:322
  22.3 0.1 collective-permute-start.7
  22.4 3.8 %collective-permute-start.5 = (bf16[128,576]{1,0:T(8,128)(2,1)S(1)}, bf16[128,576]{1,0:T(8,128)(2,1)S(1)}, u32[]{:S(2)}, u32[]{:S(2)}) collective-permute-start(bf16[128,576]{1,0:T(8,128)(2,1)S(1)} %collective-permute-done.2.refs_0_.refs_3_), channel_id=1, source_target_pairs={{0,16},{16,32},{32,48},{48,64},{64,80},{80,96},{96,112},{112,0},{1... | collective-permute-start | bytes 442376 | tf_op jit(solution)/shard_map/ppermute | solution.py:282
  26.3 1.9 %attend_own.6 = (f32[256,512]{1,0:T(8,128)S(1)}, f32[256,128]{1,0:T(8,128)S(1)}) custom-call(s32[1]{0:T(128)S(6)} %copy.7.len_ref, bf16[128,576]{1,0:T(8,128)(2,1)S(1)} %collective-permute-done.2.refs_0_.refs_3_, bf16[128,576]{1,0:T(8,128)(2,1)S(1)} %collective-permute-done.3.refs_1_.refs_4_, bf16[576,2048]{1,0:T(8,128)(2,1)S(1)} %bitcast.5), custom_call_target="tpu_custom_call" | custom-call | flops 1000000 | bytes 10000 | tf_op jit(solution)/shard_map/attend_own/pallas_call | solution.py:132
  28.2 0.6 collective-permute-done.7.refs_2_.refs_7_
  28.8 1.4 %collective-permute-done.5.refs_0_.refs_5_ = bf16[128,576]{1,0:T(8,128)(2,1)S(1)} collective-permute-done((bf16[128,576]{1,0:T(8,128)(2,1)S(1)}, bf16[128,576]{1,0:T(8,128)(2,1)S(1)}, u32[]{:S(2)}, u32[]{:S(2)}) %collective-permute-start.5) | collective-permute-done | bytes 147488 | tf_op jit(solution)/shard_map/ppermute | solution.py:282
  30.2 0.9 %collective-permute-done.6.refs_1_.refs_6_ = bf16[128,576]{1,0:T(8,128)(2,1)S(1)} collective-permute-done((bf16[128,576]{1,0:T(8,128)(2,1)S(1)}, bf16[128,576]{1,0:T(8,128)(2,1)S(1)}, u32[]{:S(2)}, u32[]{:S(2)}) %collective-permute-start.6) | collective-permute-done | bytes 147488 | tf_op jit(solution)/shard_map/ppermute | solution.py:282
  31.1 0.9 %collective-permute-done.9.direct_ref = bf16[608,512]{1,0:T(8,128)(2,1)} collective-permute-done((bf16[608,512]{1,0:T(8,128)(2,1)}, bf16[608,512]{1,0:T(8,128)(2,1)}, u32[]{:S(2)}, u32[]{:S(2)}) %collective-permute-start.9) | collective-permute-done | bytes 622624 | tf_op jit(solution)/shard_map/ppermute | solution.py:276
  32.0 1.2 %join.1.refs_16_ = bf16[608,1024]{1,0:T(8,128)(2,1)S(1)} custom-call(bf16[576,256]{1,0:T(8,128)(2,1)S(1)} %collective-permute-done.4.mine_ref, bf16[576,256]{1,0:T(8,128)(2,1)S(1)} %collective-permute-done.8.other_ref, bf16[608,512]{1,0:T(8,128)(2,1)} %collective-permute-done.9.direct_ref), custom_call_target="tpu_custom_call" | custom-call | flops 1000000 | bytes 10000 | tf_op jit(solution)/shard_map/join/pallas_call | solution.py:334
  33.2 0.0 copy-start.1
  33.3 3.5 %collective-permute-start.10 = (bf16[608,1024]{1,0:T(8,128)(2,1)S(1)}, bf16[608,1024]{1,0:T(8,128)(2,1)S(1)}, u32[]{:S(2)}, u32[]{:S(2)}) collective-permute-start(bf16[608,1024]{1,0:T(8,128)(2,1)S(1)} %join.1.refs_16_), channel_id=1, source_target_pairs={{0,1},{1,0},{2,3},{3,2},{4,5},{5,4},{6,7},{7,6},{8,9},{9,8},{10,11... | collective-permute-start | bytes 3735560 | tf_op jit(solution)/shard_map/ppermute | solution.py:279
  36.8 3.0 %attend_own.7 = (f32[384,512]{1,0:T(8,128)S(1)}, f32[384,128]{1,0:T(8,128)S(1)}) custom-call(s32[1]{0:T(128)S(6)} %copy.7.len_ref, bf16[128,576]{1,0:T(8,128)(2,1)S(1)} %collective-permute-done.5.refs_0_.refs_5_, bf16[128,576]{1,0:T(8,128)(2,1)S(1)} %collective-permute-done.6.refs_1_.refs_6_, bf16[128,576]{1,0:T(8,128)(2,1)S(1)} %collective-permute-done.7.refs_2_.refs_7_, ...), custom_call_target="tpu_custom_call" | custom-call | flops 1000000 | bytes 10000 | tf_op jit(solution)/shard_map/attend_own/pallas_call | solution.py:132
  39.8 9.5 %attend_final.1 = bf16[8,144,128]{2,1,0:T(8,128)(2,1)S(1)} custom-call(s32[256]{0:T(256)S(1)} %copy-done.5, bf16[128,576]{1,0:T(8,128)(2,1)S(1)} %get-tuple-element.40.refs_0_, bf16[128,576]{1,0:T(8,128)(2,1)S(1)} %collective-permute-done.refs_0_.refs_1_, bf16[128,576]{1,0:T(8,128)(2,1)S(1)} %collective-permute-done.1.refs_1_.refs_2_, ...), custom_call_target="tpu_custom_call" | custom-call | flops 1000000 | bytes 10000 | tf_op jit(solution)/shard_map/attend_final/pallas_call | solution.py:347
  49.4 15.9 %all_to_all.5.part_ref = bf16[8,144,128]{2,1,0:T(8,128)(2,1)S(1)} all-to-all(bf16[8,144,128]{2,1,0:T(8,128)(2,1)S(1)} %attend_final.1), channel_id=1, replica_groups={{0,16,32,48,64,80,96,112},{128,144,160,176,192,208,224,240},{1,17,33,49..., dimensions={0} | all-to-all | bytes 589824 | tf_op jit(solution)/shard_map/all_to_all | solution.py:357
  65.3 1.0 %merge.1 = bf16[128,128]{1,0:T(8,128)(2,1)} custom-call(bf16[8,144,128]{2,1,0:T(8,128)(2,1)S(1)} %all_to_all.5.part_ref), custom_call_target="tpu_custom_call" | custom-call | tf_op jit(solution)/shard_map/merge/pallas_call | solution.py:360
  (20 shorter events, 0.1 us)
Async XLA Ops:
  0.7 11.6 %copy-start = (bf16[2048,576]{0,1:T(8,128)(2,1)S(1)}, bf16[2048,576]{0,1:T(8,128)(2,1)}, u32[]{:S(2)}) copy-start(bf16[2048,576]{0,1:T(8,128)(2,1)} %param.7) | copy-start | bytes 7077892
  3.0 11.4 %collective-permute-start.1 = (bf16[128,576]{1,0:T(8,128)(2,1)S(1)}, bf16[128,576]{1,0:T(8,128)(2,1)S(1)}, u32[]{:S(2)}, u32[]{:S(2)}) collective-permute-start(bf16[128,576]{1,0:T(8,128)(2,1)S(1)} %get-tuple-element.40.refs_0_), channel_id=1, source_target_pairs={{0,112},{16,0},{32,16},{48,32},{64,48},{80,64},{96,80},{112,96},{1... | collective-permute-start | bytes 442376 | tf_op jit(solution)/shard_map/ppermute | solution.py:282
  9.5 6.0 %collective-permute-start = (bf16[128,576]{1,0:T(8,128)(2,1)S(1)}, bf16[128,576]{1,0:T(8,128)(2,1)S(1)}, u32[]{:S(2)}, u32[]{:S(2)}) collective-permute-start(bf16[128,576]{1,0:T(8,128)(2,1)S(1)} %get-tuple-element.40.refs_0_), channel_id=1, source_target_pairs={{0,16},{16,32},{32,48},{48,64},{64,80},{80,96},{96,112},{112,0},{1... | collective-permute-start | bytes 442376 | tf_op jit(solution)/shard_map/ppermute | solution.py:282
  9.5 10.5 %collective-permute-start.4 = (bf16[576,256]{1,0:T(8,128)(2,1)}, bf16[576,256]{1,0:T(8,128)(2,1)S(1)}, u32[]{:S(2)}, u32[]{:S(2)}) collective-permute-start(bf16[576,256]{1,0:T(8,128)(2,1)} %get-tuple-element.50), channel_id=1, source_target_pairs={{0,136},{1,137},{2,138},{3,139},{4,140},{5,141},{6,142},{7,143},{8... | collective-permute-start | bytes 884744 | tf_op jit(solution)/shard_map/ppermute | solution.py:276
  13.7 0.7 %copy-start.2 = (f32[128,512]{1,0:T(8,128)}, f32[128,512]{1,0:T(8,128)S(1)}, u32[]{:S(2)}) copy-start(f32[128,512]{1,0:T(8,128)S(1)} %get-tuple-element.62.refs_8_) | copy-start | bytes 786436
  14.4 17.6 %collective-permute-start.9 = (bf16[608,512]{1,0:T(8,128)(2,1)}, bf16[608,512]{1,0:T(8,128)(2,1)}, u32[]{:S(2)}, u32[]{:S(2)}) collective-permute-start(bf16[608,512]{1,0:T(8,128)(2,1)} %get-tuple-element.58), channel_id=1, source_target_pairs={{0,136},{1,137},{2,138},{3,139},{4,140},{5,141},{6,142},{7,143},{8... | collective-permute-start | bytes 1867784 | tf_op jit(solution)/shard_map/ppermute | solution.py:276
  15.4 5.7 %collective-permute-start.2 = (bf16[128,576]{1,0:T(8,128)(2,1)S(1)}, bf16[128,576]{1,0:T(8,128)(2,1)S(1)}, u32[]{:S(2)}, u32[]{:S(2)}) collective-permute-start(bf16[128,576]{1,0:T(8,128)(2,1)S(1)} %collective-permute-done.refs_0_.refs_1_), channel_id=1, source_target_pairs={{0,16},{16,32},{32,48},{48,64},{64,80},{80,96},{96,112},{112,0},{1... | collective-permute-start | bytes 442376 | tf_op jit(solution)/shard_map/ppermute | solution.py:282
  15.4 5.7 %collective-permute-start.3 = (bf16[128,576]{1,0:T(8,128)(2,1)S(1)}, bf16[128,576]{1,0:T(8,128)(2,1)S(1)}, u32[]{:S(2)}, u32[]{:S(2)}) collective-permute-start(bf16[128,576]{1,0:T(8,128)(2,1)S(1)} %collective-permute-done.1.refs_1_.refs_2_), channel_id=1, source_target_pairs={{0,112},{16,0},{32,16},{48,32},{64,48},{80,64},{96,80},{112,96},{1... | collective-permute-start | bytes 442376 | tf_op jit(solution)/shard_map/ppermute | solution.py:282
  21.1 10.0 %collective-permute-start.8 = (bf16[576,256]{1,0:T(8,128)(2,1)S(1)}, bf16[576,256]{1,0:T(8,128)(2,1)S(1)}, u32[]{:S(2)}, u32[]{:S(2)}) collective-permute-start(bf16[576,256]{1,0:T(8,128)(2,1)S(1)} %collective-permute-done.4.mine_ref), channel_id=1, source_target_pairs={{0,2},{1,3},{2,0},{3,1},{4,6},{5,7},{6,4},{7,5},{8,10},{9,11},{10,... | collective-permute-start | bytes 884744 | tf_op jit(solution)/shard_map/ppermute | solution.py:322
  22.3 6.5 %collective-permute-start.7 = (bf16[128,576]{1,0:T(8,128)(2,1)S(1)}, bf16[128,576]{1,0:T(8,128)(2,1)S(1)}, u32[]{:S(2)}, u32[]{:S(2)}) collective-permute-start(bf16[128,576]{1,0:T(8,128)(2,1)S(1)} %broadcast_select_fusion), channel_id=1, source_target_pairs={{0,32},{16,112},{32,64},{48,16},{64,96},{80,48},{96,0},{112,80},{1... | collective-permute-start | bytes 442376 | tf_op jit(solution)/shard_map/ppermute | solution.py:325
  22.4 7.8 %collective-permute-start.5 = (bf16[128,576]{1,0:T(8,128)(2,1)S(1)}, bf16[128,576]{1,0:T(8,128)(2,1)S(1)}, u32[]{:S(2)}, u32[]{:S(2)}) collective-permute-start(bf16[128,576]{1,0:T(8,128)(2,1)S(1)} %collective-permute-done.2.refs_0_.refs_3_), channel_id=1, source_target_pairs={{0,16},{16,32},{32,48},{48,64},{64,80},{80,96},{96,112},{112,0},{1... | collective-permute-start | bytes 442376 | tf_op jit(solution)/shard_map/ppermute | solution.py:282
  26.3 4.9 %collective-permute-start.6 = (bf16[128,576]{1,0:T(8,128)(2,1)S(1)}, bf16[128,576]{1,0:T(8,128)(2,1)S(1)}, u32[]{:S(2)}, u32[]{:S(2)}) collective-permute-start(bf16[128,576]{1,0:T(8,128)(2,1)S(1)} %collective-permute-done.3.refs_1_.refs_4_), channel_id=1, source_target_pairs={{0,112},{16,0},{32,16},{48,32},{64,48},{80,64},{96,80},{112,96},{1... | collective-permute-start | bytes 442376 | tf_op jit(solution)/shard_map/ppermute | solution.py:282
  33.2 6.6 %copy-start.1 = (bf16[8,512,128]{2,1,0:T(8,128)(2,1)S(1)}, bf16[8,512,128]{2,1,0:T(8,128)(2,1)}, u32[]{:S(2)}) copy-start(bf16[8,512,128]{2,1,0:T(8,128)(2,1)} %refs_19_.1) | copy-start | bytes 3145732
  33.3 6.6 %copy-start.3 = (f32[128,512]{1,0:T(8,128)S(1)}, f32[128,512]{1,0:T(8,128)}, u32[]{:S(2)}) copy-start(f32[128,512]{1,0:T(8,128)} %copy-done.2) | copy-start | bytes 786436
  33.3 6.6 %copy-start.4 = (bf16[16,576]{1,0:T(8,128)(2,1)S(1)}, bf16[16,576]{1,0:T(8,128)(2,1)}, u32[]{:S(2)}) copy-start(bf16[16,576]{1,0:T(8,128)(2,1)} %refs_18_.1) | copy-start | bytes 55300
  33.3 6.5 %copy-start.5 = (s32[256]{0:T(256)S(1)}, s32[256]{0:T(256)}, u32[]{:S(2)}) copy-start(s32[256]{0:T(256)} %offset_ref.1) | copy-start | bytes 3076
  33.3 6.5 %collective-permute-start.10 = (bf16[608,1024]{1,0:T(8,128)(2,1)S(1)}, bf16[608,1024]{1,0:T(8,128)(2,1)S(1)}, u32[]{:S(2)}, u32[]{:S(2)}) collective-permute-start(bf16[608,1024]{1,0:T(8,128)(2,1)S(1)} %join.1.refs_16_), channel_id=1, source_target_pairs={{0,1},{1,0},{2,3},{3,2},{4,5},{5,4},{6,7},{7,6},{8,9},{9,8},{10,11... | collective-permute-start | bytes 3735560 | tf_op jit(solution)/shard_map/ppermute | solution.py:279

commit v3 on v2

--- a/solution.py
+++ b/solution.py
@@ -41,31 +41,32 @@
     return jnp.where(position < valid, 0.0, masked_value)
 
 
-def pack_kernel(
-    len_ref, keys_ref, new_ref, query_ref, shared_ref, direct_ref, rows_ref, stage_ref, new_vmem, query_vmem, flat_ref, sems
-):
+def pack_kernel(len_ref, keys_ref, new_ref, shared_ref, direct_ref, stage_ref, new_vmem, sems):
     head = lax.axis_index("head")
     core, side = lax.rem(head, 2), lax.rem(head // 2, 2)
     lat, few = shared_ref.shape
     width = direct_ref.shape[1]
-    half = 2 * few + width
-    own_tokens, heads, _ = query_ref.shape
-    part = pl.multiple_of(core * half + side * few, 128)
-    rest = pl.multiple_of(core * half + 2 * few, 128)
-    load_query = pltpu.make_async_copy(query_ref, query_vmem, sems.at[0])
-    load_new = pltpu.make_async_copy(new_ref, new_vmem, sems.at[1])
-    load_shared = pltpu.make_async_copy(
-        keys_ref.at[:, pl.ds(part, few)], stage_ref.at[0:lat, 0:few], sems.at[2]
-    )
-    load_direct = pltpu.make_async_copy(
-        keys_ref.at[:, pl.ds(rest, width)], stage_ref.at[0:lat, few : few + width], sems.at[3]
-    )
-    send_shared = pltpu.make_async_copy(stage_ref.at[0:lat, 0:few], shared_ref, sems.at[4])
-    send_direct = pltpu.make_async_copy(stage_ref.at[:, few : few + width], direct_ref, sems.at[5])
-    load_shared.start()
-    load_query.start()
-    load_new.start()
-    load_direct.start()
+    early, late = few // 128, width // 128
+
+    def load(run, slot):
+        place = pl.multiple_of((2 * run + core) * 128, 128)
+        return pltpu.make_async_copy(
+            keys_ref.at[:, pl.ds(place, 128)],
+            stage_ref.at[0:lat, slot * 128 : (slot + 1) * 128],
+            sems.at[slot],
+        )
+
+    loads = [load(side * early + i, i) for i in range(early)]
+    loads += [load(2 * early + i, early + i) for i in range(late)]
+    load_new = pltpu.make_async_copy(new_ref, new_vmem, sems.at[early + late])
+    send_shared = pltpu.make_async_copy(
+        stage_ref.at[0:lat, 0:few], shared_ref, sems.at[early + late + 1]
+    )
+    send_direct = pltpu.make_async_copy(
+        stage_ref.at[:, few : few + width], direct_ref, sems.at[early + late + 2]
+    )
+    for copy in loads[:early] + [load_new] + loads[early:]:
+        copy.start()
     length = len_ref[0]
     high = length // 256
     r = lax.broadcasted_iota(jnp.int32, (16, 128), 0)
@@ -74,23 +75,14 @@
         (r == 0) & (c == 0), high, jnp.where((r == 0) & (c == 1), length - high * 256, 0)
     ).astype(jnp.float32)
     stage_ref[lat + 16 : lat + 32, few + 128 : few + 256] = note.astype(jnp.bfloat16)
-    load_shared.wait()
+    for copy in loads[:early]:
+        copy.wait()
     send_shared.start()
-    load_query.wait()
-    queries = query_vmem[...].astype(jnp.float32).reshape(own_tokens * heads, lat)
-    lanes = [slice(p, min(lat, p + 128)) for p in range(0, lat, 128)]
-    for p, lane in enumerate(lanes):
-        flat_ref[p, :, 0 : lane.stop - lane.start] = queries[:, lane]
-    for one in range(heads):
-        for p, lane in enumerate(lanes):
-            rows = flat_ref[p, pl.ds(one, own_tokens, stride=heads), :]
-            rows_ref[one * own_tokens : (one + 1) * own_tokens, lane] = rows[
-                :, 0 : lane.stop - lane.start
-            ].astype(jnp.bfloat16)
     load_new.wait()
     stage_ref[lat : lat + 16, few : few + KVR] = new_vmem[:, 0:KVR]
     stage_ref[lat + 16 : lat + 32, few : few + lat - KVR] = new_vmem[:, KVR:lat]
-    load_direct.wait()
+    for copy in loads[early:]:
+        copy.wait()
     send_direct.start()
     send_shared.wait()
     send_direct.wait()
@@ -103,6 +95,11 @@
     near_ref[0:lat, pl.ds(pl.multiple_of((1 - side) * few, 128), few)] = other_ref[...]
     near_ref[:, 2 * few :] = direct_ref[...]
     near_ref[lat:, 0 : 2 * few] = jnp.zeros((EXTRA, 2 * few), jnp.bfloat16)
+
+
+def run_bias(width, core, valid):
+    lane = lax.broadcasted_iota(jnp.int32, (1, width), 1)
+    return jnp.where(lane + (lane // 128 + core) * 128 < valid, 0.0, masked_value)
 
 
 def own_kernel(blocks, len_ref, *refs):
@@ -177,39 +174,39 @@
     ctx = lax.axis_index("ctx")
     z, pair = lax.rem(ctx, NZ), ctx // NZ
     length = partner_length(near_ref)
-    near_bias = key_bias(width, length - core * width)
-    far_bias = key_bias(width, length - (1 - core) * width)
-    first = 2 * SHARED
+    near_bias, far_bias = run_bias(width, core, length), run_bias(width, 1 - core, length)
+    start = 2 * SHARED
     partner_new = jnp.concatenate(
-        [near_ref[lat : lat + 16, first : first + KVR], near_ref[lat + 16 : lat + 32, first : first + lat - KVR]],
+        [near_ref[lat : lat + 16, start : start + KVR], near_ref[lat + 16 : lat + 32, start : start + lat - KVR]],
         axis=1,
     )
     new_keys = jnp.concatenate([new_ref[...], partner_new], axis=0)
-    lane = lax.broadcasted_iota(jnp.int32, (16, 32), 1)
-    line = lax.broadcasted_iota(jnp.int32, (16, 32), 0)
-    key_offsets = jnp.zeros((16, 32), jnp.int32)
+    lane = lax.broadcasted_iota(jnp.int32, (8, 32), 1)
+    key_offsets = jnp.zeros((8, 32), jnp.int32)
     for k in range(32):
         side = pair if k < 16 else 1 - pair
         key_offsets = jnp.where(lane == k, offset_ref[(side * NZ + z) * 16 + k % 16], key_offsets)
-    new_bias = []
-    for block in range(NZ):
-        first = (pair * NZ + lax.rem(z + OFFSETS[block], NZ)) * 16
-        token_offsets = jnp.zeros((16, 32), jnp.int32)
-        for t in range(16):
-            token_offsets = jnp.where(line == t, offset_ref[first + t], token_offsets)
-        new_bias.append(jnp.where(key_offsets <= token_offsets, 0.0, masked_value))
+    to_row = lax.broadcasted_iota(jnp.int32, (256, 256), 0)
+    from_row = lax.broadcasted_iota(jnp.int32, (256, 256), 1)
+    source = to_row // 128 * 128 + to_row % 16 * 8 + to_row % 128 // 16
+    reorder = jnp.where(from_row == source, 1.0, 0.0).astype(jnp.bfloat16)
     wide = lax.broadcasted_iota(jnp.int32, (128, 128), 1)
     levels = jnp.zeros((128, 128), jnp.float32)
     for tile in range(NZ // 2):
         both = pieces[2 * tile : 2 * tile + 2]
         rows = jnp.concatenate([queries[2 * tile][...], queries[2 * tile + 1][...]], axis=0)
         stat = jnp.concatenate([states[2 * g + 1][r : r + 128, :] for g, r in both], axis=0)
+        new_bias = []
+        for block in (2 * tile, 2 * tile + 1):
+            token = (pair * NZ + lax.rem(z + OFFSETS[block], NZ)) * 16
+            new_bias += [
+                jnp.where(key_offsets <= offset_ref[token + t], 0.0, masked_value) for t in range(16)
+            ]
         acc, high, total = fold(
             [
                 dot_nn(rows, near_ref[0:lat, :]) + near_bias,
                 dot_nn(rows, far_ref[0:lat, :]) + far_bias,
-                dot_nt(rows, new_keys)
-                + jnp.concatenate([new_bias[2 * tile]] * 8 + [new_bias[2 * tile + 1]] * 8, axis=0),
+                dot_nt(rows, new_keys) + jnp.concatenate(new_bias, axis=0),
             ],
             [
                 lambda w: dot_nt(w, near_ref[0:KVR, :]),
@@ -220,7 +217,8 @@
             stat[:, 0:1],
             stat[:, 1:2],
         )
-        latent_ref[tile * 256 : (tile + 1) * 256, :] = (acc * (1.0 / total)).astype(jnp.bfloat16)
+        latent = (acc * (1.0 / total)).astype(jnp.bfloat16)
+        latent_ref[tile * 256 : (tile + 1) * 256, :] = dot_nn(reorder, latent).astype(jnp.bfloat16)
         level = high * exp_scale + jnp.log2(total)
         levels = jnp.where(wide == 2 * tile, level[:128], levels)
         levels = jnp.where(wide == 2 * tile + 1, level[128:], levels)
@@ -254,7 +252,8 @@
     level = jnp.concatenate(levels, axis=0)
     factor = jnp.exp2(level - jnp.max(level, axis=0, keepdims=True))
     factor = factor / jnp.sum(factor, axis=0, keepdims=True)
-    factor = jnp.concatenate([factor, jnp.zeros((128 - NZ, 128), jnp.float32)], axis=0).T
+    order_ref[...] = jnp.concatenate([factor, jnp.zeros((128 - NZ, 128), jnp.float32)], axis=0).T
+    factor = jnp.concatenate([order_ref[pl.ds(head, 16, stride=8), :] for head in range(8)], axis=0)
     total = jnp.zeros((128, VDIM), jnp.float32)
     for source in range(NZ):
         total = total + part_ref[source, 0:128, :].astype(jnp.float32) * factor[:, source : source + 1]
@@ -283,23 +282,23 @@
             a, "ctx", [(c, c // NZ * NZ + (c + step) % NZ) for c in range(16)]
         )
 
+    own = queries.reshape(rows, lat)
+    up1, down1 = shift(own, 1), shift(own, -1)
+
     width = cache.shape[0] // 2
     hbm = pl.BlockSpec(memory_space=pltpu.HBM)
-    shared, direct, own = pl.pallas_call(
+    shared, direct = pl.pallas_call(
         pack_kernel,
-        in_specs=[SMEM, hbm, hbm, hbm],
-        out_specs=[hbm, hbm, VMEM],
+        in_specs=[SMEM, hbm, hbm],
+        out_specs=[hbm, hbm],
         out_shape=[
             jax.ShapeDtypeStruct((lat, SHARED), jnp.bfloat16),
             jax.ShapeDtypeStruct((lat + EXTRA, width - 2 * SHARED), jnp.bfloat16),
-            jax.ShapeDtypeStruct((rows, lat), jnp.bfloat16),
         ],
         scratch_shapes=[
             pltpu.VMEM((lat + EXTRA, width - SHARED), jnp.bfloat16),
             pltpu.VMEM((own_tokens, lat), jnp.bfloat16),
-            pltpu.VMEM((own_tokens, head_local, lat), jnp.bfloat16),
-            pltpu.VMEM((-(-lat // 128), rows, 128), jnp.float32),
-            pltpu.SemaphoreType.DMA((6,)),
+            pltpu.SemaphoreType.DMA(((width - SHARED) // 128 + 3,)),
         ],
         compiler_params=pltpu.CompilerParams(vmem_limit_bytes=4 * 2**20),
         name="pack",
@@ -307,17 +306,12 @@
         cache_lengths,
         pltpu.with_memory_space_constraint(keys, pltpu.HBM),
         pltpu.with_memory_space_constraint(new_latents, pltpu.HBM),
-        pltpu.with_memory_space_constraint(queries, pltpu.HBM),
-    )
-    mine = across(shared)
-
-    state0 = attend_own(cache_lengths, [own], keys)
-    up1, down1 = shift(own, 1), shift(own, -1)
-    state0, direct = lax.optimization_barrier((state0, direct))
-    direct = across(direct)
-    up1, down1, state0 = lax.optimization_barrier((up1, down1, state0))
+    )
+    mine, direct = across(shared), across(direct)
+
+    up1, down1 = lax.optimization_barrier((up1, down1))
     up2, down2 = shift(up1, 1), shift(down1, -1)
-    state1 = attend_own(cache_lengths, [up1, down1], keys)
+    state1 = attend_own(cache_lengths, [own, up1, down1], keys)
     state1, mine = lax.optimization_barrier((state1, mine))
     other = lax.ppermute(mine, "head", [(h, h ^ 2) for h in range(16)])
     up2, down2, state1 = lax.optimization_barrier((up2, down2, state1))
@@ -339,14 +333,14 @@
         compiler_params=pltpu.CompilerParams(vmem_limit_bytes=6 * 2**20),
         cost_estimate=small_cost,
         name="join",
-    )(mine, other, direct)
+    )(mine, other, pltpu.with_memory_space_constraint(direct, pltpu.VMEM))
     far = swap(near)
     state3 = attend_own(cache_lengths, [up3, down3, four], keys)
     far, state3 = lax.optimization_barrier((far, state3))
-    states = [part for state in (state0, state1, state2, state3) for part in state]
+    states = [part for state in (state1, state2, state3) for part in state]
     parts = pl.pallas_call(
-        functools.partial(final_kernel, [1, 2, 2, 3]),
-        in_specs=[SMEM] + [VMEM] * (NZ + 12),
+        functools.partial(final_kernel, [3, 2, 3]),
+        in_specs=[SMEM] + [VMEM] * (NZ + 10),
         out_specs=VMEM,
         out_shape=jax.ShapeDtypeStruct((NZ, rows + STAT, VDIM), jnp.bfloat16),
         scratch_shapes=[pltpu.VMEM((NZ * rows, KVR), jnp.bfloat16)],

time: 66.4 us -> 65.6 us (0.988)
  starting transfers between devices: 20.5 us -> 18.3 us
  waiting for transfers between devices: 5.98 us -> 6.97 us
    ppermute x2, waiting for transfers between devices: 0.89 us -> 3.64 us  [across(): return lax.ppermute(a, ('ctx', 'head'), moves)]
    ppermute x6, waiting for transfers between devices: 4.46 us -> 1.93 us  [shift(): lax.ppermute(a, 'ctx', [(c, c // NZ * NZ + (c + step) % NZ) for c in rang...]
    ppermute x1, starting transfers between devices: 3.51 us -> 1.89 us  [swap(): return lax.ppermute(a, 'head', [(h, h ^ 1) for h in range(16)])]
    ppermute x6, starting transfers between devices: 13 us -> 12.2 us  [shift(): lax.ppermute(a, 'ctx', [(c, c // NZ * NZ + (c + step) % NZ) for c in rang...]
    ppermute x1, waiting for transfers between devices: 0.62 us -> 1.4 us  [shards(): lax.ppermute(jnp.where(z % 2 == 0, up2, down2), 'ctx', [(c, c // NZ * NZ...]
    pallas_call x4 -> x3, Pallas kernels: 8.22 us -> 7.57 us  [attend_own(): pl.pallas_call(functools.partial(own_kernel, len(blocks)), in_specs=[SMEM...]
  transfers between devices with their start and end apart: 11 -> 11, of which waited for: 6 -> 5; matrix products, arithmetic and copies ran while one was open for 0% -> 0% of each run, Pallas kernels for 12% -> 15%
where the time goes in v3:
time: 65.6 us; the launch traced here: 65.8 us
  Pallas kernels  22.3 us (34%)
  starting transfers between devices  18.3 us (28%)
  blocking collectives  16.4 us (25%)
  waiting for transfers between devices  6.97 us (11%)
  local copies, waits for them, and re-layouts  0.94 us (1%)
  between operations  0.82 us (1%)
    all_to_all x1, blocking collectives, shards(): lax.all_to_all(parts, 'ctx', 0, 0, axis_index_groups=[[*range(NZ)], [*ran...  16.4 us
    ppermute x6, starting transfers between devices, shift(): lax.ppermute(a, 'ctx', [(c, c // NZ * NZ + (c + step) % NZ) for c in rang...  12.2 us
    pallas_call x1, Pallas kernels, shards(): pl.pallas_call(functools.partial(final_kernel, [3, 2, 3]), in_specs=[SMEM...  10.3 us
    pallas_call x3, Pallas kernels, attend_own(): pl.pallas_call(functools.partial(own_kernel, len(blocks)), in_specs=[SMEM...  7.57 us
    ppermute x2, waiting for transfers between devices, across(): return lax.ppermute(a, ('ctx', 'head'), moves)  3.64 us
    ppermute x2, starting transfers between devices, across(): return lax.ppermute(a, ('ctx', 'head'), moves)  2.92 us
    pallas_call x1, Pallas kernels, shards(): pl.pallas_call(pack_kernel, in_specs=[SMEM, hbm, hbm], out_specs=[hbm, hb...  2.21 us
    ppermute x6, waiting for transfers between devices, shift(): lax.ppermute(a, 'ctx', [(c, c // NZ * NZ + (c + step) % NZ) for c in rang...  1.93 us
  transfers between devices with their start and end apart: 11, of which 5 were waited for; matrix products, arithmetic and copies ran while one was open for 0% of the time, Pallas kernels for 15%

profile of v3, /device:TPU:1, one launch (start us, length us, event | category | flops | bytes accessed | tf_op | source)
XLA Modules:
  0.0 65.8 jit_solution(3081744562098396226)
XLA Ops:
  0.0 6.4 %collective-permute-start.1 = (bf16[128,576]{1,0:T(8,128)(2,1)}, bf16[128,576]{1,0:T(8,128)(2,1)S(1)}, u32[]{:S(2)}, u32[]{:S(2)}) collective-permute-start(bf16[128,576]{1,0:T(8,128)(2,1)} %bitcast.7), channel_id=1, source_target_pairs={{0,112},{16,0},{32,16},{48,32},{64,48},{80,64},{96,80},{112,96},{1... | collective-permute-start | bytes 442376 | tf_op jit(solution)/shard_map/ppermute | solution.py:281
  7.1 2.2 %pack.1 = (bf16[576,256]{1,0:T(8,128)(2,1)}, bf16[608,512]{1,0:T(8,128)(2,1)}) custom-call(s32[1]{0:T(128)S(6)} %copy.7.len_ref, bf16[576,2048]{1,0:T(8,128)(2,1)} %bitcast.3, bf16[16,576]{1,0:T(8,128)(2,1)} %refs_16_.1), custom_call_target="tpu_custom_call" | custom-call | tf_op jit(solution)/shard_map/pack/pallas_call | solution.py:290
  9.3 2.8 %collective-permute-start.4 = (bf16[576,256]{1,0:T(8,128)(2,1)}, bf16[576,256]{1,0:T(8,128)(2,1)S(1)}, u32[]{:S(2)}, u32[]{:S(2)}) collective-permute-start(bf16[576,256]{1,0:T(8,128)(2,1)} %get-tuple-element.36), channel_id=1, source_target_pairs={{0,136},{1,137},{2,138},{3,139},{4,140},{5,141},{6,142},{7,143},{8... | collective-permute-start | bytes 884744 | tf_op jit(solution)/shard_map/ppermute | solution.py:275
  12.1 0.1 collective-permute-start.9
  12.2 0.4 collective-permute-done.refs_1_
  12.6 2.7 %collective-permute-start.3 = (bf16[128,576]{1,0:T(8,128)(2,1)S(1)}, bf16[128,576]{1,0:T(8,128)(2,1)S(1)}, u32[]{:S(2)}, u32[]{:S(2)}) collective-permute-start(bf16[128,576]{1,0:T(8,128)(2,1)S(1)} %collective-permute-done.1.refs_2_), channel_id=1, source_target_pairs={{0,112},{16,0},{32,16},{48,32},{64,48},{80,64},{96,80},{112,96},{1... | collective-permute-start | bytes 442376 | tf_op jit(solution)/shard_map/ppermute | solution.py:281
  15.3 0.9 %copy-done.2 = bf16[16,8,576]{2,1,0:T(8,128)(2,1)S(1)} copy-done((bf16[16,8,576]{2,1,0:T(8,128)(2,1)S(1)}, bf16[16,8,576]{2,1,0:T(8,128)(2,1)}, u32[]{:S(2)}) %copy-start.2) | copy-done | bytes 147480
  16.2 2.7 %attend_own.3 = (f32[384,512]{1,0:T(8,128)S(1)}, f32[384,128]{1,0:T(8,128)S(1)}) custom-call(s32[1]{0:T(128)S(6)} %copy.7.len_ref, bf16[128,576]{1,0:T(8,128)(2,1)S(1)} %bitcast.9, bf16[128,576]{1,0:T(8,128)(2,1)S(1)} %collective-permute-done.refs_1_, bf16[128,576]{1,0:T(8,128)(2,1)S(1)} %collective-permute-done.1.refs_2_, bf16[576,2048]{1,0:T(8,128)(2,1)S(1)} %bitcast.4), custom_call_target="tpu_custom_call" | custom-call | flops 1000000 | bytes 10000 | tf_op jit(solution)/shard_map/attend_own/pallas_call | solution.py:129
  18.9 1.3 %collective-permute-start.8 = (bf16[576,256]{1,0:T(8,128)(2,1)S(1)}, bf16[576,256]{1,0:T(8,128)(2,1)S(1)}, u32[]{:S(2)}, u32[]{:S(2)}) collective-permute-start(bf16[576,256]{1,0:T(8,128)(2,1)S(1)} %collective-permute-done.4.mine_ref), channel_id=1, source_target_pairs={{0,2},{1,3},{2,0},{3,1},{4,6},{5,7},{6,4},{7,5},{8,10},{9,11},{10,... | collective-permute-start | bytes 884744 | tf_op jit(solution)/shard_map/ppermute | solution.py:316
  20.3 0.1 collective-permute-start.7
  20.4 3.1 %collective-permute-start.5 = (bf16[128,576]{1,0:T(8,128)(2,1)S(1)}, bf16[128,576]{1,0:T(8,128)(2,1)S(1)}, u32[]{:S(2)}, u32[]{:S(2)}) collective-permute-start(bf16[128,576]{1,0:T(8,128)(2,1)S(1)} %collective-permute-done.2.refs_0_.refs_3_), channel_id=1, source_target_pairs={{0,16},{16,32},{32,48},{48,64},{64,80},{80,96},{96,112},{112,0},{1... | collective-permute-start | bytes 442376 | tf_op jit(solution)/shard_map/ppermute | solution.py:281
  23.4 1.9 %attend_own.4 = (f32[256,512]{1,0:T(8,128)S(1)}, f32[256,128]{1,0:T(8,128)S(1)}) custom-call(s32[1]{0:T(128)S(6)} %copy.7.len_ref, bf16[128,576]{1,0:T(8,128)(2,1)S(1)} %collective-permute-done.2.refs_0_.refs_3_, bf16[128,576]{1,0:T(8,128)(2,1)S(1)} %collective-permute-done.3.refs_1_.refs_4_, bf16[576,2048]{1,0:T(8,128)(2,1)S(1)} %bitcast.5), custom_call_target="tpu_custom_call" | custom-call | flops 1000000 | bytes 10000 | tf_op jit(solution)/shard_map/attend_own/pallas_call | solution.py:129
  25.3 1.4 %collective-permute-done.7.refs_2_.refs_7_ = bf16[128,576]{1,0:T(8,128)(2,1)S(1)} collective-permute-done((bf16[128,576]{1,0:T(8,128)(2,1)S(1)}, bf16[128,576]{1,0:T(8,128)(2,1)S(1)}, u32[]{:S(2)}, u32[]{:S(2)}) %collective-permute-start.7) | collective-permute-done | bytes 147488 | tf_op jit(solution)/shard_map/ppermute | solution.py:319
  26.7 1.2 %collective-permute-done.5.refs_0_.refs_5_ = bf16[128,576]{1,0:T(8,128)(2,1)S(1)} collective-permute-done((bf16[128,576]{1,0:T(8,128)(2,1)S(1)}, bf16[128,576]{1,0:T(8,128)(2,1)S(1)}, u32[]{:S(2)}, u32[]{:S(2)}) %collective-permute-start.5) | collective-permute-done | bytes 147488 | tf_op jit(solution)/shard_map/ppermute | solution.py:281
  28.0 0.3 collective-permute-done.6.refs_1_.refs_6_
  28.3 3.6 %collective-permute-done.9.direct_ref = bf16[608,512]{1,0:T(8,128)(2,1)} collective-permute-done((bf16[608,512]{1,0:T(8,128)(2,1)}, bf16[608,512]{1,0:T(8,128)(2,1)}, u32[]{:S(2)}, u32[]{:S(2)}) %collective-permute-start.9) | collective-permute-done | bytes 622624 | tf_op jit(solution)/shard_map/ppermute | solution.py:275
  31.9 1.2 %join.1.refs_14_ = bf16[608,1024]{1,0:T(8,128)(2,1)S(1)} custom-call(bf16[576,256]{1,0:T(8,128)(2,1)S(1)} %collective-permute-done.4.mine_ref, bf16[576,256]{1,0:T(8,128)(2,1)S(1)} %collective-permute-done.8.other_ref, bf16[608,512]{1,0:T(8,128)(2,1)} %collective-permute-done.9.direct_ref), custom_call_target="tpu_custom_call" | custom-call | flops 1000000 | bytes 10000 | tf_op jit(solution)/shard_map/join/pallas_call | solution.py:328
  33.1 0.0 copy-start.1
  33.2 0.0 copy-start.5
  33.2 1.9 %collective-permute-start.10 = (bf16[608,1024]{1,0:T(8,128)(2,1)S(1)}, bf16[608,1024]{1,0:T(8,128)(2,1)S(1)}, u32[]{:S(2)}, u32[]{:S(2)}) collective-permute-start(bf16[608,1024]{1,0:T(8,128)(2,1)S(1)} %join.1.refs_14_), channel_id=1, source_target_pairs={{0,1},{1,0},{2,3},{3,2},{4,5},{5,4},{6,7},{7,6},{8,9},{9,8},{10,11... | collective-permute-start | bytes 3735560 | tf_op jit(solution)/shard_map/ppermute | solution.py:278
  35.1 2.9 %attend_own.5 = (f32[384,512]{1,0:T(8,128)S(1)}, f32[384,128]{1,0:T(8,128)S(1)}) custom-call(s32[1]{0:T(128)S(6)} %copy.7.len_ref, bf16[128,576]{1,0:T(8,128)(2,1)S(1)} %collective-permute-done.5.refs_0_.refs_5_, bf16[128,576]{1,0:T(8,128)(2,1)S(1)} %collective-permute-done.6.refs_1_.refs_6_, bf16[128,576]{1,0:T(8,128)(2,1)S(1)} %collective-permute-done.7.refs_2_.refs_7_, ...), custom_call_target="tpu_custom_call" | custom-call | flops 1000000 | bytes 10000 | tf_op jit(solution)/shard_map/attend_own/pallas_call | solution.py:129
  38.1 10.3 %attend_final.1 = bf16[8,144,128]{2,1,0:T(8,128)(2,1)S(1)} custom-call(s32[256]{0:T(256)S(1)} %copy-done.5, bf16[128,576]{1,0:T(8,128)(2,1)S(1)} %bitcast.10, bf16[128,576]{1,0:T(8,128)(2,1)S(1)} %collective-permute-done.refs_1_, bf16[128,576]{1,0:T(8,128)(2,1)S(1)} %collective-permute-done.1.refs_2_, ...), custom_call_target="tpu_custom_call" | custom-call | flops 1000000 | bytes 10000 | tf_op jit(solution)/shard_map/attend_final/pallas_call | solution.py:341
  48.4 16.4 %all_to_all.5.part_ref = bf16[8,144,128]{2,1,0:T(8,128)(2,1)S(1)} all-to-all(bf16[8,144,128]{2,1,0:T(8,128)(2,1)S(1)} %attend_final.1), channel_id=1, replica_groups={{0,16,32,48,64,80,96,112},{128,144,160,176,192,208,224,240},{1,17,33,49..., dimensions={0} | all-to-all | bytes 589824 | tf_op jit(solution)/shard_map/all_to_all | solution.py:351
  64.8 1.0 %merge.1 = bf16[128,128]{1,0:T(8,128)(2,1)} custom-call(bf16[8,144,128]{2,1,0:T(8,128)(2,1)S(1)} %all_to_all.5.part_ref), custom_call_target="tpu_custom_call" | custom-call | tf_op jit(solution)/shard_map/merge/pallas_call | solution.py:354
  (19 shorter events, 0.1 us)
Async XLA Ops:
  0.0 15.3 %copy-start = (bf16[2048,576]{0,1:T(8,128)(2,1)S(1)}, bf16[2048,576]{0,1:T(8,128)(2,1)}, u32[]{:S(2)}) copy-start(bf16[2048,576]{0,1:T(8,128)(2,1)} %param.7) | copy-start | bytes 7077892
  0.0 12.2 %collective-permute-start.1 = (bf16[128,576]{1,0:T(8,128)(2,1)}, bf16[128,576]{1,0:T(8,128)(2,1)S(1)}, u32[]{:S(2)}, u32[]{:S(2)}) collective-permute-start(bf16[128,576]{1,0:T(8,128)(2,1)} %bitcast.7), channel_id=1, source_target_pairs={{0,112},{16,0},{32,16},{48,32},{64,48},{80,64},{96,80},{112,96},{1... | collective-permute-start | bytes 442376 | tf_op jit(solution)/shard_map/ppermute | solution.py:281
  6.4 6.2 %collective-permute-start = (bf16[128,576]{1,0:T(8,128)(2,1)}, bf16[128,576]{1,0:T(8,128)(2,1)S(1)}, u32[]{:S(2)}, u32[]{:S(2)}) collective-permute-start(bf16[128,576]{1,0:T(8,128)(2,1)} %bitcast.8), channel_id=1, source_target_pairs={{0,16},{16,32},{32,48},{48,64},{64,80},{80,96},{96,112},{112,0},{1... | collective-permute-start | bytes 442376 | tf_op jit(solution)/shard_map/ppermute | solution.py:281
  9.3 9.6 %collective-permute-start.4 = (bf16[576,256]{1,0:T(8,128)(2,1)}, bf16[576,256]{1,0:T(8,128)(2,1)S(1)}, u32[]{:S(2)}, u32[]{:S(2)}) collective-permute-start(bf16[576,256]{1,0:T(8,128)(2,1)} %get-tuple-element.36), channel_id=1, source_target_pairs={{0,136},{1,137},{2,138},{3,139},{4,140},{5,141},{6,142},{7,143},{8... | collective-permute-start | bytes 884744 | tf_op jit(solution)/shard_map/ppermute | solution.py:275
  12.1 19.8 %collective-permute-start.9 = (bf16[608,512]{1,0:T(8,128)(2,1)}, bf16[608,512]{1,0:T(8,128)(2,1)}, u32[]{:S(2)}, u32[]{:S(2)}) collective-permute-start(bf16[608,512]{1,0:T(8,128)(2,1)} %get-tuple-element.44), channel_id=1, source_target_pairs={{0,136},{1,137},{2,138},{3,139},{4,140},{5,141},{6,142},{7,143},{8... | collective-permute-start | bytes 1867784 | tf_op jit(solution)/shard_map/ppermute | solution.py:275
  12.6 6.3 %collective-permute-start.2 = (bf16[128,576]{1,0:T(8,128)(2,1)S(1)}, bf16[128,576]{1,0:T(8,128)(2,1)S(1)}, u32[]{:S(2)}, u32[]{:S(2)}) collective-permute-start(bf16[128,576]{1,0:T(8,128)(2,1)S(1)} %collective-permute-done.refs_1_), channel_id=1, source_target_pairs={{0,16},{16,32},{32,48},{48,64},{64,80},{80,96},{96,112},{112,0},{1... | collective-permute-start | bytes 442376 | tf_op jit(solution)/shard_map/ppermute | solution.py:281
  12.6 6.4 %collective-permute-start.3 = (bf16[128,576]{1,0:T(8,128)(2,1)S(1)}, bf16[128,576]{1,0:T(8,128)(2,1)S(1)}, u32[]{:S(2)}, u32[]{:S(2)}) collective-permute-start(bf16[128,576]{1,0:T(8,128)(2,1)S(1)} %collective-permute-done.1.refs_2_), channel_id=1, source_target_pairs={{0,112},{16,0},{32,16},{48,32},{64,48},{80,64},{96,80},{112,96},{1... | collective-permute-start | bytes 442376 | tf_op jit(solution)/shard_map/ppermute | solution.py:281
  15.3 0.9 %copy-start.2 = (bf16[16,8,576]{2,1,0:T(8,128)(2,1)S(1)}, bf16[16,8,576]{2,1,0:T(8,128)(2,1)}, u32[]{:S(2)}) copy-start(bf16[16,8,576]{2,1,0:T(8,128)(2,1)} %param.6) | copy-start | bytes 442372
  18.9 9.3 %collective-permute-start.8 = (bf16[576,256]{1,0:T(8,128)(2,1)S(1)}, bf16[576,256]{1,0:T(8,128)(2,1)S(1)}, u32[]{:S(2)}, u32[]{:S(2)}) collective-permute-start(bf16[576,256]{1,0:T(8,128)(2,1)S(1)} %collective-permute-done.4.mine_ref), channel_id=1, source_target_pairs={{0,2},{1,3},{2,0},{3,1},{4,6},{5,7},{6,4},{7,5},{8,10},{9,11},{10,... | collective-permute-start | bytes 884744 | tf_op jit(solution)/shard_map/ppermute | solution.py:316
  20.3 6.5 %collective-permute-start.7 = (bf16[128,576]{1,0:T(8,128)(2,1)S(1)}, bf16[128,576]{1,0:T(8,128)(2,1)S(1)}, u32[]{:S(2)}, u32[]{:S(2)}) collective-permute-start(bf16[128,576]{1,0:T(8,128)(2,1)S(1)} %broadcast_select_fusion), channel_id=1, source_target_pairs={{0,32},{16,112},{32,64},{48,16},{64,96},{80,48},{96,0},{112,80},{1... | collective-permute-start | bytes 442376 | tf_op jit(solution)/shard_map/ppermute | solution.py:319
  20.4 7.6 %collective-permute-start.5 = (bf16[128,576]{1,0:T(8,128)(2,1)S(1)}, bf16[128,576]{1,0:T(8,128)(2,1)S(1)}, u32[]{:S(2)}, u32[]{:S(2)}) collective-permute-start(bf16[128,576]{1,0:T(8,128)(2,1)S(1)} %collective-permute-done.2.refs_0_.refs_3_), channel_id=1, source_target_pairs={{0,16},{16,32},{32,48},{48,64},{64,80},{80,96},{96,112},{112,0},{1... | collective-permute-start | bytes 442376 | tf_op jit(solution)/shard_map/ppermute | solution.py:281
  23.4 4.9 %collective-permute-start.6 = (bf16[128,576]{1,0:T(8,128)(2,1)S(1)}, bf16[128,576]{1,0:T(8,128)(2,1)S(1)}, u32[]{:S(2)}, u32[]{:S(2)}) collective-permute-start(bf16[128,576]{1,0:T(8,128)(2,1)S(1)} %collective-permute-done.3.refs_1_.refs_4_), channel_id=1, source_target_pairs={{0,112},{16,0},{32,16},{48,32},{64,48},{80,64},{96,80},{112,96},{1... | collective-permute-start | bytes 442376 | tf_op jit(solution)/shard_map/ppermute | solution.py:281
  33.1 4.9 %copy-start.1 = (bf16[8,512,128]{2,1,0:T(8,128)(2,1)S(1)}, bf16[8,512,128]{2,1,0:T(8,128)(2,1)}, u32[]{:S(2)}) copy-start(bf16[8,512,128]{2,1,0:T(8,128)(2,1)} %refs_17_.1) | copy-start | bytes 3145732
  33.2 4.9 %copy-start.3 = (bf16[16,8,576]{2,1,0:T(8,128)(2,1)S(1)}, bf16[16,8,576]{2,1,0:T(8,128)(2,1)}, u32[]{:S(2)}) copy-start(bf16[16,8,576]{2,1,0:T(8,128)(2,1)} %param.6) | copy-start | bytes 442372
  33.2 4.9 %copy-start.4 = (bf16[16,576]{1,0:T(8,128)(2,1)S(1)}, bf16[16,576]{1,0:T(8,128)(2,1)}, u32[]{:S(2)}) copy-start(bf16[16,576]{1,0:T(8,128)(2,1)} %refs_16_.1) | copy-start | bytes 55300
  33.2 4.9 %copy-start.5 = (s32[256]{0:T(256)S(1)}, s32[256]{0:T(256)}, u32[]{:S(2)}) copy-start(s32[256]{0:T(256)} %offset_ref.1) | copy-start | bytes 3076
  33.2 4.8 %collective-permute-start.10 = (bf16[608,1024]{1,0:T(8,128)(2,1)S(1)}, bf16[608,1024]{1,0:T(8,128)(2,1)S(1)}, u32[]{:S(2)}, u32[]{:S(2)}) collective-permute-start(bf16[608,1024]{1,0:T(8,128)(2,1)S(1)} %join.1.refs_14_), channel_id=1, source_target_pairs={{0,1},{1,0},{2,3},{3,2},{4,5},{5,4},{6,7},{7,6},{8,9},{9,8},{10,11... | collective-permute-start | bytes 3735560 | tf_op jit(solution)/shard_map/ppermute | solution.py:278

commit v4 on v3

--- a/solution.py
+++ b/solution.py
@@ -88,18 +88,10 @@
     send_direct.wait()
 
 
-def join_kernel(mine_ref, other_ref, direct_ref, near_ref):
-    side = lax.rem(lax.axis_index("head") // 2, 2)
-    lat, few = mine_ref.shape
-    near_ref[0:lat, pl.ds(pl.multiple_of(side * few, 128), few)] = mine_ref[...]
-    near_ref[0:lat, pl.ds(pl.multiple_of((1 - side) * few, 128), few)] = other_ref[...]
-    near_ref[:, 2 * few :] = direct_ref[...]
-    near_ref[lat:, 0 : 2 * few] = jnp.zeros((EXTRA, 2 * few), jnp.bfloat16)
-
-
-def run_bias(width, core, valid):
+def run_bias(width, first, core, valid):
     lane = lax.broadcasted_iota(jnp.int32, (1, width), 1)
-    return jnp.where(lane + (lane // 128 + core) * 128 < valid, 0.0, masked_value)
+    position = lane + lane // 128 * 128 + 2 * first + core * 128
+    return jnp.where(position < valid, 0.0, masked_value)
 
 
 def own_kernel(blocks, len_ref, *refs):
@@ -142,7 +134,7 @@
 
 def partner_length(part_ref):
     lat = part_ref.shape[0] - EXTRA
-    row = part_ref[lat + 16 : lat + 32, 2 * SHARED + 128 : 2 * SHARED + 256].astype(jnp.float32)
+    row = part_ref[lat + 16 : lat + 32, 128:256].astype(jnp.float32)
     r = lax.broadcasted_iota(jnp.int32, row.shape, 0)
     c = lax.broadcasted_iota(jnp.int32, row.shape, 1)
     high = jnp.sum(jnp.where((r == 0) & (c == 0), row, 0.0))
@@ -167,18 +159,27 @@
 def final_kernel(counts, offset_ref, *refs):
     queries, refs = refs[:NZ], refs[NZ:]
     states, refs = refs[: 2 * len(counts)], refs[2 * len(counts) :]
-    near_ref, far_ref, new_ref, up_ref, out_ref, latent_ref = refs
+    parts, (new_ref, up_ref, out_ref, latent_ref) = refs[:6], refs[6:]
     pieces = [(g, 128 * i) for g, count in enumerate(counts) for i in range(count)]
-    lat, width = near_ref.shape[0] - EXTRA, near_ref.shape[1]
-    core = lax.rem(lax.axis_index("head"), 2)
+    mine_ref, direct_ref = parts[0], parts[2]
+    lat = mine_ref.shape[0]
+    head = lax.axis_index("head")
+    core, side = lax.rem(head, 2), lax.rem(head // 2, 2)
     ctx = lax.axis_index("ctx")
     z, pair = lax.rem(ctx, NZ), ctx // NZ
-    length = partner_length(near_ref)
-    near_bias, far_bias = run_bias(width, core, length), run_bias(width, 1 - core, length)
-    start = 2 * SHARED
+    length = partner_length(direct_ref)
+    firsts = [side * SHARED, (1 - side) * SHARED, 2 * SHARED]
+    biases = [
+        run_bias(parts[3 * i + j].shape[1], firsts[j], core if i == 0 else 1 - core, length)
+        for i in range(2)
+        for j in range(3)
+    ]
+
+    def values_of(ref):
+        return lambda w: dot_nt(w, ref[0:KVR, :])
+
     partner_new = jnp.concatenate(
-        [near_ref[lat : lat + 16, start : start + KVR], near_ref[lat + 16 : lat + 32, start : start + lat - KVR]],
-        axis=1,
+        [direct_ref[lat : lat + 16, 0:KVR], direct_ref[lat + 16 : lat + 32, 0 : lat - KVR]], axis=1
     )
     new_keys = jnp.concatenate([new_ref[...], partner_new], axis=0)
     lane = lax.broadcasted_iota(jnp.int32, (8, 32), 1)
@@ -203,16 +204,9 @@
                 jnp.where(key_offsets <= offset_ref[token + t], 0.0, masked_value) for t in range(16)
             ]
         acc, high, total = fold(
-            [
-                dot_nn(rows, near_ref[0:lat, :]) + near_bias,
-                dot_nn(rows, far_ref[0:lat, :]) + far_bias,
-                dot_nt(rows, new_keys) + jnp.concatenate(new_bias, axis=0),
-            ],
-            [
-                lambda w: dot_nt(w, near_ref[0:KVR, :]),
-                lambda w: dot_nt(w, far_ref[0:KVR, :]),
-                lambda w: dot_nn(w, new_keys[:, 0:KVR]),
-            ],
+            [dot_nn(rows, ref[0:lat, :]) + bias for ref, bias in zip(parts, biases)]
+            + [dot_nt(rows, new_keys) + jnp.concatenate(new_bias, axis=0)],
+            [values_of(ref) for ref in parts] + [lambda w: dot_nn(w, new_keys[:, 0:KVR])],
             jnp.concatenate([states[2 * g][r : r + 128, :] for g, r in both], axis=0),
             stat[:, 0:1],
             stat[:, 1:2],
@@ -322,32 +316,23 @@
         [(c, c // NZ * NZ + (c + (2 if c % 2 == 0 else -2)) % NZ) for c in range(16)],
     )
     state2 = attend_own(cache_lengths, [up2, down2], keys)
-    up3, down3, four, state2, other, direct = lax.optimization_barrier(
-        (up3, down3, four, state2, other, direct)
-    )
-    near = pl.pallas_call(
-        join_kernel,
-        in_specs=[VMEM] * 3,
-        out_specs=VMEM,
-        out_shape=jax.ShapeDtypeStruct((lat + EXTRA, width), jnp.bfloat16),
-        compiler_params=pltpu.CompilerParams(vmem_limit_bytes=6 * 2**20),
-        cost_estimate=small_cost,
-        name="join",
-    )(mine, other, pltpu.with_memory_space_constraint(direct, pltpu.VMEM))
-    far = swap(near)
+    up3, down3, four, state2, mine, other, direct = lax.optimization_barrier(
+        (up3, down3, four, state2, mine, other, direct)
+    )
+    far_mine, far_other, far_direct = swap(mine), swap(other), swap(direct)
     state3 = attend_own(cache_lengths, [up3, down3, four], keys)
-    far, state3 = lax.optimization_barrier((far, state3))
+    far_mine, far_other, far_direct, state3 = lax.optimization_barrier((far_mine, far_other, far_direct, state3))
     states = [part for state in (state1, state2, state3) for part in state]
     parts = pl.pallas_call(
         functools.partial(final_kernel, [3, 2, 3]),
-        in_specs=[SMEM] + [VMEM] * (NZ + 10),
+        in_specs=[SMEM] + [VMEM] * (NZ + 14),
         out_specs=VMEM,
         out_shape=jax.ShapeDtypeStruct((NZ, rows + STAT, VDIM), jnp.bfloat16),
         scratch_shapes=[pltpu.VMEM((NZ * rows, KVR), jnp.bfloat16)],
         compiler_params=pltpu.CompilerParams(vmem_limit_bytes=16 * 2**20),
         cost_estimate=small_cost,
         name="attend_final",
-    )(new_offsets, own, up1, down1, up2, down2, up3, down3, four, *states, near, far, new_latents, value_up_weight)
+    )(new_offsets, own, up1, down1, up2, down2, up3, down3, four, *states, mine, other, direct, far_mine, far_other, far_direct, new_latents, value_up_weight)
     got = lax.all_to_all(
         parts, "ctx", 0, 0, axis_index_groups=[[*range(NZ)], [*range(NZ, 2 * NZ)]], tiled=True
     )

time: 65.6 us -> 64.8 us (0.988); the launches traced: 65.8 us -> 63.9 us
  Pallas kernels: 22.3 us -> 19.5 us
  starting transfers between devices: 18.3 us -> 19.2 us
    pallas_call x3, Pallas kernels: 7.57 us -> 5.86 us  [attend_own(): pl.pallas_call(functools.partial(own_kernel, len(blocks)), in_specs=[SMEM...]
    pallas_call x1 -> x0, Pallas kernels: 1.22 us -> none  [shards(): pl.pallas_call(join_kernel, in_specs=[VMEM] * 3, out_specs=VMEM, out_shap...]
    ppermute x1 -> x3, starting transfers between devices: 1.89 us -> 2.31 us  [swap(): return lax.ppermute(a, 'head', [(h, h ^ 1) for h in range(16)])]
  transfers between devices with their start and end apart: 11 -> 13, of which waited for: 5 -> 6; matrix products, arithmetic and copies ran while one was open for 0% -> 0% of each run, Pallas kernels for 15% -> 13%
where the time goes in v4:
time: 64.8 us; the launch traced here: 63.9 us
  Pallas kernels  19.5 us (30%)
  starting transfers between devices  19.2 us (30%)
  blocking collectives  15.9 us (25%)
  waiting for transfers between devices  7.57 us (12%)
  local copies, waits for them, and re-layouts  0.94 us (1%)
  between operations  0.8 us (1%)
    all_to_all x1, blocking collectives, shards(): lax.all_to_all(parts, 'ctx', 0, 0, axis_index_groups=[[*range(NZ)], [*ran...  15.9 us
    ppermute x6, starting transfers between devices, shift(): lax.ppermute(a, 'ctx', [(c, c // NZ * NZ + (c + step) % NZ) for c in rang...  12.5 us
    pallas_call x1, Pallas kernels, shards(): pl.pallas_call(functools.partial(final_kernel, [3, 2, 3]), in_specs=[SMEM...  10.4 us
    pallas_call x3, Pallas kernels, attend_own(): pl.pallas_call(functools.partial(own_kernel, len(blocks)), in_specs=[SMEM...  5.86 us
    ppermute x2, waiting for transfers between devices, across(): return lax.ppermute(a, ('ctx', 'head'), moves)  3.81 us
    ppermute x2, starting transfers between devices, across(): return lax.ppermute(a, ('ctx', 'head'), moves)  2.92 us
    ppermute x6, waiting for transfers between devices, shift(): lax.ppermute(a, 'ctx', [(c, c // NZ * NZ + (c + step) % NZ) for c in rang...  2.47 us
    ppermute x3, starting transfers between devices, swap(): return lax.ppermute(a, 'head', [(h, h ^ 1) for h in range(16)])  2.31 us
  transfers between devices with their start and end apart: 13, of which 6 were waited for; matrix products, arithmetic and copies ran while one was open for 0% of the time, Pallas kernels for 13%

profile of v4, /device:TPU:1, one launch (start us, length us, event | category | flops | bytes accessed | tf_op | source)
XLA Modules:
  0.0 63.9 jit_solution(14555783088014748552)
XLA Ops:
  0.0 6.4 %collective-permute-start.1 = (bf16[128,576]{1,0:T(8,128)(2,1)}, bf16[128,576]{1,0:T(8,128)(2,1)S(1)}, u32[]{:S(2)}, u32[]{:S(2)}) collective-permute-start(bf16[128,576]{1,0:T(8,128)(2,1)} %bitcast.7), channel_id=1, source_target_pairs={{0,112},{16,0},{32,16},{48,32},{64,48},{80,64},{96,80},{112,96},{1... | collective-permute-start | bytes 442376 | tf_op jit(solution)/shard_map/ppermute | solution.py:275
  7.1 2.2 %pack.1 = (bf16[576,256]{1,0:T(8,128)(2,1)}, bf16[608,512]{1,0:T(8,128)(2,1)}) custom-call(s32[1]{0:T(128)S(6)} %copy.7.len_ref, bf16[576,2048]{1,0:T(8,128)(2,1)} %bitcast.3, bf16[16,576]{1,0:T(8,128)(2,1)} %refs_20_.1), custom_call_target="tpu_custom_call" | custom-call | tf_op jit(solution)/shard_map/pack/pallas_call | solution.py:284
  9.3 2.8 %collective-permute-start.4 = (bf16[576,256]{1,0:T(8,128)(2,1)}, bf16[576,256]{1,0:T(8,128)(2,1)S(1)}, u32[]{:S(2)}, u32[]{:S(2)}) collective-permute-start(bf16[576,256]{1,0:T(8,128)(2,1)} %get-tuple-element.39), channel_id=1, source_target_pairs={{0,136},{1,137},{2,138},{3,139},{4,140},{5,141},{6,142},{7,143},{8... | collective-permute-start | bytes 884744 | tf_op jit(solution)/shard_map/ppermute | solution.py:269
  12.1 0.1 collective-permute-start.9
  12.2 0.4 collective-permute-done.refs_1_
  12.6 2.7 %collective-permute-start.3 = (bf16[128,576]{1,0:T(8,128)(2,1)S(1)}, bf16[128,576]{1,0:T(8,128)(2,1)S(1)}, u32[]{:S(2)}, u32[]{:S(2)}) collective-permute-start(bf16[128,576]{1,0:T(8,128)(2,1)S(1)} %collective-permute-done.1.refs_2_), channel_id=1, source_target_pairs={{0,112},{16,0},{32,16},{48,32},{64,48},{80,64},{96,80},{112,96},{1... | collective-permute-start | bytes 442376 | tf_op jit(solution)/shard_map/ppermute | solution.py:275
  15.3 0.9 %copy-done.2 = bf16[16,8,576]{2,1,0:T(8,128)(2,1)S(1)} copy-done((bf16[16,8,576]{2,1,0:T(8,128)(2,1)S(1)}, bf16[16,8,576]{2,1,0:T(8,128)(2,1)}, u32[]{:S(2)}) %copy-start.2) | copy-done | bytes 147480
  16.2 2.1 %attend_own.3 = (f32[384,512]{1,0:T(8,128)S(1)}, f32[384,128]{1,0:T(8,128)S(1)}) custom-call(s32[1]{0:T(128)S(6)} %copy.7.len_ref, bf16[128,576]{1,0:T(8,128)(2,1)S(1)} %bitcast.9, bf16[128,576]{1,0:T(8,128)(2,1)S(1)} %collective-permute-done.refs_1_, bf16[128,576]{1,0:T(8,128)(2,1)S(1)} %collective-permute-done.1.refs_2_, bf16[576,2048]{1,0:T(8,128)(2,1)S(1)} %bitcast.4), custom_call_target="tpu_custom_call" | custom-call | flops 1000000 | bytes 10000 | tf_op jit(solution)/shard_map/attend_own/pallas_call | solution.py:121
  18.3 0.2 collective-permute-done.4.refs_14_
  18.5 1.2 %collective-permute-start.8 = (bf16[576,256]{1,0:T(8,128)(2,1)S(1)}, bf16[576,256]{1,0:T(8,128)(2,1)S(1)}, u32[]{:S(2)}, u32[]{:S(2)}) collective-permute-start(bf16[576,256]{1,0:T(8,128)(2,1)S(1)} %collective-permute-done.4.refs_14_), channel_id=1, source_target_pairs={{0,2},{1,3},{2,0},{3,1},{4,6},{5,7},{6,4},{7,5},{8,10},{9,11},{10,... | collective-permute-start | bytes 884744 | tf_op jit(solution)/shard_map/ppermute | solution.py:310
  19.8 0.0 copy-start.4
  19.8 0.2 collective-permute-start.7
  20.0 3.5 %collective-permute-start.5 = (bf16[128,576]{1,0:T(8,128)(2,1)S(1)}, bf16[128,576]{1,0:T(8,128)(2,1)S(1)}, u32[]{:S(2)}, u32[]{:S(2)}) collective-permute-start(bf16[128,576]{1,0:T(8,128)(2,1)S(1)} %collective-permute-done.2.refs_0_.refs_3_), channel_id=1, source_target_pairs={{0,16},{16,32},{32,48},{48,64},{64,80},{80,96},{96,112},{112,0},{1... | collective-permute-start | bytes 442376 | tf_op jit(solution)/shard_map/ppermute | solution.py:275
  23.5 1.5 %attend_own.4 = (f32[256,512]{1,0:T(8,128)S(1)}, f32[256,128]{1,0:T(8,128)S(1)}) custom-call(s32[1]{0:T(128)S(6)} %copy.7.len_ref, bf16[128,576]{1,0:T(8,128)(2,1)S(1)} %collective-permute-done.2.refs_0_.refs_3_, bf16[128,576]{1,0:T(8,128)(2,1)S(1)} %collective-permute-done.3.refs_1_.refs_4_, bf16[576,2048]{1,0:T(8,128)(2,1)S(1)} %bitcast.5), custom_call_target="tpu_custom_call" | custom-call | flops 1000000 | bytes 10000 | tf_op jit(solution)/shard_map/attend_own/pallas_call | solution.py:121
  25.0 1.3 %collective-permute-done.7.refs_2_.refs_7_ = bf16[128,576]{1,0:T(8,128)(2,1)S(1)} collective-permute-done((bf16[128,576]{1,0:T(8,128)(2,1)S(1)}, bf16[128,576]{1,0:T(8,128)(2,1)S(1)}, u32[]{:S(2)}, u32[]{:S(2)}) %collective-permute-start.7) | collective-permute-done | bytes 147488 | tf_op jit(solution)/shard_map/ppermute | solution.py:313
  26.2 1.3 %collective-permute-done.5.refs_0_.refs_5_ = bf16[128,576]{1,0:T(8,128)(2,1)S(1)} collective-permute-done((bf16[128,576]{1,0:T(8,128)(2,1)S(1)}, bf16[128,576]{1,0:T(8,128)(2,1)S(1)}, u32[]{:S(2)}, u32[]{:S(2)}) %collective-permute-start.5) | collective-permute-done | bytes 147488 | tf_op jit(solution)/shard_map/ppermute | solution.py:275
  27.6 0.8 %collective-permute-done.6.refs_1_.refs_6_ = bf16[128,576]{1,0:T(8,128)(2,1)S(1)} collective-permute-done((bf16[128,576]{1,0:T(8,128)(2,1)S(1)}, bf16[128,576]{1,0:T(8,128)(2,1)S(1)}, u32[]{:S(2)}, u32[]{:S(2)}) %collective-permute-start.6) | collective-permute-done | bytes 147488 | tf_op jit(solution)/shard_map/ppermute | solution.py:275
  28.3 3.6 %collective-permute-done.9.refs_16_ = bf16[608,512]{1,0:T(8,128)(2,1)} collective-permute-done((bf16[608,512]{1,0:T(8,128)(2,1)}, bf16[608,512]{1,0:T(8,128)(2,1)}, u32[]{:S(2)}, u32[]{:S(2)}) %collective-permute-start.9) | collective-permute-done | bytes 622624 | tf_op jit(solution)/shard_map/ppermute | solution.py:269
  31.9 1.8 %collective-permute-start.12 = (bf16[608,512]{1,0:T(8,128)(2,1)}, bf16[608,512]{1,0:T(8,128)(2,1)S(1)}, u32[]{:S(2)}, u32[]{:S(2)}) collective-permute-start(bf16[608,512]{1,0:T(8,128)(2,1)} %collective-permute-done.9.refs_16_), channel_id=1, source_target_pairs={{0,1},{1,0},{2,3},{3,2},{4,5},{5,4},{6,7},{7,6},{8,9},{9,8},{10,11... | collective-permute-start | bytes 1867784 | tf_op jit(solution)/shard_map/ppermute | solution.py:272
  33.7 0.5 collective-permute-start.11
  34.2 2.3 %attend_own.5 = (f32[384,512]{1,0:T(8,128)S(1)}, f32[384,128]{1,0:T(8,128)S(1)}) custom-call(s32[1]{0:T(128)S(6)} %copy.7.len_ref, bf16[128,576]{1,0:T(8,128)(2,1)S(1)} %collective-permute-done.5.refs_0_.refs_5_, bf16[128,576]{1,0:T(8,128)(2,1)S(1)} %collective-permute-done.6.refs_1_.refs_6_, bf16[128,576]{1,0:T(8,128)(2,1)S(1)} %collective-permute-done.7.refs_2_.refs_7_, ...), custom_call_target="tpu_custom_call" | custom-call | flops 1000000 | bytes 10000 | tf_op jit(solution)/shard_map/attend_own/pallas_call | solution.py:121
  36.6 10.4 %attend_final.1 = bf16[8,144,128]{2,1,0:T(8,128)(2,1)S(1)} custom-call(s32[256]{0:T(256)S(1)} %copy-done.5, bf16[128,576]{1,0:T(8,128)(2,1)S(1)} %bitcast.10, bf16[128,576]{1,0:T(8,128)(2,1)S(1)} %collective-permute-done.refs_1_, bf16[128,576]{1,0:T(8,128)(2,1)S(1)} %collective-permute-done.1.refs_2_, ...), custom_call_target="tpu_custom_call" | custom-call | flops 1000000 | bytes 10000 | tf_op jit(solution)/shard_map/attend_final/pallas_call | solution.py:326
  47.0 15.9 %all_to_all.5.part_ref = bf16[8,144,128]{2,1,0:T(8,128)(2,1)S(1)} all-to-all(bf16[8,144,128]{2,1,0:T(8,128)(2,1)S(1)} %attend_final.1), channel_id=1, replica_groups={{0,16,32,48,64,80,96,112},{128,144,160,176,192,208,224,240},{1,17,33,49..., dimensions={0} | all-to-all | bytes 589824 | tf_op jit(solution)/shard_map/all_to_all | solution.py:336
  62.9 1.0 %merge.1 = bf16[128,128]{1,0:T(8,128)(2,1)} custom-call(bf16[8,144,128]{2,1,0:T(8,128)(2,1)S(1)} %all_to_all.5.part_ref), custom_call_target="tpu_custom_call" | custom-call | tf_op jit(solution)/shard_map/merge/pallas_call | solution.py:339
  (22 shorter events, 0.1 us)
Async XLA Ops:
  0.0 15.3 %copy-start = (bf16[2048,576]{0,1:T(8,128)(2,1)S(1)}, bf16[2048,576]{0,1:T(8,128)(2,1)}, u32[]{:S(2)}) copy-start(bf16[2048,576]{0,1:T(8,128)(2,1)} %param.7) | copy-start | bytes 7077892
  0.0 12.2 %collective-permute-start.1 = (bf16[128,576]{1,0:T(8,128)(2,1)}, bf16[128,576]{1,0:T(8,128)(2,1)S(1)}, u32[]{:S(2)}, u32[]{:S(2)}) collective-permute-start(bf16[128,576]{1,0:T(8,128)(2,1)} %bitcast.7), channel_id=1, source_target_pairs={{0,112},{16,0},{32,16},{48,32},{64,48},{80,64},{96,80},{112,96},{1... | collective-permute-start | bytes 442376 | tf_op jit(solution)/shard_map/ppermute | solution.py:275
  6.4 6.2 %collective-permute-start = (bf16[128,576]{1,0:T(8,128)(2,1)}, bf16[128,576]{1,0:T(8,128)(2,1)S(1)}, u32[]{:S(2)}, u32[]{:S(2)}) collective-permute-start(bf16[128,576]{1,0:T(8,128)(2,1)} %bitcast.8), channel_id=1, source_target_pairs={{0,16},{16,32},{32,48},{48,64},{64,80},{80,96},{96,112},{112,0},{1... | collective-permute-start | bytes 442376 | tf_op jit(solution)/shard_map/ppermute | solution.py:275
  9.3 9.2 %collective-permute-start.4 = (bf16[576,256]{1,0:T(8,128)(2,1)}, bf16[576,256]{1,0:T(8,128)(2,1)S(1)}, u32[]{:S(2)}, u32[]{:S(2)}) collective-permute-start(bf16[576,256]{1,0:T(8,128)(2,1)} %get-tuple-element.39), channel_id=1, source_target_pairs={{0,136},{1,137},{2,138},{3,139},{4,140},{5,141},{6,142},{7,143},{8... | collective-permute-start | bytes 884744 | tf_op jit(solution)/shard_map/ppermute | solution.py:269
  12.1 19.8 %collective-permute-start.9 = (bf16[608,512]{1,0:T(8,128)(2,1)}, bf16[608,512]{1,0:T(8,128)(2,1)}, u32[]{:S(2)}, u32[]{:S(2)}) collective-permute-start(bf16[608,512]{1,0:T(8,128)(2,1)} %get-tuple-element.47), channel_id=1, source_target_pairs={{0,136},{1,137},{2,138},{3,139},{4,140},{5,141},{6,142},{7,143},{8... | collective-permute-start | bytes 1867784 | tf_op jit(solution)/shard_map/ppermute | solution.py:269
  12.6 5.9 %collective-permute-start.2 = (bf16[128,576]{1,0:T(8,128)(2,1)S(1)}, bf16[128,576]{1,0:T(8,128)(2,1)S(1)}, u32[]{:S(2)}, u32[]{:S(2)}) collective-permute-start(bf16[128,576]{1,0:T(8,128)(2,1)S(1)} %collective-permute-done.refs_1_), channel_id=1, source_target_pairs={{0,16},{16,32},{32,48},{48,64},{64,80},{80,96},{96,112},{112,0},{1... | collective-permute-start | bytes 442376 | tf_op jit(solution)/shard_map/ppermute | solution.py:275
  12.6 5.9 %collective-permute-start.3 = (bf16[128,576]{1,0:T(8,128)(2,1)S(1)}, bf16[128,576]{1,0:T(8,128)(2,1)S(1)}, u32[]{:S(2)}, u32[]{:S(2)}) collective-permute-start(bf16[128,576]{1,0:T(8,128)(2,1)S(1)} %collective-permute-done.1.refs_2_), channel_id=1, source_target_pairs={{0,112},{16,0},{32,16},{48,32},{64,48},{80,64},{96,80},{112,96},{1... | collective-permute-start | bytes 442376 | tf_op jit(solution)/shard_map/ppermute | solution.py:275
  15.3 0.9 %copy-start.2 = (bf16[16,8,576]{2,1,0:T(8,128)(2,1)S(1)}, bf16[16,8,576]{2,1,0:T(8,128)(2,1)}, u32[]{:S(2)}) copy-start(bf16[16,8,576]{2,1,0:T(8,128)(2,1)} %param.6) | copy-start | bytes 442372
  18.5 9.8 %collective-permute-start.8 = (bf16[576,256]{1,0:T(8,128)(2,1)S(1)}, bf16[576,256]{1,0:T(8,128)(2,1)S(1)}, u32[]{:S(2)}, u32[]{:S(2)}) collective-permute-start(bf16[576,256]{1,0:T(8,128)(2,1)S(1)} %collective-permute-done.4.refs_14_), channel_id=1, source_target_pairs={{0,2},{1,3},{2,0},{3,1},{4,6},{5,7},{6,4},{7,5},{8,10},{9,11},{10,... | collective-permute-start | bytes 884744 | tf_op jit(solution)/shard_map/ppermute | solution.py:310
  19.7 16.9 %copy-start.1 = (bf16[8,512,128]{2,1,0:T(8,128)(2,1)S(1)}, bf16[8,512,128]{2,1,0:T(8,128)(2,1)}, u32[]{:S(2)}) copy-start(bf16[8,512,128]{2,1,0:T(8,128)(2,1)} %refs_21_.1) | copy-start | bytes 3145732
  19.7 16.9 %copy-start.3 = (bf16[16,8,576]{2,1,0:T(8,128)(2,1)S(1)}, bf16[16,8,576]{2,1,0:T(8,128)(2,1)}, u32[]{:S(2)}) copy-start(bf16[16,8,576]{2,1,0:T(8,128)(2,1)} %param.6) | copy-start | bytes 442372
  19.8 16.9 %copy-start.4 = (bf16[16,576]{1,0:T(8,128)(2,1)S(1)}, bf16[16,576]{1,0:T(8,128)(2,1)}, u32[]{:S(2)}) copy-start(bf16[16,576]{1,0:T(8,128)(2,1)} %refs_20_.1) | copy-start | bytes 55300
  19.8 16.8 %copy-start.5 = (s32[256]{0:T(256)S(1)}, s32[256]{0:T(256)}, u32[]{:S(2)}) copy-start(s32[256]{0:T(256)} %offset_ref.1) | copy-start | bytes 3076
  19.8 6.5 %collective-permute-start.7 = (bf16[128,576]{1,0:T(8,128)(2,1)S(1)}, bf16[128,576]{1,0:T(8,128)(2,1)S(1)}, u32[]{:S(2)}, u32[]{:S(2)}) collective-permute-start(bf16[128,576]{1,0:T(8,128)(2,1)S(1)} %broadcast_select_fusion), channel_id=1, source_target_pairs={{0,32},{16,112},{32,64},{48,16},{64,96},{80,48},{96,0},{112,80},{1... | collective-permute-start | bytes 442376 | tf_op jit(solution)/shard_map/ppermute | solution.py:313
  20.0 7.5 %collective-permute-start.5 = (bf16[128,576]{1,0:T(8,128)(2,1)S(1)}, bf16[128,576]{1,0:T(8,128)(2,1)S(1)}, u32[]{:S(2)}, u32[]{:S(2)}) collective-permute-start(bf16[128,576]{1,0:T(8,128)(2,1)S(1)} %collective-permute-done.2.refs_0_.refs_3_), channel_id=1, source_target_pairs={{0,16},{16,32},{32,48},{48,64},{64,80},{80,96},{96,112},{112,0},{1... | collective-permute-start | bytes 442376 | tf_op jit(solution)/shard_map/ppermute | solution.py:275
  23.5 4.9 %collective-permute-start.6 = (bf16[128,576]{1,0:T(8,128)(2,1)S(1)}, bf16[128,576]{1,0:T(8,128)(2,1)S(1)}, u32[]{:S(2)}, u32[]{:S(2)}) collective-permute-start(bf16[128,576]{1,0:T(8,128)(2,1)S(1)} %collective-permute-done.3.refs_1_.refs_4_), channel_id=1, source_target_pairs={{0,112},{16,0},{32,16},{48,32},{64,48},{80,64},{96,80},{112,96},{1... | collective-permute-start | bytes 442376 | tf_op jit(solution)/shard_map/ppermute | solution.py:275
  31.9 4.6 %collective-permute-start.12 = (bf16[608,512]{1,0:T(8,128)(2,1)}, bf16[608,512]{1,0:T(8,128)(2,1)S(1)}, u32[]{:S(2)}, u32[]{:S(2)}) collective-permute-start(bf16[608,512]{1,0:T(8,128)(2,1)} %collective-permute-done.9.refs_16_), channel_id=1, source_target_pairs={{0,1},{1,0},{2,3},{3,2},{4,5},{5,4},{6,7},{7,6},{8,9},{9,8},{10,11... | collective-permute-start | bytes 1867784 | tf_op jit(solution)/shard_map/ppermute | solution.py:272
  33.7 2.8 %collective-permute-start.10 = (bf16[576,256]{1,0:T(8,128)(2,1)S(1)}, bf16[576,256]{1,0:T(8,128)(2,1)S(1)}, u32[]{:S(2)}, u32[]{:S(2)}) collective-permute-start(bf16[576,256]{1,0:T(8,128)(2,1)S(1)} %collective-permute-done.4.refs_14_), channel_id=1, source_target_pairs={{0,1},{1,0},{2,3},{3,2},{4,5},{5,4},{6,7},{7,6},{8,9},{9,8},{10,11... | collective-permute-start | bytes 884744 | tf_op jit(solution)/shard_map/ppermute | solution.py:272
  33.7 2.8 %collective-permute-start.11 = (bf16[576,256]{1,0:T(8,128)(2,1)S(1)}, bf16[576,256]{1,0:T(8,128)(2,1)S(1)}, u32[]{:S(2)}, u32[]{:S(2)}) collective-permute-start(bf16[576,256]{1,0:T(8,128)(2,1)S(1)} %collective-permute-done.8.refs_15_), channel_id=1, source_target_pairs={{0,1},{1,0},{2,3},{3,2},{4,5},{5,4},{6,7},{7,6},{8,9},{9,8},{10,11... | collective-permute-start | bytes 884744 | tf_op jit(solution)/shard_map/ppermute | solution.py:272

commit v5 on v4

--- a/solution.py
+++ b/solution.py
@@ -95,14 +95,18 @@
 
 
 def own_kernel(blocks, len_ref, *refs):
-    query_refs, (keys_ref, acc_ref, stat_ref) = refs[:blocks], refs[blocks:]
+    query_refs, (keys_ref, acc_ref, stat_ref, rows_ref) = refs[:blocks], refs[blocks:]
+    to_row = lax.broadcasted_iota(jnp.int32, (128, 128), 0)
+    from_row = lax.broadcasted_iota(jnp.int32, (128, 128), 1)
+    reorder = jnp.where(from_row == to_row % 16 * 8 + to_row // 16, 1.0, 0.0).astype(jnp.bfloat16)
+    for i, ref in enumerate(query_refs):
+        rows_ref[i * 128 : (i + 1) * 128, :] = dot_nn(reorder, ref[...]).astype(jnp.bfloat16)
     valid = len_ref[0]
     full = keys_ref.shape[1]
     widths = [full // 2, full * 3 // 4, full]
 
     def attend(width):
-        rows = jnp.concatenate([r[...] for r in query_refs], axis=0)
-        scores = dot_nn(rows, keys_ref[:, 0:width]) + key_bias(width, valid)
+        scores = dot_nn(rows_ref[...], keys_ref[:, 0:width]) + key_bias(width, valid)
         high = jnp.max(scores, axis=1, keepdims=True)
         weights = jnp.exp2((scores - high) * exp_scale)
         total = jnp.sum(weights, axis=1, keepdims=True)
@@ -121,10 +125,11 @@
     return pl.pallas_call(
         functools.partial(own_kernel, len(blocks)),
         in_specs=[SMEM] + [VMEM] * (len(blocks) + 1),
-        out_specs=[VMEM, VMEM],
+        out_specs=[VMEM, VMEM, VMEM],
         out_shape=[
             jax.ShapeDtypeStruct((rows, KVR), jnp.float32),
             jax.ShapeDtypeStruct((rows, 128), jnp.float32),
+            jax.ShapeDtypeStruct((rows, keys.shape[0]), jnp.bfloat16),
         ],
         compiler_params=pltpu.CompilerParams(vmem_limit_bytes=12 * 2**20),
         cost_estimate=small_cost,
@@ -157,8 +162,7 @@
 
 
 def final_kernel(counts, offset_ref, *refs):
-    queries, refs = refs[:NZ], refs[NZ:]
-    states, refs = refs[: 2 * len(counts)], refs[2 * len(counts) :]
+    states, refs = refs[: 3 * len(counts)], refs[3 * len(counts) :]
     parts, (new_ref, up_ref, out_ref, latent_ref) = refs[:6], refs[6:]
     pieces = [(g, 128 * i) for g, count in enumerate(counts) for i in range(count)]
     mine_ref, direct_ref = parts[0], parts[2]
@@ -182,37 +186,35 @@
         [direct_ref[lat : lat + 16, 0:KVR], direct_ref[lat + 16 : lat + 32, 0 : lat - KVR]], axis=1
     )
     new_keys = jnp.concatenate([new_ref[...], partner_new], axis=0)
-    lane = lax.broadcasted_iota(jnp.int32, (8, 32), 1)
-    key_offsets = jnp.zeros((8, 32), jnp.int32)
+    lane = lax.broadcasted_iota(jnp.int32, (16, 32), 1)
+    line = lax.broadcasted_iota(jnp.int32, (16, 32), 0)
+    key_offsets = jnp.zeros((16, 32), jnp.int32)
     for k in range(32):
-        side = pair if k < 16 else 1 - pair
-        key_offsets = jnp.where(lane == k, offset_ref[(side * NZ + z) * 16 + k % 16], key_offsets)
-    to_row = lax.broadcasted_iota(jnp.int32, (256, 256), 0)
-    from_row = lax.broadcasted_iota(jnp.int32, (256, 256), 1)
-    source = to_row // 128 * 128 + to_row % 16 * 8 + to_row % 128 // 16
-    reorder = jnp.where(from_row == source, 1.0, 0.0).astype(jnp.bfloat16)
+        place = ((pair if k < 16 else 1 - pair) * NZ + z) * 16 + k % 16
+        key_offsets = jnp.where(lane == k, offset_ref[place], key_offsets)
+    new_bias = []
+    for block in range(NZ):
+        token = (pair * NZ + lax.rem(z + OFFSETS[block], NZ)) * 16
+        token_offsets = jnp.zeros((16, 32), jnp.int32)
+        for t in range(16):
+            token_offsets = jnp.where(line == t, offset_ref[token + t], token_offsets)
+        new_bias.append(jnp.where(key_offsets <= token_offsets, 0.0, masked_value))
     wide = lax.broadcasted_iota(jnp.int32, (128, 128), 1)
     levels = jnp.zeros((128, 128), jnp.float32)
     for tile in range(NZ // 2):
         both = pieces[2 * tile : 2 * tile + 2]
-        rows = jnp.concatenate([queries[2 * tile][...], queries[2 * tile + 1][...]], axis=0)
-        stat = jnp.concatenate([states[2 * g + 1][r : r + 128, :] for g, r in both], axis=0)
-        new_bias = []
-        for block in (2 * tile, 2 * tile + 1):
-            token = (pair * NZ + lax.rem(z + OFFSETS[block], NZ)) * 16
-            new_bias += [
-                jnp.where(key_offsets <= offset_ref[token + t], 0.0, masked_value) for t in range(16)
-            ]
+        rows = jnp.concatenate([states[3 * g + 2][r : r + 128, :] for g, r in both], axis=0)
+        stat = jnp.concatenate([states[3 * g + 1][r : r + 128, :] for g, r in both], axis=0)
+        bias = jnp.concatenate([new_bias[2 * tile]] * 8 + [new_bias[2 * tile + 1]] * 8, axis=0)
         acc, high, total = fold(
-            [dot_nn(rows, ref[0:lat, :]) + bias for ref, bias in zip(parts, biases)]
-            + [dot_nt(rows, new_keys) + jnp.concatenate(new_bias, axis=0)],
+            [dot_nn(rows, ref[0:lat, :]) + mask for ref, mask in zip(parts, biases)]
+            + [dot_nt(rows, new_keys) + bias],
             [values_of(ref) for ref in parts] + [lambda w: dot_nn(w, new_keys[:, 0:KVR])],
-            jnp.concatenate([states[2 * g][r : r + 128, :] for g, r in both], axis=0),
+            jnp.concatenate([states[3 * g][r : r + 128, :] for g, r in both], axis=0),
             stat[:, 0:1],
             stat[:, 1:2],
         )
-        latent = (acc * (1.0 / total)).astype(jnp.bfloat16)
-        latent_ref[tile * 256 : (tile + 1) * 256, :] = dot_nn(reorder, latent).astype(jnp.bfloat16)
+        latent_ref[tile * 256 : (tile + 1) * 256, :] = (acc * (1.0 / total)).astype(jnp.bfloat16)
         level = high * exp_scale + jnp.log2(total)
         levels = jnp.where(wide == 2 * tile, level[:128], levels)
         levels = jnp.where(wide == 2 * tile + 1, level[128:], levels)
@@ -246,8 +248,7 @@
     level = jnp.concatenate(levels, axis=0)
     factor = jnp.exp2(level - jnp.max(level, axis=0, keepdims=True))
     factor = factor / jnp.sum(factor, axis=0, keepdims=True)
-    order_ref[...] = jnp.concatenate([factor, jnp.zeros((128 - NZ, 128), jnp.float32)], axis=0).T
-    factor = jnp.concatenate([order_ref[pl.ds(head, 16, stride=8), :] for head in range(8)], axis=0)
+    factor = jnp.concatenate([factor, jnp.zeros((128 - NZ, 128), jnp.float32)], axis=0).T
     total = jnp.zeros((128, VDIM), jnp.float32)
     for source in range(NZ):
         total = total + part_ref[source, 0:128, :].astype(jnp.float32) * factor[:, source : source + 1]
@@ -306,7 +307,6 @@
     up1, down1 = lax.optimization_barrier((up1, down1))
     up2, down2 = shift(up1, 1), shift(down1, -1)
     state1 = attend_own(cache_lengths, [own, up1, down1], keys)
-    state1, mine = lax.optimization_barrier((state1, mine))
     other = lax.ppermute(mine, "head", [(h, h ^ 2) for h in range(16)])
     up2, down2, state1 = lax.optimization_barrier((up2, down2, state1))
     up3, down3 = shift(up2, 1), shift(down2, -1)
@@ -325,14 +325,14 @@
     states = [part for state in (state1, state2, state3) for part in state]
     parts = pl.pallas_call(
         functools.partial(final_kernel, [3, 2, 3]),
-        in_specs=[SMEM] + [VMEM] * (NZ + 14),
+        in_specs=[SMEM] + [VMEM] * 17,
         out_specs=VMEM,
         out_shape=jax.ShapeDtypeStruct((NZ, rows + STAT, VDIM), jnp.bfloat16),
         scratch_shapes=[pltpu.VMEM((NZ * rows, KVR), jnp.bfloat16)],
         compiler_params=pltpu.CompilerParams(vmem_limit_bytes=16 * 2**20),
         cost_estimate=small_cost,
         name="attend_final",
-    )(new_offsets, own, up1, down1, up2, down2, up3, down3, four, *states, mine, other, direct, far_mine, far_other, far_direct, new_latents, value_up_weight)
+    )(new_offsets, *states, mine, other, direct, far_mine, far_other, far_direct, new_latents, value_up_weight)
     got = lax.all_to_all(
         parts, "ctx", 0, 0, axis_index_groups=[[*range(NZ)], [*range(NZ, 2 * NZ)]], tiled=True
     )

time: 64.8 us -> 65.9 us (1.017); the launches traced: 63.9 us -> 66.1 us
  blocking collectives: 15.9 us -> 18.9 us
  waiting for transfers between devices: 7.57 us -> 6.48 us
    all_to_all x1, blocking collectives: 15.9 us -> 18.9 us  [shards(): lax.all_to_all(parts, 'ctx', 0, 0, axis_index_groups=[[*range(NZ)], [*ran...]
    ppermute x2, waiting for transfers between devices: 3.81 us -> 2.46 us  [across(): return lax.ppermute(a, ('ctx', 'head'), moves)]
    ppermute x1, starting transfers between devices: 0.24 us -> 1.53 us  [shards(): lax.ppermute(jnp.where(z % 2 == 0, up2, down2), 'ctx', [(c, c // NZ * NZ...]
    ppermute x6, starting transfers between devices: 12.5 us -> 11.8 us  [shift(): lax.ppermute(a, 'ctx', [(c, c // NZ * NZ + (c + step) % NZ) for c in rang...]
    ppermute x6, waiting for transfers between devices: 2.47 us -> 3.15 us  [shift(): lax.ppermute(a, 'ctx', [(c, c // NZ * NZ + (c + step) % NZ) for c in rang...]
where the time goes in v5:
time: 65.9 us; the launch traced here: 66.1 us
  starting transfers between devices  19.8 us (30%)
  Pallas kernels  19.2 us (29%)
  blocking collectives  18.9 us (29%)
  waiting for transfers between devices  6.48 us (10%)
  local copies, waits for them, and re-layouts  0.94 us (1%)
  between operations  0.78 us (1%)
    all_to_all x1, blocking collectives, shards(): lax.all_to_all(parts, 'ctx', 0, 0, axis_index_groups=[[*range(NZ)], [*ran...  18.9 us
    ppermute x6, starting transfers between devices, shift(): lax.ppermute(a, 'ctx', [(c, c // NZ * NZ + (c + step) % NZ) for c in rang...  11.8 us
    pallas_call x1, Pallas kernels, shards(): pl.pallas_call(functools.partial(final_kernel, [3, 2, 3]), in_specs=[SMEM...  9.85 us
    pallas_call x3, Pallas kernels, attend_own(): pl.pallas_call(functools.partial(own_kernel, len(blocks)), in_specs=[SMEM...  6.1 us
    ppermute x6, waiting for transfers between devices, shift(): lax.ppermute(a, 'ctx', [(c, c // NZ * NZ + (c + step) % NZ) for c in rang...  3.15 us
    ppermute x2, starting transfers between devices, across(): return lax.ppermute(a, ('ctx', 'head'), moves)  2.92 us
    ppermute x2, waiting for transfers between devices, across(): return lax.ppermute(a, ('ctx', 'head'), moves)  2.46 us
    ppermute x3, starting transfers between devices, swap(): return lax.ppermute(a, 'head', [(h, h ^ 1) for h in range(16)])  2.31 us
  transfers between devices with their start and end apart: 13, of which 6 were waited for; matrix products, arithmetic and copies ran while one was open for 0% of the time, Pallas kernels for 13%

profile of v5, /device:TPU:1, one launch (start us, length us, event | category | flops | bytes accessed | tf_op | source)
XLA Modules:
  0.0 66.1 jit_solution(18235566642235623330)
XLA Ops:
  0.0 2.5 %collective-permute-start = (bf16[128,576]{1,0:T(8,128)(2,1)}, bf16[128,576]{1,0:T(8,128)(2,1)S(1)}, u32[]{:S(2)}, u32[]{:S(2)}) collective-permute-start(bf16[128,576]{1,0:T(8,128)(2,1)} %bitcast.7), channel_id=1, source_target_pairs={{0,16},{16,32},{32,48},{48,64},{64,80},{80,96},{96,112},{112,0},{1... | collective-permute-start | bytes 442376 | tf_op jit(solution)/shard_map/ppermute | solution.py:276
  2.5 4.0 %collective-permute-start.1 = (bf16[128,576]{1,0:T(8,128)(2,1)}, bf16[128,576]{1,0:T(8,128)(2,1)}, u32[]{:S(2)}, u32[]{:S(2)}) collective-permute-start(bf16[128,576]{1,0:T(8,128)(2,1)} %bitcast.8), channel_id=1, source_target_pairs={{0,112},{16,0},{32,16},{48,32},{64,48},{80,64},{96,80},{112,96},{1... | collective-permute-start | bytes 442376 | tf_op jit(solution)/shard_map/ppermute | solution.py:276
  7.1 2.2 %pack.1 = (bf16[576,256]{1,0:T(8,128)(2,1)}, bf16[608,512]{1,0:T(8,128)(2,1)}) custom-call(s32[1]{0:T(128)S(6)} %copy.7.len_ref, bf16[576,2048]{1,0:T(8,128)(2,1)} %bitcast.3, bf16[16,576]{1,0:T(8,128)(2,1)} %refs_15_.1), custom_call_target="tpu_custom_call" | custom-call | tf_op jit(solution)/shard_map/pack/pallas_call | solution.py:285
  9.4 2.8 %collective-permute-start.7 = (bf16[576,256]{1,0:T(8,128)(2,1)}, bf16[576,256]{1,0:T(8,128)(2,1)}, u32[]{:S(2)}, u32[]{:S(2)}) collective-permute-start(bf16[576,256]{1,0:T(8,128)(2,1)} %get-tuple-element.51), channel_id=1, source_target_pairs={{0,136},{1,137},{2,138},{3,139},{4,140},{5,141},{6,142},{7,143},{8... | collective-permute-start | bytes 884744 | tf_op jit(solution)/shard_map/ppermute | solution.py:270
  12.2 0.1 collective-permute-start.9
  12.3 2.7 %collective-permute-start.3 = (bf16[128,576]{1,0:T(8,128)(2,1)}, bf16[128,576]{1,0:T(8,128)(2,1)S(1)}, u32[]{:S(2)}, u32[]{:S(2)}) collective-permute-start(bf16[128,576]{1,0:T(8,128)(2,1)} %collective-permute-done.1.refs_2_), channel_id=1, source_target_pairs={{0,112},{16,0},{32,16},{48,32},{64,48},{80,64},{96,80},{112,96},{1... | collective-permute-start | bytes 442376 | tf_op jit(solution)/shard_map/ppermute | solution.py:276
  15.0 0.9 %copy-done.2 = bf16[16,8,576]{2,1,0:T(8,128)(2,1)S(1)} copy-done((bf16[16,8,576]{2,1,0:T(8,128)(2,1)S(1)}, bf16[16,8,576]{2,1,0:T(8,128)(2,1)}, u32[]{:S(2)}) %copy-start.2) | copy-done | bytes 147480
  15.9 2.6 %attend_own.3 = (f32[384,512]{1,0:T(8,128)S(1)}, f32[384,128]{1,0:T(8,128)S(1)}, bf16[384,576]{1,0:T(8,128)(2,1)S(1)}) custom-call(s32[1]{0:T(128)S(6)} %copy.7.len_ref, bf16[128,576]{1,0:T(8,128)(2,1)S(1)} %bitcast.9, bf16[128,576]{1,0:T(8,128)(2,1)S(1)} %collective-permute-done.refs_1_, bf16[128,576]{1,0:T(8,128)(2,1)} %collective-permute-done.1.refs_2_, ...), custom_call_target="tpu_custom_call" | custom-call | flops 1000000 | bytes 10000 | tf_op jit(solution)/shard_map/attend_own/pallas_call | solution.py:125
  18.7 1.2 %collective-permute-start.8 = (bf16[576,256]{1,0:T(8,128)(2,1)}, bf16[576,256]{1,0:T(8,128)(2,1)S(1)}, u32[]{:S(2)}, u32[]{:S(2)}) collective-permute-start(bf16[576,256]{1,0:T(8,128)(2,1)} %collective-permute-done.7.refs_9_), channel_id=1, source_target_pairs={{0,2},{1,3},{2,0},{3,1},{4,6},{5,7},{6,4},{7,5},{8,10},{9,11},{10,... | collective-permute-start | bytes 884744 | tf_op jit(solution)/shard_map/ppermute | solution.py:310
  19.9 1.5 %collective-permute-start.6 = (bf16[128,576]{1,0:T(8,128)(2,1)S(1)}, bf16[128,576]{1,0:T(8,128)(2,1)S(1)}, u32[]{:S(2)}, u32[]{:S(2)}) collective-permute-start(bf16[128,576]{1,0:T(8,128)(2,1)S(1)} %broadcast_select_fusion), channel_id=1, source_target_pairs={{0,32},{16,112},{32,64},{48,16},{64,96},{80,48},{96,0},{112,80},{1... | collective-permute-start | bytes 442376 | tf_op jit(solution)/shard_map/ppermute | solution.py:313
  21.5 2.0 %collective-permute-start.4 = (bf16[128,576]{1,0:T(8,128)(2,1)S(1)}, bf16[128,576]{1,0:T(8,128)(2,1)S(1)}, u32[]{:S(2)}, u32[]{:S(2)}) collective-permute-start(bf16[128,576]{1,0:T(8,128)(2,1)S(1)} %collective-permute-done.2.refs_0_), channel_id=1, source_target_pairs={{0,16},{16,32},{32,48},{48,64},{64,80},{80,96},{96,112},{112,0},{1... | collective-permute-start | bytes 442376 | tf_op jit(solution)/shard_map/ppermute | solution.py:276
  23.5 0.6 collective-permute-start.5
  24.1 1.5 %attend_own.4 = (f32[256,512]{1,0:T(8,128)S(1)}, f32[256,128]{1,0:T(8,128)S(1)}, bf16[256,576]{1,0:T(8,128)(2,1)S(1)}) custom-call(s32[1]{0:T(128)S(6)} %copy.7.len_ref, bf16[128,576]{1,0:T(8,128)(2,1)S(1)} %collective-permute-done.2.refs_0_, bf16[128,576]{1,0:T(8,128)(2,1)S(1)} %collective-permute-done.3.refs_1_, bf16[576,2048]{1,0:T(8,128)(2,1)S(1)} %bitcast.5), custom_call_target="tpu_custom_call" | custom-call | flops 1000000 | bytes 10000 | tf_op jit(solution)/shard_map/attend_own/pallas_call | solution.py:125
  25.7 0.7 %collective-permute-done.6.refs_2_ = bf16[128,576]{1,0:T(8,128)(2,1)S(1)} collective-permute-done((bf16[128,576]{1,0:T(8,128)(2,1)S(1)}, bf16[128,576]{1,0:T(8,128)(2,1)S(1)}, u32[]{:S(2)}, u32[]{:S(2)}) %collective-permute-start.6) | collective-permute-done | bytes 147488 | tf_op jit(solution)/shard_map/ppermute | solution.py:313
  26.4 1.9 %collective-permute-done.4.refs_0_ = bf16[128,576]{1,0:T(8,128)(2,1)S(1)} collective-permute-done((bf16[128,576]{1,0:T(8,128)(2,1)S(1)}, bf16[128,576]{1,0:T(8,128)(2,1)S(1)}, u32[]{:S(2)}, u32[]{:S(2)}) %collective-permute-start.4) | collective-permute-done | bytes 147488 | tf_op jit(solution)/shard_map/ppermute | solution.py:276
  28.3 1.2 %collective-permute-done.5.refs_1_ = bf16[128,576]{1,0:T(8,128)(2,1)S(1)} collective-permute-done((bf16[128,576]{1,0:T(8,128)(2,1)S(1)}, bf16[128,576]{1,0:T(8,128)(2,1)S(1)}, u32[]{:S(2)}, u32[]{:S(2)}) %collective-permute-start.5) | collective-permute-done | bytes 147488 | tf_op jit(solution)/shard_map/ppermute | solution.py:276
  29.5 2.4 %collective-permute-done.9.refs_11_ = bf16[608,512]{1,0:T(8,128)(2,1)S(1)} collective-permute-done((bf16[608,512]{1,0:T(8,128)(2,1)}, bf16[608,512]{1,0:T(8,128)(2,1)S(1)}, u32[]{:S(2)}, u32[]{:S(2)}) %collective-permute-start.9) | collective-permute-done | bytes 622624 | tf_op jit(solution)/shard_map/ppermute | solution.py:270
  31.9 1.8 %collective-permute-start.12 = (bf16[608,512]{1,0:T(8,128)(2,1)S(1)}, bf16[608,512]{1,0:T(8,128)(2,1)S(1)}, u32[]{:S(2)}, u32[]{:S(2)}) collective-permute-start(bf16[608,512]{1,0:T(8,128)(2,1)S(1)} %collective-permute-done.9.refs_11_), channel_id=1, source_target_pairs={{0,1},{1,0},{2,3},{3,2},{4,5},{5,4},{6,7},{7,6},{8,9},{9,8},{10,11... | collective-permute-start | bytes 1867784 | tf_op jit(solution)/shard_map/ppermute | solution.py:273
  33.7 0.5 collective-permute-start.11
  34.2 1.9 %attend_own.5 = (f32[384,512]{1,0:T(8,128)S(1)}, f32[384,128]{1,0:T(8,128)S(1)}, bf16[384,576]{1,0:T(8,128)(2,1)S(1)}) custom-call(s32[1]{0:T(128)S(6)} %copy.7.len_ref, bf16[128,576]{1,0:T(8,128)(2,1)S(1)} %collective-permute-done.4.refs_0_, bf16[128,576]{1,0:T(8,128)(2,1)S(1)} %collective-permute-done.5.refs_1_, ...), custom_call_target="tpu_custom_call" | custom-call | flops 1000000 | bytes 10000 | tf_op jit(solution)/shard_map/attend_own/pallas_call | solution.py:125
  36.2 0.1 collective-permute-done.10.refs_12_
  36.3 9.8 %attend_final.1 = bf16[8,144,128]{2,1,0:T(8,128)(2,1)S(1)} custom-call(s32[256]{0:T(256)S(1)} %copy-done.4, f32[384,512]{1,0:T(8,128)S(1)} %get-tuple-element.43.refs_0_, f32[384,128]{1,0:T(8,128)S(1)} %get-tuple-element.44.refs_1_, bf16[384,576]{1,0:T(8,128)(2,1)S(1)} %get-tuple-element.45.refs_2_, f32[256,512]{1,0:T(8,128)S(1)} %get-tuple-element.53.refs_3_, ...), custom_call_target="tpu_custom_call" | custom-call | flops 1000000 | bytes 10000 | tf_op jit(solution)/shard_map/attend_final/pallas_call | solution.py:326
  46.2 18.9 %all_to_all.5.part_ref = bf16[8,144,128]{2,1,0:T(8,128)(2,1)S(1)} all-to-all(bf16[8,144,128]{2,1,0:T(8,128)(2,1)S(1)} %attend_final.1), channel_id=1, replica_groups={{0,16,32,48,64,80,96,112},{128,144,160,176,192,208,224,240},{1,17,33,49..., dimensions={0} | all-to-all | bytes 589824 | tf_op jit(solution)/shard_map/all_to_all | solution.py:336
  65.1 1.0 %merge.1 = bf16[128,128]{1,0:T(8,128)(2,1)} custom-call(bf16[8,144,128]{2,1,0:T(8,128)(2,1)S(1)} %all_to_all.5.part_ref), custom_call_target="tpu_custom_call" | custom-call | tf_op jit(solution)/shard_map/merge/pallas_call | solution.py:339
  (20 shorter events, 0.2 us)
Async XLA Ops:
  0.0 15.0 %copy-start = (bf16[2048,576]{0,1:T(8,128)(2,1)S(1)}, bf16[2048,576]{0,1:T(8,128)(2,1)}, u32[]{:S(2)}) copy-start(bf16[2048,576]{0,1:T(8,128)(2,1)} %param.7) | copy-start | bytes 7077892
  0.0 12.3 %collective-permute-start = (bf16[128,576]{1,0:T(8,128)(2,1)}, bf16[128,576]{1,0:T(8,128)(2,1)S(1)}, u32[]{:S(2)}, u32[]{:S(2)}) collective-permute-start(bf16[128,576]{1,0:T(8,128)(2,1)} %bitcast.7), channel_id=1, source_target_pairs={{0,16},{16,32},{32,48},{48,64},{64,80},{80,96},{96,112},{112,0},{1... | collective-permute-start | bytes 442376 | tf_op jit(solution)/shard_map/ppermute | solution.py:276
  2.5 9.8 %collective-permute-start.1 = (bf16[128,576]{1,0:T(8,128)(2,1)}, bf16[128,576]{1,0:T(8,128)(2,1)}, u32[]{:S(2)}, u32[]{:S(2)}) collective-permute-start(bf16[128,576]{1,0:T(8,128)(2,1)} %bitcast.8), channel_id=1, source_target_pairs={{0,112},{16,0},{32,16},{48,32},{64,48},{80,64},{96,80},{112,96},{1... | collective-permute-start | bytes 442376 | tf_op jit(solution)/shard_map/ppermute | solution.py:276
  9.4 9.3 %collective-permute-start.7 = (bf16[576,256]{1,0:T(8,128)(2,1)}, bf16[576,256]{1,0:T(8,128)(2,1)}, u32[]{:S(2)}, u32[]{:S(2)}) collective-permute-start(bf16[576,256]{1,0:T(8,128)(2,1)} %get-tuple-element.51), channel_id=1, source_target_pairs={{0,136},{1,137},{2,138},{3,139},{4,140},{5,141},{6,142},{7,143},{8... | collective-permute-start | bytes 884744 | tf_op jit(solution)/shard_map/ppermute | solution.py:270
  12.2 19.7 %collective-permute-start.9 = (bf16[608,512]{1,0:T(8,128)(2,1)}, bf16[608,512]{1,0:T(8,128)(2,1)S(1)}, u32[]{:S(2)}, u32[]{:S(2)}) collective-permute-start(bf16[608,512]{1,0:T(8,128)(2,1)} %get-tuple-element.52), channel_id=1, source_target_pairs={{0,136},{1,137},{2,138},{3,139},{4,140},{5,141},{6,142},{7,143},{8... | collective-permute-start | bytes 1867784 | tf_op jit(solution)/shard_map/ppermute | solution.py:270
  12.3 6.3 %collective-permute-start.2 = (bf16[128,576]{1,0:T(8,128)(2,1)S(1)}, bf16[128,576]{1,0:T(8,128)(2,1)S(1)}, u32[]{:S(2)}, u32[]{:S(2)}) collective-permute-start(bf16[128,576]{1,0:T(8,128)(2,1)S(1)} %collective-permute-done.refs_1_), channel_id=1, source_target_pairs={{0,16},{16,32},{32,48},{48,64},{64,80},{80,96},{96,112},{112,0},{1... | collective-permute-start | bytes 442376 | tf_op jit(solution)/shard_map/ppermute | solution.py:276
  12.3 6.2 %collective-permute-start.3 = (bf16[128,576]{1,0:T(8,128)(2,1)}, bf16[128,576]{1,0:T(8,128)(2,1)S(1)}, u32[]{:S(2)}, u32[]{:S(2)}) collective-permute-start(bf16[128,576]{1,0:T(8,128)(2,1)} %collective-permute-done.1.refs_2_), channel_id=1, source_target_pairs={{0,112},{16,0},{32,16},{48,32},{64,48},{80,64},{96,80},{112,96},{1... | collective-permute-start | bytes 442376 | tf_op jit(solution)/shard_map/ppermute | solution.py:276
  15.0 0.9 %copy-start.2 = (bf16[16,8,576]{2,1,0:T(8,128)(2,1)S(1)}, bf16[16,8,576]{2,1,0:T(8,128)(2,1)}, u32[]{:S(2)}) copy-start(bf16[16,8,576]{2,1,0:T(8,128)(2,1)} %param.6) | copy-start | bytes 442372
  18.7 10.9 %collective-permute-start.8 = (bf16[576,256]{1,0:T(8,128)(2,1)}, bf16[576,256]{1,0:T(8,128)(2,1)S(1)}, u32[]{:S(2)}, u32[]{:S(2)}) collective-permute-start(bf16[576,256]{1,0:T(8,128)(2,1)} %collective-permute-done.7.refs_9_), channel_id=1, source_target_pairs={{0,2},{1,3},{2,0},{3,1},{4,6},{5,7},{6,4},{7,5},{8,10},{9,11},{10,... | collective-permute-start | bytes 884744 | tf_op jit(solution)/shard_map/ppermute | solution.py:310
  19.9 16.4 %copy-start.1 = (bf16[8,512,128]{2,1,0:T(8,128)(2,1)S(1)}, bf16[8,512,128]{2,1,0:T(8,128)(2,1)}, u32[]{:S(2)}) copy-start(bf16[8,512,128]{2,1,0:T(8,128)(2,1)} %refs_16_.1) | copy-start | bytes 3145732
  19.9 16.4 %copy-start.3 = (bf16[16,576]{1,0:T(8,128)(2,1)S(1)}, bf16[16,576]{1,0:T(8,128)(2,1)}, u32[]{:S(2)}) copy-start(bf16[16,576]{1,0:T(8,128)(2,1)} %refs_15_.1) | copy-start | bytes 55300
  19.9 16.4 %copy-start.4 = (s32[256]{0:T(256)S(1)}, s32[256]{0:T(256)}, u32[]{:S(2)}) copy-start(s32[256]{0:T(256)} %offset_ref.1) | copy-start | bytes 3076
  19.9 6.5 %collective-permute-start.6 = (bf16[128,576]{1,0:T(8,128)(2,1)S(1)}, bf16[128,576]{1,0:T(8,128)(2,1)S(1)}, u32[]{:S(2)}, u32[]{:S(2)}) collective-permute-start(bf16[128,576]{1,0:T(8,128)(2,1)S(1)} %broadcast_select_fusion), channel_id=1, source_target_pairs={{0,32},{16,112},{32,64},{48,16},{64,96},{80,48},{96,0},{112,80},{1... | collective-permute-start | bytes 442376 | tf_op jit(solution)/shard_map/ppermute | solution.py:313
  21.5 6.9 %collective-permute-start.4 = (bf16[128,576]{1,0:T(8,128)(2,1)S(1)}, bf16[128,576]{1,0:T(8,128)(2,1)S(1)}, u32[]{:S(2)}, u32[]{:S(2)}) collective-permute-start(bf16[128,576]{1,0:T(8,128)(2,1)S(1)} %collective-permute-done.2.refs_0_), channel_id=1, source_target_pairs={{0,16},{16,32},{32,48},{48,64},{64,80},{80,96},{96,112},{112,0},{1... | collective-permute-start | bytes 442376 | tf_op jit(solution)/shard_map/ppermute | solution.py:276
  23.5 6.0 %collective-permute-start.5 = (bf16[128,576]{1,0:T(8,128)(2,1)S(1)}, bf16[128,576]{1,0:T(8,128)(2,1)S(1)}, u32[]{:S(2)}, u32[]{:S(2)}) collective-permute-start(bf16[128,576]{1,0:T(8,128)(2,1)S(1)} %collective-permute-done.3.refs_1_), channel_id=1, source_target_pairs={{0,112},{16,0},{32,16},{48,32},{64,48},{80,64},{96,80},{112,96},{1... | collective-permute-start | bytes 442376 | tf_op jit(solution)/shard_map/ppermute | solution.py:276
  31.9 4.4 %collective-permute-start.12 = (bf16[608,512]{1,0:T(8,128)(2,1)S(1)}, bf16[608,512]{1,0:T(8,128)(2,1)S(1)}, u32[]{:S(2)}, u32[]{:S(2)}) collective-permute-start(bf16[608,512]{1,0:T(8,128)(2,1)S(1)} %collective-permute-done.9.refs_11_), channel_id=1, source_target_pairs={{0,1},{1,0},{2,3},{3,2},{4,5},{5,4},{6,7},{7,6},{8,9},{9,8},{10,11... | collective-permute-start | bytes 1867784 | tf_op jit(solution)/shard_map/ppermute | solution.py:273
  33.7 2.6 %collective-permute-start.10 = (bf16[576,256]{1,0:T(8,128)(2,1)}, bf16[576,256]{1,0:T(8,128)(2,1)S(1)}, u32[]{:S(2)}, u32[]{:S(2)}) collective-permute-start(bf16[576,256]{1,0:T(8,128)(2,1)} %collective-permute-done.7.refs_9_), channel_id=1, source_target_pairs={{0,1},{1,0},{2,3},{3,2},{4,5},{5,4},{6,7},{7,6},{8,9},{9,8},{10,11... | collective-permute-start | bytes 884744 | tf_op jit(solution)/shard_map/ppermute | solution.py:273
  33.7 2.6 %collective-permute-start.11 = (bf16[576,256]{1,0:T(8,128)(2,1)S(1)}, bf16[576,256]{1,0:T(8,128)(2,1)S(1)}, u32[]{:S(2)}, u32[]{:S(2)}) collective-permute-start(bf16[576,256]{1,0:T(8,128)(2,1)S(1)} %collective-permute-done.8.refs_10_), channel_id=1, source_target_pairs={{0,1},{1,0},{2,3},{3,2},{4,5},{5,4},{6,7},{7,6},{8,9},{9,8},{10,11... | collective-permute-start | bytes 884744 | tf_op jit(solution)/shard_map/ppermute | solution.py:273

commit v6 on v5

--- a/solution.py
+++ b/solution.py
@@ -41,31 +41,41 @@
     return jnp.where(position < valid, 0.0, masked_value)
 
 
-def pack_kernel(len_ref, keys_ref, new_ref, shared_ref, direct_ref, stage_ref, new_vmem, sems):
-    head = lax.axis_index("head")
-    core, side = lax.rem(head, 2), lax.rem(head // 2, 2)
-    lat, few = shared_ref.shape
-    width = direct_ref.shape[1]
-    early, late = few // 128, width // 128
-
-    def load(run, slot):
-        place = pl.multiple_of((2 * run + core) * 128, 128)
-        return pltpu.make_async_copy(
-            keys_ref.at[:, pl.ds(place, 128)],
-            stage_ref.at[0:lat, slot * 128 : (slot + 1) * 128],
-            sems.at[slot],
-        )
-
-    loads = [load(side * early + i, i) for i in range(early)]
-    loads += [load(2 * early + i, early + i) for i in range(late)]
-    load_new = pltpu.make_async_copy(new_ref, new_vmem, sems.at[early + late])
-    send_shared = pltpu.make_async_copy(
-        stage_ref.at[0:lat, 0:few], shared_ref, sems.at[early + late + 1]
-    )
-    send_direct = pltpu.make_async_copy(
-        stage_ref.at[:, few : few + width], direct_ref, sems.at[early + late + 2]
-    )
-    for copy in loads[:early] + [load_new] + loads[early:]:
+def runs_of(keys_ref, stage_ref, sems, first, count):
+    core = lax.rem(lax.axis_index("head"), 2)
+    copies = []
+    for i in range(count):
+        place = pl.multiple_of((2 * (first + i) + core) * 128, 128)
+        copies.append(
+            pltpu.make_async_copy(
+                keys_ref.at[:, pl.ds(place, 128)],
+                stage_ref.at[0 : keys_ref.shape[0], i * 128 : (i + 1) * 128],
+                sems.at[i],
+            )
+        )
+    return copies
+
+
+def pack_shared_kernel(keys_ref, shared_ref, stage_ref, sems):
+    side = lax.rem(lax.axis_index("head") // 2, 2)
+    count = shared_ref.shape[1] // 128
+    loads = runs_of(keys_ref, stage_ref, sems, side * count, count)
+    send = pltpu.make_async_copy(stage_ref, shared_ref, sems.at[count])
+    for copy in loads:
+        copy.start()
+    for copy in loads:
+        copy.wait()
+    send.start()
+    send.wait()
+
+
+def pack_direct_kernel(len_ref, keys_ref, new_ref, direct_ref, stage_ref, new_vmem, sems):
+    lat, count = keys_ref.shape[0], direct_ref.shape[1] // 128
+    loads = runs_of(keys_ref, stage_ref, sems, 2 * SHARED // 128, count)
+    load_new = pltpu.make_async_copy(new_ref, new_vmem, sems.at[count])
+    send = pltpu.make_async_copy(stage_ref, direct_ref, sems.at[count + 1])
+    load_new.start()
+    for copy in loads:
         copy.start()
     length = len_ref[0]
     high = length // 256
@@ -74,18 +84,14 @@
     note = jnp.where(
         (r == 0) & (c == 0), high, jnp.where((r == 0) & (c == 1), length - high * 256, 0)
     ).astype(jnp.float32)
-    stage_ref[lat + 16 : lat + 32, few + 128 : few + 256] = note.astype(jnp.bfloat16)
-    for copy in loads[:early]:
+    stage_ref[lat + 16 : lat + 32, 128:256] = note.astype(jnp.bfloat16)
+    load_new.wait()
+    stage_ref[lat : lat + 16, 0:KVR] = new_vmem[:, 0:KVR]
+    stage_ref[lat + 16 : lat + 32, 0 : lat - KVR] = new_vmem[:, KVR:lat]
+    for copy in loads:
         copy.wait()
-    send_shared.start()
-    load_new.wait()
-    stage_ref[lat : lat + 16, few : few + KVR] = new_vmem[:, 0:KVR]
-    stage_ref[lat + 16 : lat + 32, few : few + lat - KVR] = new_vmem[:, KVR:lat]
-    for copy in loads[early:]:
-        copy.wait()
-    send_direct.start()
-    send_shared.wait()
-    send_direct.wait()
+    send.start()
+    send.wait()
 
 
 def run_bias(width, first, core, valid):
@@ -282,26 +288,33 @@
 
     width = cache.shape[0] // 2
     hbm = pl.BlockSpec(memory_space=pltpu.HBM)
-    shared, direct = pl.pallas_call(
-        pack_kernel,
-        in_specs=[SMEM, hbm, hbm],
-        out_specs=[hbm, hbm],
-        out_shape=[
-            jax.ShapeDtypeStruct((lat, SHARED), jnp.bfloat16),
-            jax.ShapeDtypeStruct((lat + EXTRA, width - 2 * SHARED), jnp.bfloat16),
-        ],
+    keys_hbm = pltpu.with_memory_space_constraint(keys, pltpu.HBM)
+    shared = pl.pallas_call(
+        pack_shared_kernel,
+        in_specs=[hbm],
+        out_specs=hbm,
+        out_shape=jax.ShapeDtypeStruct((lat, SHARED), jnp.bfloat16),
         scratch_shapes=[
-            pltpu.VMEM((lat + EXTRA, width - SHARED), jnp.bfloat16),
-            pltpu.VMEM((own_tokens, lat), jnp.bfloat16),
-            pltpu.SemaphoreType.DMA(((width - SHARED) // 128 + 3,)),
+            pltpu.VMEM((lat, SHARED), jnp.bfloat16),
+            pltpu.SemaphoreType.DMA((SHARED // 128 + 1,)),
         ],
         compiler_params=pltpu.CompilerParams(vmem_limit_bytes=4 * 2**20),
-        name="pack",
-    )(
-        cache_lengths,
-        pltpu.with_memory_space_constraint(keys, pltpu.HBM),
-        pltpu.with_memory_space_constraint(new_latents, pltpu.HBM),
-    )
+        name="pack_shared",
+    )(keys_hbm)
+    rest = width - 2 * SHARED
+    direct = pl.pallas_call(
+        pack_direct_kernel,
+        in_specs=[SMEM, hbm, hbm],
+        out_specs=hbm,
+        out_shape=jax.ShapeDtypeStruct((lat + EXTRA, rest), jnp.bfloat16),
+        scratch_shapes=[
+            pltpu.VMEM((lat + EXTRA, rest), jnp.bfloat16),
+            pltpu.VMEM((own_tokens, lat), jnp.bfloat16),
+            pltpu.SemaphoreType.DMA((rest // 128 + 2,)),
+        ],
+        compiler_params=pltpu.CompilerParams(vmem_limit_bytes=4 * 2**20),
+        name="pack_direct",
+    )(cache_lengths, keys_hbm, pltpu.with_memory_space_constraint(new_latents, pltpu.HBM))
     mine, direct = across(shared), across(direct)
 
     up1, down1 = lax.optimization_barrier((up1, down1))

time: 65.9 us -> 66.4 us (level)
  Pallas kernels: 19.2 us -> 22.6 us
  waiting for transfers between devices: 6.48 us -> 3.65 us
  starting transfers between devices: 19.8 us -> 20.8 us
  local copies, waits for them, and re-layouts: 0.94 us -> 0.03 us
    ppermute x2, waiting for transfers between devices: 2.46 us -> 0.73 us  [across(): return lax.ppermute(a, ('ctx', 'head'), moves)]
    pallas_call x3, Pallas kernels: 6.1 us -> 7.82 us  [attend_own(): pl.pallas_call(functools.partial(own_kernel, len(blocks)), in_specs=[SMEM...]
    pallas_call x1 -> x2, Pallas kernels: 2.22 us -> 3.92 us  [the longest x1 2.03 us: shards(): pl.pallas_call(pack_direct_kernel, in_specs=[SMEM, hbm, hbm], out_specs=h...]
    unnamed x10, local copies, waits for them, and re-layouts: 0.94 us -> 0.03 us
    ppermute x3, starting transfers between devices: 2.31 us -> 3.03 us  [swap(): return lax.ppermute(a, 'head', [(h, h ^ 1) for h in range(16)])]
  transfers between devices with their start and end apart: 13 -> 13, of which waited for: 6 -> 3; matrix products, arithmetic and copies ran while one was open for 0% -> 0% of each run, Pallas kernels for 13% -> 18%
where the time goes in v6:
time: 66.4 us; the launch traced here: 66.2 us
  Pallas kernels  22.6 us (34%)
  starting transfers between devices  20.8 us (31%)
  blocking collectives  18.3 us (28%)
  waiting for transfers between devices  3.65 us (5%)
  between operations  0.84 us (1%)
    all_to_all x1, blocking collectives, shards(): lax.all_to_all(parts, 'ctx', 0, 0, axis_index_groups=[[*range(NZ)], [*ran...  18.3 us
    ppermute x6, starting transfers between devices, shift(): lax.ppermute(a, 'ctx', [(c, c // NZ * NZ + (c + step) % NZ) for c in rang...  11.8 us
    pallas_call x1, Pallas kernels, shards(): pl.pallas_call(functools.partial(final_kernel, [3, 2, 3]), in_specs=[SMEM...  9.84 us
    pallas_call x3, Pallas kernels, attend_own(): pl.pallas_call(functools.partial(own_kernel, len(blocks)), in_specs=[SMEM...  7.82 us
    ppermute x3, starting transfers between devices, swap(): return lax.ppermute(a, 'head', [(h, h ^ 1) for h in range(16)])  3.03 us
    ppermute x2, starting transfers between devices, across(): return lax.ppermute(a, ('ctx', 'head'), moves)  2.92 us
    ppermute x6, waiting for transfers between devices, shift(): lax.ppermute(a, 'ctx', [(c, c // NZ * NZ + (c + step) % NZ) for c in rang...  2.7 us
    pallas_call x1, Pallas kernels, shards(): pl.pallas_call(pack_direct_kernel, in_specs=[SMEM, hbm, hbm], out_specs=h...  2.03 us
  transfers between devices with their start and end apart: 13, of which 3 were waited for; matrix products, arithmetic and copies ran while one was open for 0% of the time, Pallas kernels for 18%

profile of v6, /device:TPU:1, one launch (start us, length us, event | category | flops | bytes accessed | tf_op | source)
XLA Modules:
  0.0 66.2 jit_solution(7792598841051343183)
XLA Ops:
  0.0 2.5 %collective-permute-start = (bf16[128,576]{1,0:T(8,128)(2,1)}, bf16[128,576]{1,0:T(8,128)(2,1)}, u32[]{:S(2)}, u32[]{:S(2)}) collective-permute-start(bf16[128,576]{1,0:T(8,128)(2,1)} %bitcast.8), channel_id=1, source_target_pairs={{0,16},{16,32},{32,48},{48,64},{64,80},{80,96},{96,112},{112,0},{1... | collective-permute-start | bytes 442376 | tf_op jit(solution)/shard_map/ppermute | solution.py:282
  2.5 3.9 %collective-permute-start.1 = (bf16[128,576]{1,0:T(8,128)(2,1)}, bf16[128,576]{1,0:T(8,128)(2,1)}, u32[]{:S(2)}, u32[]{:S(2)}) collective-permute-start(bf16[128,576]{1,0:T(8,128)(2,1)} %bitcast.9), channel_id=1, source_target_pairs={{0,112},{16,0},{32,16},{48,32},{64,48},{80,64},{96,80},{112,96},{1... | collective-permute-start | bytes 442376 | tf_op jit(solution)/shard_map/ppermute | solution.py:282
  6.4 1.9 %pack_shared.1 = bf16[576,256]{1,0:T(8,128)(2,1)} custom-call(bf16[576,2048]{1,0:T(8,128)(2,1)} %bitcast.3), custom_call_target="tpu_custom_call" | custom-call | tf_op jit(solution)/shard_map/pack_shared/pallas_call | solution.py:292
  8.3 2.8 %collective-permute-start.7 = (bf16[576,256]{1,0:T(8,128)(2,1)}, bf16[576,256]{1,0:T(8,128)(2,1)}, u32[]{:S(2)}, u32[]{:S(2)}) collective-permute-start(bf16[576,256]{1,0:T(8,128)(2,1)} %pack_shared.1), channel_id=1, source_target_pairs={{0,136},{1,137},{2,138},{3,139},{4,140},{5,141},{6,142},{7,143},{8... | collective-permute-start | bytes 884744 | tf_op jit(solution)/shard_map/ppermute | solution.py:276
  11.8 2.0 %pack_direct.1 = bf16[608,512]{1,0:T(8,128)(2,1)} custom-call(s32[1]{0:T(128)S(6)} %copy.7.len_ref, bf16[576,2048]{1,0:T(8,128)(2,1)} %bitcast.4, bf16[16,576]{1,0:T(8,128)(2,1)} %refs_15_.1), custom_call_target="tpu_custom_call" | custom-call | tf_op jit(solution)/shard_map/pack_direct/pallas_call | solution.py:305
  13.8 0.1 collective-permute-start.9
  13.9 0.1 collective-permute-start.2
  14.0 2.7 %collective-permute-start.3 = (bf16[128,576]{1,0:T(8,128)(2,1)}, bf16[128,576]{1,0:T(8,128)(2,1)S(1)}, u32[]{:S(2)}, u32[]{:S(2)}) collective-permute-start(bf16[128,576]{1,0:T(8,128)(2,1)} %collective-permute-done.1.refs_2_), channel_id=1, source_target_pairs={{0,112},{16,0},{32,16},{48,32},{64,48},{80,64},{96,80},{112,96},{1... | collective-permute-start | bytes 442376 | tf_op jit(solution)/shard_map/ppermute | solution.py:282
  16.7 3.4 %attend_own.3 = (f32[384,512]{1,0:T(8,128)S(1)}, f32[384,128]{1,0:T(8,128)S(1)}, bf16[384,576]{1,0:T(8,128)(2,1)S(1)}) custom-call(s32[1]{0:T(128)S(6)} %copy.7.len_ref, bf16[128,576]{1,0:T(8,128)(2,1)S(1)} %bitcast.10, bf16[128,576]{1,0:T(8,128)(2,1)} %collective-permute-done.refs_1_, bf16[128,576]{1,0:T(8,128)(2,1)} %collective-permute-done.1.refs_2_, ...), custom_call_target="tpu_custom_call" | custom-call | flops 1000000 | bytes 10000 | tf_op jit(solution)/shard_map/attend_own/pallas_call | solution.py:131
  20.1 1.3 %collective-permute-start.8 = (bf16[576,256]{1,0:T(8,128)(2,1)}, bf16[576,256]{1,0:T(8,128)(2,1)S(1)}, u32[]{:S(2)}, u32[]{:S(2)}) collective-permute-start(bf16[576,256]{1,0:T(8,128)(2,1)} %collective-permute-done.7.refs_9_), channel_id=1, source_target_pairs={{0,2},{1,3},{2,0},{3,1},{4,6},{5,7},{6,4},{7,5},{8,10},{9,11},{10,... | collective-permute-start | bytes 884744 | tf_op jit(solution)/shard_map/ppermute | solution.py:323
  21.5 1.7 %collective-permute-start.6 = (bf16[128,576]{1,0:T(8,128)(2,1)S(1)}, bf16[128,576]{1,0:T(8,128)(2,1)S(1)}, u32[]{:S(2)}, u32[]{:S(2)}) collective-permute-start(bf16[128,576]{1,0:T(8,128)(2,1)S(1)} %broadcast_select_fusion), channel_id=1, source_target_pairs={{0,32},{16,112},{32,64},{48,16},{64,96},{80,48},{96,0},{112,80},{1... | collective-permute-start | bytes 442376 | tf_op jit(solution)/shard_map/ppermute | solution.py:326
  23.2 2.0 %collective-permute-start.4 = (bf16[128,576]{1,0:T(8,128)(2,1)S(1)}, bf16[128,576]{1,0:T(8,128)(2,1)S(1)}, u32[]{:S(2)}, u32[]{:S(2)}) collective-permute-start(bf16[128,576]{1,0:T(8,128)(2,1)S(1)} %collective-permute-done.2.refs_0_), channel_id=1, source_target_pairs={{0,16},{16,32},{32,48},{48,64},{64,80},{80,96},{96,112},{112,0},{1... | collective-permute-start | bytes 442376 | tf_op jit(solution)/shard_map/ppermute | solution.py:282
  25.1 0.7 %collective-permute-start.5 = (bf16[128,576]{1,0:T(8,128)(2,1)S(1)}, bf16[128,576]{1,0:T(8,128)(2,1)S(1)}, u32[]{:S(2)}, u32[]{:S(2)}) collective-permute-start(bf16[128,576]{1,0:T(8,128)(2,1)S(1)} %collective-permute-done.3.refs_1_), channel_id=1, source_target_pairs={{0,112},{16,0},{32,16},{48,32},{64,48},{80,64},{96,80},{112,96},{1... | collective-permute-start | bytes 442376 | tf_op jit(solution)/shard_map/ppermute | solution.py:282
  25.8 1.9 %attend_own.4 = (f32[256,512]{1,0:T(8,128)S(1)}, f32[256,128]{1,0:T(8,128)S(1)}, bf16[256,576]{1,0:T(8,128)(2,1)S(1)}) custom-call(s32[1]{0:T(128)S(6)} %copy.7.len_ref, bf16[128,576]{1,0:T(8,128)(2,1)S(1)} %collective-permute-done.2.refs_0_, bf16[128,576]{1,0:T(8,128)(2,1)S(1)} %collective-permute-done.3.refs_1_, bf16[576,2048]{1,0:T(8,128)(2,1)S(1)} %bitcast.6), custom_call_target="tpu_custom_call" | custom-call | flops 1000000 | bytes 10000 | tf_op jit(solution)/shard_map/attend_own/pallas_call | solution.py:131
  27.7 0.2 collective-permute-done.6.refs_2_
  27.9 2.7 %collective-permute-done.4.refs_0_ = bf16[128,576]{1,0:T(8,128)(2,1)S(1)} collective-permute-done((bf16[128,576]{1,0:T(8,128)(2,1)S(1)}, bf16[128,576]{1,0:T(8,128)(2,1)S(1)}, u32[]{:S(2)}, u32[]{:S(2)}) %collective-permute-start.4) | collective-permute-done | bytes 147488 | tf_op jit(solution)/shard_map/ppermute | solution.py:282
  30.6 0.7 %collective-permute-done.9.refs_11_ = bf16[608,512]{1,0:T(8,128)(2,1)S(1)} collective-permute-done((bf16[608,512]{1,0:T(8,128)(2,1)}, bf16[608,512]{1,0:T(8,128)(2,1)S(1)}, u32[]{:S(2)}, u32[]{:S(2)}) %collective-permute-start.9) | collective-permute-done | bytes 622624 | tf_op jit(solution)/shard_map/ppermute | solution.py:276
  31.4 2.5 %collective-permute-start.12 = (bf16[608,512]{1,0:T(8,128)(2,1)S(1)}, bf16[608,512]{1,0:T(8,128)(2,1)S(1)}, u32[]{:S(2)}, u32[]{:S(2)}) collective-permute-start(bf16[608,512]{1,0:T(8,128)(2,1)S(1)} %collective-permute-done.9.refs_11_), channel_id=1, source_target_pairs={{0,1},{1,0},{2,3},{3,2},{4,5},{5,4},{6,7},{7,6},{8,9},{9,8},{10,11... | collective-permute-start | bytes 1867784 | tf_op jit(solution)/shard_map/ppermute | solution.py:279
  33.9 0.1 collective-permute-start.10
  34.0 0.4 collective-permute-start.11
  34.4 2.6 %attend_own.5 = (f32[384,512]{1,0:T(8,128)S(1)}, f32[384,128]{1,0:T(8,128)S(1)}, bf16[384,576]{1,0:T(8,128)(2,1)S(1)}) custom-call(s32[1]{0:T(128)S(6)} %copy.7.len_ref, bf16[128,576]{1,0:T(8,128)(2,1)S(1)} %collective-permute-done.4.refs_0_, bf16[128,576]{1,0:T(8,128)(2,1)S(1)} %collective-permute-done.5.refs_1_, ...), custom_call_target="tpu_custom_call" | custom-call | flops 1000000 | bytes 10000 | tf_op jit(solution)/shard_map/attend_own/pallas_call | solution.py:131
  37.1 9.8 %attend_final.1 = bf16[8,144,128]{2,1,0:T(8,128)(2,1)S(1)} custom-call(s32[256]{0:T(256)S(1)} %copy-done.4, f32[384,512]{1,0:T(8,128)S(1)} %get-tuple-element.41.refs_0_, f32[384,128]{1,0:T(8,128)S(1)} %get-tuple-element.42.refs_1_, bf16[384,576]{1,0:T(8,128)(2,1)S(1)} %get-tuple-element.43.refs_2_, f32[256,512]{1,0:T(8,128)S(1)} %get-tuple-element.49.refs_3_, ...), custom_call_target="tpu_custom_call" | custom-call | flops 1000000 | bytes 10000 | tf_op jit(solution)/shard_map/attend_final/pallas_call | solution.py:339
  46.9 18.3 %all_to_all.5.part_ref = bf16[8,144,128]{2,1,0:T(8,128)(2,1)S(1)} all-to-all(bf16[8,144,128]{2,1,0:T(8,128)(2,1)S(1)} %attend_final.1), channel_id=1, replica_groups={{0,16,32,48,64,80,96,112},{128,144,160,176,192,208,224,240},{1,17,33,49..., dimensions={0} | all-to-all | bytes 589824 | tf_op jit(solution)/shard_map/all_to_all | solution.py:349
  65.2 1.0 %merge.1 = bf16[128,128]{1,0:T(8,128)(2,1)} custom-call(bf16[8,144,128]{2,1,0:T(8,128)(2,1)S(1)} %all_to_all.5.part_ref), custom_call_target="tpu_custom_call" | custom-call | tf_op jit(solution)/shard_map/merge/pallas_call | solution.py:352
  (21 shorter events, 0.1 us)
Async XLA Ops:
  0.0 13.9 %collective-permute-start = (bf16[128,576]{1,0:T(8,128)(2,1)}, bf16[128,576]{1,0:T(8,128)(2,1)}, u32[]{:S(2)}, u32[]{:S(2)}) collective-permute-start(bf16[128,576]{1,0:T(8,128)(2,1)} %bitcast.8), channel_id=1, source_target_pairs={{0,16},{16,32},{32,48},{48,64},{64,80},{80,96},{96,112},{112,0},{1... | collective-permute-start | bytes 442376 | tf_op jit(solution)/shard_map/ppermute | solution.py:282
  2.5 11.5 %collective-permute-start.1 = (bf16[128,576]{1,0:T(8,128)(2,1)}, bf16[128,576]{1,0:T(8,128)(2,1)}, u32[]{:S(2)}, u32[]{:S(2)}) collective-permute-start(bf16[128,576]{1,0:T(8,128)(2,1)} %bitcast.9), channel_id=1, source_target_pairs={{0,112},{16,0},{32,16},{48,32},{64,48},{80,64},{96,80},{112,96},{1... | collective-permute-start | bytes 442376 | tf_op jit(solution)/shard_map/ppermute | solution.py:282
  6.4 10.3 %copy-start = (bf16[2048,576]{0,1:T(8,128)(2,1)S(1)}, bf16[2048,576]{0,1:T(8,128)(2,1)}, u32[]{:S(2)}) copy-start(bf16[2048,576]{0,1:T(8,128)(2,1)} %param.7) | copy-start | bytes 7077892
  6.4 10.3 %copy-start.2 = (bf16[16,8,576]{2,1,0:T(8,128)(2,1)S(1)}, bf16[16,8,576]{2,1,0:T(8,128)(2,1)}, u32[]{:S(2)}) copy-start(bf16[16,8,576]{2,1,0:T(8,128)(2,1)} %param.6) | copy-start | bytes 442372
  8.3 11.8 %collective-permute-start.7 = (bf16[576,256]{1,0:T(8,128)(2,1)}, bf16[576,256]{1,0:T(8,128)(2,1)}, u32[]{:S(2)}, u32[]{:S(2)}) collective-permute-start(bf16[576,256]{1,0:T(8,128)(2,1)} %pack_shared.1), channel_id=1, source_target_pairs={{0,136},{1,137},{2,138},{3,139},{4,140},{5,141},{6,142},{7,143},{8... | collective-permute-start | bytes 884744 | tf_op jit(solution)/shard_map/ppermute | solution.py:276
  13.8 17.5 %collective-permute-start.9 = (bf16[608,512]{1,0:T(8,128)(2,1)}, bf16[608,512]{1,0:T(8,128)(2,1)S(1)}, u32[]{:S(2)}, u32[]{:S(2)}) collective-permute-start(bf16[608,512]{1,0:T(8,128)(2,1)} %pack_direct.1), channel_id=1, source_target_pairs={{0,136},{1,137},{2,138},{3,139},{4,140},{5,141},{6,142},{7,143},{8... | collective-permute-start | bytes 1867784 | tf_op jit(solution)/shard_map/ppermute | solution.py:276
  13.9 6.1 %collective-permute-start.2 = (bf16[128,576]{1,0:T(8,128)(2,1)}, bf16[128,576]{1,0:T(8,128)(2,1)S(1)}, u32[]{:S(2)}, u32[]{:S(2)}) collective-permute-start(bf16[128,576]{1,0:T(8,128)(2,1)} %collective-permute-done.refs_1_), channel_id=1, source_target_pairs={{0,16},{16,32},{32,48},{48,64},{64,80},{80,96},{96,112},{112,0},{1... | collective-permute-start | bytes 442376 | tf_op jit(solution)/shard_map/ppermute | solution.py:282
  14.0 6.0 %collective-permute-start.3 = (bf16[128,576]{1,0:T(8,128)(2,1)}, bf16[128,576]{1,0:T(8,128)(2,1)S(1)}, u32[]{:S(2)}, u32[]{:S(2)}) collective-permute-start(bf16[128,576]{1,0:T(8,128)(2,1)} %collective-permute-done.1.refs_2_), channel_id=1, source_target_pairs={{0,112},{16,0},{32,16},{48,32},{64,48},{80,64},{96,80},{112,96},{1... | collective-permute-start | bytes 442376 | tf_op jit(solution)/shard_map/ppermute | solution.py:282
  20.1 10.5 %collective-permute-start.8 = (bf16[576,256]{1,0:T(8,128)(2,1)}, bf16[576,256]{1,0:T(8,128)(2,1)S(1)}, u32[]{:S(2)}, u32[]{:S(2)}) collective-permute-start(bf16[576,256]{1,0:T(8,128)(2,1)} %collective-permute-done.7.refs_9_), channel_id=1, source_target_pairs={{0,2},{1,3},{2,0},{3,1},{4,6},{5,7},{6,4},{7,5},{8,10},{9,11},{10,... | collective-permute-start | bytes 884744 | tf_op jit(solution)/shard_map/ppermute | solution.py:323
  21.4 15.6 %copy-start.1 = (bf16[8,512,128]{2,1,0:T(8,128)(2,1)S(1)}, bf16[8,512,128]{2,1,0:T(8,128)(2,1)}, u32[]{:S(2)}) copy-start(bf16[8,512,128]{2,1,0:T(8,128)(2,1)} %refs_16_.1) | copy-start | bytes 3145732
  21.4 15.6 %copy-start.3 = (bf16[16,576]{1,0:T(8,128)(2,1)S(1)}, bf16[16,576]{1,0:T(8,128)(2,1)}, u32[]{:S(2)}) copy-start(bf16[16,576]{1,0:T(8,128)(2,1)} %refs_15_.1) | copy-start | bytes 55300
  21.5 15.6 %copy-start.4 = (s32[256]{0:T(256)S(1)}, s32[256]{0:T(256)}, u32[]{:S(2)}) copy-start(s32[256]{0:T(256)} %offset_ref.1) | copy-start | bytes 3076
  21.5 6.5 %collective-permute-start.6 = (bf16[128,576]{1,0:T(8,128)(2,1)S(1)}, bf16[128,576]{1,0:T(8,128)(2,1)S(1)}, u32[]{:S(2)}, u32[]{:S(2)}) collective-permute-start(bf16[128,576]{1,0:T(8,128)(2,1)S(1)} %broadcast_select_fusion), channel_id=1, source_target_pairs={{0,32},{16,112},{32,64},{48,16},{64,96},{80,48},{96,0},{112,80},{1... | collective-permute-start | bytes 442376 | tf_op jit(solution)/shard_map/ppermute | solution.py:326
  23.2 7.5 %collective-permute-start.4 = (bf16[128,576]{1,0:T(8,128)(2,1)S(1)}, bf16[128,576]{1,0:T(8,128)(2,1)S(1)}, u32[]{:S(2)}, u32[]{:S(2)}) collective-permute-start(bf16[128,576]{1,0:T(8,128)(2,1)S(1)} %collective-permute-done.2.refs_0_), channel_id=1, source_target_pairs={{0,16},{16,32},{32,48},{48,64},{64,80},{80,96},{96,112},{112,0},{1... | collective-permute-start | bytes 442376 | tf_op jit(solution)/shard_map/ppermute | solution.py:282
  25.1 5.5 %collective-permute-start.5 = (bf16[128,576]{1,0:T(8,128)(2,1)S(1)}, bf16[128,576]{1,0:T(8,128)(2,1)S(1)}, u32[]{:S(2)}, u32[]{:S(2)}) collective-permute-start(bf16[128,576]{1,0:T(8,128)(2,1)S(1)} %collective-permute-done.3.refs_1_), channel_id=1, source_target_pairs={{0,112},{16,0},{32,16},{48,32},{64,48},{80,64},{96,80},{112,96},{1... | collective-permute-start | bytes 442376 | tf_op jit(solution)/shard_map/ppermute | solution.py:282
  31.4 5.7 %collective-permute-start.12 = (bf16[608,512]{1,0:T(8,128)(2,1)S(1)}, bf16[608,512]{1,0:T(8,128)(2,1)S(1)}, u32[]{:S(2)}, u32[]{:S(2)}) collective-permute-start(bf16[608,512]{1,0:T(8,128)(2,1)S(1)} %collective-permute-done.9.refs_11_), channel_id=1, source_target_pairs={{0,1},{1,0},{2,3},{3,2},{4,5},{5,4},{6,7},{7,6},{8,9},{9,8},{10,11... | collective-permute-start | bytes 1867784 | tf_op jit(solution)/shard_map/ppermute | solution.py:279
  33.9 3.1 %collective-permute-start.10 = (bf16[576,256]{1,0:T(8,128)(2,1)}, bf16[576,256]{1,0:T(8,128)(2,1)S(1)}, u32[]{:S(2)}, u32[]{:S(2)}) collective-permute-start(bf16[576,256]{1,0:T(8,128)(2,1)} %collective-permute-done.7.refs_9_), channel_id=1, source_target_pairs={{0,1},{1,0},{2,3},{3,2},{4,5},{5,4},{6,7},{7,6},{8,9},{9,8},{10,11... | collective-permute-start | bytes 884744 | tf_op jit(solution)/shard_map/ppermute | solution.py:279
  34.0 3.0 %collective-permute-start.11 = (bf16[576,256]{1,0:T(8,128)(2,1)S(1)}, bf16[576,256]{1,0:T(8,128)(2,1)S(1)}, u32[]{:S(2)}, u32[]{:S(2)}) collective-permute-start(bf16[576,256]{1,0:T(8,128)(2,1)S(1)} %collective-permute-done.8.refs_10_), channel_id=1, source_target_pairs={{0,1},{1,0},{2,3},{3,2},{4,5},{5,4},{6,7},{7,6},{8,9},{9,8},{10,11... | collective-permute-start | bytes 884744 | tf_op jit(solution)/shard_map/ppermute | solution.py:279

commit v7 on v5

--- a/solution.py
+++ b/solution.py
@@ -12,7 +12,7 @@
 EXTRA = 32
 STAT = 16
 NZ = 8
-OFFSETS = [0, 7, 1, 6, 2, 5, 3, 4]
+OFFSETS = [7, 1, 6, 2, 0, 5, 3, 4]
 SHARED = 256
 
 exp_scale = 192.0 ** (-0.5) * 1.4426950408889634
@@ -306,7 +306,7 @@
 
     up1, down1 = lax.optimization_barrier((up1, down1))
     up2, down2 = shift(up1, 1), shift(down1, -1)
-    state1 = attend_own(cache_lengths, [own, up1, down1], keys)
+    state1 = attend_own(cache_lengths, [up1, down1], keys)
     other = lax.ppermute(mine, "head", [(h, h ^ 2) for h in range(16)])
     up2, down2, state1 = lax.optimization_barrier((up2, down2, state1))
     up3, down3 = shift(up2, 1), shift(down2, -1)
@@ -315,7 +315,7 @@
         "ctx",
         [(c, c // NZ * NZ + (c + (2 if c % 2 == 0 else -2)) % NZ) for c in range(16)],
     )
-    state2 = attend_own(cache_lengths, [up2, down2], keys)
+    state2 = attend_own(cache_lengths, [up2, down2, own], keys)
     up3, down3, four, state2, mine, other, direct = lax.optimization_barrier(
         (up3, down3, four, state2, mine, other, direct)
     )
@@ -324,7 +324,7 @@
     far_mine, far_other, far_direct, state3 = lax.optimization_barrier((far_mine, far_other, far_direct, state3))
     states = [part for state in (state1, state2, state3) for part in state]
     parts = pl.pallas_call(
-        functools.partial(final_kernel, [3, 2, 3]),
+        functools.partial(final_kernel, [2, 3, 3]),
         in_specs=[SMEM] + [VMEM] * 17,
         out_specs=VMEM,
         out_shape=jax.ShapeDtypeStruct((NZ, rows + STAT, VDIM), jnp.bfloat16),

time: 65.9 us -> 65.5 us (level); the launches traced: 66.1 us -> 64.5 us
  blocking collectives: 18.9 us -> 17.4 us
  local copies, waits for them, and re-layouts: 0.94 us -> 0.03 us
  waiting for transfers between devices: 6.48 us -> 7.33 us
    all_to_all x1, blocking collectives: 18.9 us -> 17.4 us  [shards(): lax.all_to_all(parts, 'ctx', 0, 0, axis_index_groups=[[*range(NZ)], [*ran...]
    ppermute x2, waiting for transfers between devices: 2.46 us -> 3.9 us  [across(): return lax.ppermute(a, ('ctx', 'head'), moves)]
    unnamed x10, local copies, waits for them, and re-layouts: 0.94 us -> 0.03 us
where the time goes in v7:
time: 65.5 us; the launch traced here: 64.5 us
  starting transfers between devices  19.8 us (30%)
  Pallas kernels  19.2 us (29%)
  blocking collectives  17.4 us (27%)
  waiting for transfers between devices  7.33 us (11%)
  between operations  0.77 us (1%)
    all_to_all x1, blocking collectives, shards(): lax.all_to_all(parts, 'ctx', 0, 0, axis_index_groups=[[*range(NZ)], [*ran...  17.4 us
    ppermute x6, starting transfers between devices, shift(): lax.ppermute(a, 'ctx', [(c, c // NZ * NZ + (c + step) % NZ) for c in rang...  11.8 us
    pallas_call x1, Pallas kernels, shards(): pl.pallas_call(functools.partial(final_kernel, [2, 3, 3]), in_specs=[SMEM...  9.76 us
    pallas_call x3, Pallas kernels, attend_own(): pl.pallas_call(functools.partial(own_kernel, len(blocks)), in_specs=[SMEM...  6.18 us
    ppermute x2, waiting for transfers between devices, across(): return lax.ppermute(a, ('ctx', 'head'), moves)  3.9 us
    ppermute x6, waiting for transfers between devices, shift(): lax.ppermute(a, 'ctx', [(c, c // NZ * NZ + (c + step) % NZ) for c in rang...  2.97 us
    ppermute x2, starting transfers between devices, across(): return lax.ppermute(a, ('ctx', 'head'), moves)  2.92 us
    ppermute x3, starting transfers between devices, swap(): return lax.ppermute(a, 'head', [(h, h ^ 1) for h in range(16)])  2.31 us
  transfers between devices with their start and end apart: 13, of which 6 were waited for; matrix products, arithmetic and copies ran while one was open for 0% of the time, Pallas kernels for 13%

profile of v7, /device:TPU:1, one launch (start us, length us, event | category | flops | bytes accessed | tf_op | source)
XLA Modules:
  0.0 64.5 jit_solution(14645963812561655523)
XLA Ops:
  0.0 2.5 %collective-permute-start = (bf16[128,576]{1,0:T(8,128)(2,1)}, bf16[128,576]{1,0:T(8,128)(2,1)}, u32[]{:S(2)}, u32[]{:S(2)}) collective-permute-start(bf16[128,576]{1,0:T(8,128)(2,1)} %bitcast.7), channel_id=1, source_target_pairs={{0,16},{16,32},{32,48},{48,64},{64,80},{80,96},{96,112},{112,0},{1... | collective-permute-start | bytes 442376 | tf_op jit(solution)/shard_map/ppermute | solution.py:276
  2.5 4.0 %collective-permute-start.1 = (bf16[128,576]{1,0:T(8,128)(2,1)}, bf16[128,576]{1,0:T(8,128)(2,1)}, u32[]{:S(2)}, u32[]{:S(2)}) collective-permute-start(bf16[128,576]{1,0:T(8,128)(2,1)} %bitcast.8), channel_id=1, source_target_pairs={{0,112},{16,0},{32,16},{48,32},{64,48},{80,64},{96,80},{112,96},{1... | collective-permute-start | bytes 442376 | tf_op jit(solution)/shard_map/ppermute | solution.py:276
  7.1 2.3 %pack.1 = (bf16[576,256]{1,0:T(8,128)(2,1)}, bf16[608,512]{1,0:T(8,128)(2,1)}) custom-call(s32[1]{0:T(128)S(6)} %copy.7.len_ref, bf16[576,2048]{1,0:T(8,128)(2,1)} %bitcast.3, bf16[16,576]{1,0:T(8,128)(2,1)} %refs_15_.1), custom_call_target="tpu_custom_call" | custom-call | tf_op jit(solution)/shard_map/pack/pallas_call | solution.py:285
  9.4 2.8 %collective-permute-start.7 = (bf16[576,256]{1,0:T(8,128)(2,1)}, bf16[576,256]{1,0:T(8,128)(2,1)}, u32[]{:S(2)}, u32[]{:S(2)}) collective-permute-start(bf16[576,256]{1,0:T(8,128)(2,1)} %get-tuple-element.51), channel_id=1, source_target_pairs={{0,136},{1,137},{2,138},{3,139},{4,140},{5,141},{6,142},{7,143},{8... | collective-permute-start | bytes 884744 | tf_op jit(solution)/shard_map/ppermute | solution.py:270
  12.2 0.1 collective-permute-start.9
  12.4 2.7 %collective-permute-start.3 = (bf16[128,576]{1,0:T(8,128)(2,1)}, bf16[128,576]{1,0:T(8,128)(2,1)S(1)}, u32[]{:S(2)}, u32[]{:S(2)}) collective-permute-start(bf16[128,576]{1,0:T(8,128)(2,1)} %collective-permute-done.1.refs_1_), channel_id=1, source_target_pairs={{0,112},{16,0},{32,16},{48,32},{64,48},{80,64},{96,80},{112,96},{1... | collective-permute-start | bytes 442376 | tf_op jit(solution)/shard_map/ppermute | solution.py:276
  15.0 2.3 %attend_own.3 = (f32[256,512]{1,0:T(8,128)S(1)}, f32[256,128]{1,0:T(8,128)S(1)}, bf16[256,576]{1,0:T(8,128)(2,1)S(1)}) custom-call(s32[1]{0:T(128)S(6)} %copy.7.len_ref, bf16[128,576]{1,0:T(8,128)(2,1)} %collective-permute-done.refs_0_, bf16[128,576]{1,0:T(8,128)(2,1)} %collective-permute-done.1.refs_1_, bf16[576,2048]{1,0:T(8,128)(2,1)S(1)} %bitcast.4), custom_call_target="tpu_custom_call" | custom-call | flops 1000000 | bytes 10000 | tf_op jit(solution)/shard_map/attend_own/pallas_call | solution.py:125
  17.4 1.0 %collective-permute-done.2.refs_0_ = bf16[128,576]{1,0:T(8,128)(2,1)S(1)} collective-permute-done((bf16[128,576]{1,0:T(8,128)(2,1)}, bf16[128,576]{1,0:T(8,128)(2,1)S(1)}, u32[]{:S(2)}, u32[]{:S(2)}) %collective-permute-start.2) | collective-permute-done | bytes 147488 | tf_op jit(solution)/shard_map/ppermute | solution.py:276
  18.3 0.4 collective-permute-done.7.refs_9_
  18.7 1.2 %collective-permute-start.8 = (bf16[576,256]{1,0:T(8,128)(2,1)}, bf16[576,256]{1,0:T(8,128)(2,1)S(1)}, u32[]{:S(2)}, u32[]{:S(2)}) collective-permute-start(bf16[576,256]{1,0:T(8,128)(2,1)} %collective-permute-done.7.refs_9_), channel_id=1, source_target_pairs={{0,2},{1,3},{2,0},{3,1},{4,6},{5,7},{6,4},{7,5},{8,10},{9,11},{10,... | collective-permute-start | bytes 884744 | tf_op jit(solution)/shard_map/ppermute | solution.py:310
  20.0 1.5 %collective-permute-start.6 = (bf16[128,576]{1,0:T(8,128)(2,1)S(1)}, bf16[128,576]{1,0:T(8,128)(2,1)S(1)}, u32[]{:S(2)}, u32[]{:S(2)}) collective-permute-start(bf16[128,576]{1,0:T(8,128)(2,1)S(1)} %broadcast_select_fusion), channel_id=1, source_target_pairs={{0,32},{16,112},{32,64},{48,16},{64,96},{80,48},{96,0},{112,80},{1... | collective-permute-start | bytes 442376 | tf_op jit(solution)/shard_map/ppermute | solution.py:313
  21.5 2.0 %collective-permute-start.4 = (bf16[128,576]{1,0:T(8,128)(2,1)S(1)}, bf16[128,576]{1,0:T(8,128)(2,1)S(1)}, u32[]{:S(2)}, u32[]{:S(2)}) collective-permute-start(bf16[128,576]{1,0:T(8,128)(2,1)S(1)} %collective-permute-done.2.refs_0_), channel_id=1, source_target_pairs={{0,16},{16,32},{32,48},{48,64},{64,80},{80,96},{96,112},{112,0},{1... | collective-permute-start | bytes 442376 | tf_op jit(solution)/shard_map/ppermute | solution.py:276
  23.6 0.6 %collective-permute-start.5 = (bf16[128,576]{1,0:T(8,128)(2,1)S(1)}, bf16[128,576]{1,0:T(8,128)(2,1)S(1)}, u32[]{:S(2)}, u32[]{:S(2)}) collective-permute-start(bf16[128,576]{1,0:T(8,128)(2,1)S(1)} %collective-permute-done.3.refs_1_), channel_id=1, source_target_pairs={{0,112},{16,0},{32,16},{48,32},{64,48},{80,64},{96,80},{112,96},{1... | collective-permute-start | bytes 442376 | tf_op jit(solution)/shard_map/ppermute | solution.py:276
  24.2 1.9 %attend_own.4 = (f32[384,512]{1,0:T(8,128)S(1)}, f32[384,128]{1,0:T(8,128)S(1)}, bf16[384,576]{1,0:T(8,128)(2,1)S(1)}) custom-call(s32[1]{0:T(128)S(6)} %copy.7.len_ref, bf16[128,576]{1,0:T(8,128)(2,1)S(1)} %collective-permute-done.2.refs_0_, bf16[128,576]{1,0:T(8,128)(2,1)S(1)} %collective-permute-done.3.refs_1_, bf16[128,576]{1,0:T(8,128)(2,1)S(1)} %bitcast.9, ...), custom_call_target="tpu_custom_call" | custom-call | flops 1000000 | bytes 10000 | tf_op jit(solution)/shard_map/attend_own/pallas_call | solution.py:125
  26.1 0.3 collective-permute-done.6.refs_2_
  26.5 1.9 %collective-permute-done.4.refs_0_ = bf16[128,576]{1,0:T(8,128)(2,1)S(1)} collective-permute-done((bf16[128,576]{1,0:T(8,128)(2,1)S(1)}, bf16[128,576]{1,0:T(8,128)(2,1)S(1)}, u32[]{:S(2)}, u32[]{:S(2)}) %collective-permute-start.4) | collective-permute-done | bytes 147488 | tf_op jit(solution)/shard_map/ppermute | solution.py:276
  28.4 3.5 %collective-permute-done.9.refs_11_ = bf16[608,512]{1,0:T(8,128)(2,1)S(1)} collective-permute-done((bf16[608,512]{1,0:T(8,128)(2,1)}, bf16[608,512]{1,0:T(8,128)(2,1)S(1)}, u32[]{:S(2)}, u32[]{:S(2)}) %collective-permute-start.9) | collective-permute-done | bytes 622624 | tf_op jit(solution)/shard_map/ppermute | solution.py:270
  32.0 1.8 %collective-permute-start.12 = (bf16[608,512]{1,0:T(8,128)(2,1)S(1)}, bf16[608,512]{1,0:T(8,128)(2,1)S(1)}, u32[]{:S(2)}, u32[]{:S(2)}) collective-permute-start(bf16[608,512]{1,0:T(8,128)(2,1)S(1)} %collective-permute-done.9.refs_11_), channel_id=1, source_target_pairs={{0,1},{1,0},{2,3},{3,2},{4,5},{5,4},{6,7},{7,6},{8,9},{9,8},{10,11... | collective-permute-start | bytes 1867784 | tf_op jit(solution)/shard_map/ppermute | solution.py:273
  33.8 0.5 collective-permute-start.11
  34.3 2.0 %attend_own.5 = (f32[384,512]{1,0:T(8,128)S(1)}, f32[384,128]{1,0:T(8,128)S(1)}, bf16[384,576]{1,0:T(8,128)(2,1)S(1)}) custom-call(s32[1]{0:T(128)S(6)} %copy.7.len_ref, bf16[128,576]{1,0:T(8,128)(2,1)S(1)} %collective-permute-done.4.refs_0_, bf16[128,576]{1,0:T(8,128)(2,1)S(1)} %collective-permute-done.5.refs_1_, ...), custom_call_target="tpu_custom_call" | custom-call | flops 1000000 | bytes 10000 | tf_op jit(solution)/shard_map/attend_own/pallas_call | solution.py:125
  36.2 0.1 collective-permute-done.10.refs_12_
  36.4 9.8 %attend_final.1 = bf16[8,144,128]{2,1,0:T(8,128)(2,1)S(1)} custom-call(s32[256]{0:T(256)S(1)} %copy-done.4, f32[256,512]{1,0:T(8,128)S(1)} %get-tuple-element.43.refs_0_, f32[256,128]{1,0:T(8,128)S(1)} %get-tuple-element.44.refs_1_, bf16[256,576]{1,0:T(8,128)(2,1)S(1)} %get-tuple-element.45.refs_2_, f32[384,512]{1,0:T(8,128)S(1)} %get-tuple-element.53.refs_3_, ...), custom_call_target="tpu_custom_call" | custom-call | flops 1000000 | bytes 10000 | tf_op jit(solution)/shard_map/attend_final/pallas_call | solution.py:326
  46.2 17.4 %all_to_all.5.part_ref = bf16[8,144,128]{2,1,0:T(8,128)(2,1)S(1)} all-to-all(bf16[8,144,128]{2,1,0:T(8,128)(2,1)S(1)} %attend_final.1), channel_id=1, replica_groups={{0,16,32,48,64,80,96,112},{128,144,160,176,192,208,224,240},{1,17,33,49..., dimensions={0} | all-to-all | bytes 589824 | tf_op jit(solution)/shard_map/all_to_all | solution.py:336
  63.5 1.0 %merge.1 = bf16[128,128]{1,0:T(8,128)(2,1)} custom-call(bf16[8,144,128]{2,1,0:T(8,128)(2,1)S(1)} %all_to_all.5.part_ref), custom_call_target="tpu_custom_call" | custom-call | tf_op jit(solution)/shard_map/merge/pallas_call | solution.py:339
  (20 shorter events, 0.1 us)
Async XLA Ops:
  0.0 15.0 %copy-start = (bf16[2048,576]{0,1:T(8,128)(2,1)S(1)}, bf16[2048,576]{0,1:T(8,128)(2,1)}, u32[]{:S(2)}) copy-start(bf16[2048,576]{0,1:T(8,128)(2,1)} %param.7) | copy-start | bytes 7077892
  0.0 12.3 %collective-permute-start = (bf16[128,576]{1,0:T(8,128)(2,1)}, bf16[128,576]{1,0:T(8,128)(2,1)}, u32[]{:S(2)}, u32[]{:S(2)}) collective-permute-start(bf16[128,576]{1,0:T(8,128)(2,1)} %bitcast.7), channel_id=1, source_target_pairs={{0,16},{16,32},{32,48},{48,64},{64,80},{80,96},{96,112},{112,0},{1... | collective-permute-start | bytes 442376 | tf_op jit(solution)/shard_map/ppermute | solution.py:276
  2.5 9.9 %collective-permute-start.1 = (bf16[128,576]{1,0:T(8,128)(2,1)}, bf16[128,576]{1,0:T(8,128)(2,1)}, u32[]{:S(2)}, u32[]{:S(2)}) collective-permute-start(bf16[128,576]{1,0:T(8,128)(2,1)} %bitcast.8), channel_id=1, source_target_pairs={{0,112},{16,0},{32,16},{48,32},{64,48},{80,64},{96,80},{112,96},{1... | collective-permute-start | bytes 442376 | tf_op jit(solution)/shard_map/ppermute | solution.py:276
  7.1 17.1 %copy-start.2 = (bf16[16,8,576]{2,1,0:T(8,128)(2,1)S(1)}, bf16[16,8,576]{2,1,0:T(8,128)(2,1)}, u32[]{:S(2)}) copy-start(bf16[16,8,576]{2,1,0:T(8,128)(2,1)} %param.6) | copy-start | bytes 442372
  9.4 9.3 %collective-permute-start.7 = (bf16[576,256]{1,0:T(8,128)(2,1)}, bf16[576,256]{1,0:T(8,128)(2,1)}, u32[]{:S(2)}, u32[]{:S(2)}) collective-permute-start(bf16[576,256]{1,0:T(8,128)(2,1)} %get-tuple-element.51), channel_id=1, source_target_pairs={{0,136},{1,137},{2,138},{3,139},{4,140},{5,141},{6,142},{7,143},{8... | collective-permute-start | bytes 884744 | tf_op jit(solution)/shard_map/ppermute | solution.py:270
  12.2 19.7 %collective-permute-start.9 = (bf16[608,512]{1,0:T(8,128)(2,1)}, bf16[608,512]{1,0:T(8,128)(2,1)S(1)}, u32[]{:S(2)}, u32[]{:S(2)}) collective-permute-start(bf16[608,512]{1,0:T(8,128)(2,1)} %get-tuple-element.52), channel_id=1, source_target_pairs={{0,136},{1,137},{2,138},{3,139},{4,140},{5,141},{6,142},{7,143},{8... | collective-permute-start | bytes 1867784 | tf_op jit(solution)/shard_map/ppermute | solution.py:270
  12.3 6.0 %collective-permute-start.2 = (bf16[128,576]{1,0:T(8,128)(2,1)}, bf16[128,576]{1,0:T(8,128)(2,1)S(1)}, u32[]{:S(2)}, u32[]{:S(2)}) collective-permute-start(bf16[128,576]{1,0:T(8,128)(2,1)} %collective-permute-done.refs_0_), channel_id=1, source_target_pairs={{0,16},{16,32},{32,48},{48,64},{64,80},{80,96},{96,112},{112,0},{1... | collective-permute-start | bytes 442376 | tf_op jit(solution)/shard_map/ppermute | solution.py:276
  12.4 6.0 %collective-permute-start.3 = (bf16[128,576]{1,0:T(8,128)(2,1)}, bf16[128,576]{1,0:T(8,128)(2,1)S(1)}, u32[]{:S(2)}, u32[]{:S(2)}) collective-permute-start(bf16[128,576]{1,0:T(8,128)(2,1)} %collective-permute-done.1.refs_1_), channel_id=1, source_target_pairs={{0,112},{16,0},{32,16},{48,32},{64,48},{80,64},{96,80},{112,96},{1... | collective-permute-start | bytes 442376 | tf_op jit(solution)/shard_map/ppermute | solution.py:276
  18.7 9.7 %collective-permute-start.8 = (bf16[576,256]{1,0:T(8,128)(2,1)}, bf16[576,256]{1,0:T(8,128)(2,1)S(1)}, u32[]{:S(2)}, u32[]{:S(2)}) collective-permute-start(bf16[576,256]{1,0:T(8,128)(2,1)} %collective-permute-done.7.refs_9_), channel_id=1, source_target_pairs={{0,2},{1,3},{2,0},{3,1},{4,6},{5,7},{6,4},{7,5},{8,10},{9,11},{10,... | collective-permute-start | bytes 884744 | tf_op jit(solution)/shard_map/ppermute | solution.py:310
  20.0 16.4 %copy-start.1 = (bf16[8,512,128]{2,1,0:T(8,128)(2,1)S(1)}, bf16[8,512,128]{2,1,0:T(8,128)(2,1)}, u32[]{:S(2)}) copy-start(bf16[8,512,128]{2,1,0:T(8,128)(2,1)} %refs_16_.1) | copy-start | bytes 3145732
  20.0 16.4 %copy-start.3 = (bf16[16,576]{1,0:T(8,128)(2,1)S(1)}, bf16[16,576]{1,0:T(8,128)(2,1)}, u32[]{:S(2)}) copy-start(bf16[16,576]{1,0:T(8,128)(2,1)} %refs_15_.1) | copy-start | bytes 55300
  20.0 16.4 %copy-start.4 = (s32[256]{0:T(256)S(1)}, s32[256]{0:T(256)}, u32[]{:S(2)}) copy-start(s32[256]{0:T(256)} %offset_ref.1) | copy-start | bytes 3076
  20.0 6.5 %collective-permute-start.6 = (bf16[128,576]{1,0:T(8,128)(2,1)S(1)}, bf16[128,576]{1,0:T(8,128)(2,1)S(1)}, u32[]{:S(2)}, u32[]{:S(2)}) collective-permute-start(bf16[128,576]{1,0:T(8,128)(2,1)S(1)} %broadcast_select_fusion), channel_id=1, source_target_pairs={{0,32},{16,112},{32,64},{48,16},{64,96},{80,48},{96,0},{112,80},{1... | collective-permute-start | bytes 442376 | tf_op jit(solution)/shard_map/ppermute | solution.py:313
  21.5 6.9 %collective-permute-start.4 = (bf16[128,576]{1,0:T(8,128)(2,1)S(1)}, bf16[128,576]{1,0:T(8,128)(2,1)S(1)}, u32[]{:S(2)}, u32[]{:S(2)}) collective-permute-start(bf16[128,576]{1,0:T(8,128)(2,1)S(1)} %collective-permute-done.2.refs_0_), channel_id=1, source_target_pairs={{0,16},{16,32},{32,48},{48,64},{64,80},{80,96},{96,112},{112,0},{1... | collective-permute-start | bytes 442376 | tf_op jit(solution)/shard_map/ppermute | solution.py:276
  23.6 4.9 %collective-permute-start.5 = (bf16[128,576]{1,0:T(8,128)(2,1)S(1)}, bf16[128,576]{1,0:T(8,128)(2,1)S(1)}, u32[]{:S(2)}, u32[]{:S(2)}) collective-permute-start(bf16[128,576]{1,0:T(8,128)(2,1)S(1)} %collective-permute-done.3.refs_1_), channel_id=1, source_target_pairs={{0,112},{16,0},{32,16},{48,32},{64,48},{80,64},{96,80},{112,96},{1... | collective-permute-start | bytes 442376 | tf_op jit(solution)/shard_map/ppermute | solution.py:276
  32.0 4.4 %collective-permute-start.12 = (bf16[608,512]{1,0:T(8,128)(2,1)S(1)}, bf16[608,512]{1,0:T(8,128)(2,1)S(1)}, u32[]{:S(2)}, u32[]{:S(2)}) collective-permute-start(bf16[608,512]{1,0:T(8,128)(2,1)S(1)} %collective-permute-done.9.refs_11_), channel_id=1, source_target_pairs={{0,1},{1,0},{2,3},{3,2},{4,5},{5,4},{6,7},{7,6},{8,9},{9,8},{10,11... | collective-permute-start | bytes 1867784 | tf_op jit(solution)/shard_map/ppermute | solution.py:273
  33.8 2.6 %collective-permute-start.10 = (bf16[576,256]{1,0:T(8,128)(2,1)}, bf16[576,256]{1,0:T(8,128)(2,1)S(1)}, u32[]{:S(2)}, u32[]{:S(2)}) collective-permute-start(bf16[576,256]{1,0:T(8,128)(2,1)} %collective-permute-done.7.refs_9_), channel_id=1, source_target_pairs={{0,1},{1,0},{2,3},{3,2},{4,5},{5,4},{6,7},{7,6},{8,9},{9,8},{10,11... | collective-permute-start | bytes 884744 | tf_op jit(solution)/shard_map/ppermute | solution.py:273
  33.8 2.6 %collective-permute-start.11 = (bf16[576,256]{1,0:T(8,128)(2,1)S(1)}, bf16[576,256]{1,0:T(8,128)(2,1)S(1)}, u32[]{:S(2)}, u32[]{:S(2)}) collective-permute-start(bf16[576,256]{1,0:T(8,128)(2,1)S(1)} %collective-permute-done.8.refs_10_), channel_id=1, source_target_pairs={{0,1},{1,0},{2,3},{3,2},{4,5},{5,4},{6,7},{7,6},{8,9},{9,8},{10,11... | collective-permute-start | bytes 884744 | tf_op jit(solution)/shard_map/ppermute | solution.py:273
